TPU v7x, 32 devices: a whole 2x2x4 slice. The times are simulated.
32 devices in a mesh: dp: 8 (over y, x, core), mp: 4 (over z).
Axes of the slice: x: 2, y: 2, z: 4, core: 2. Of those that a mesh axis runs over, the one named last changes fastest.
Arguments:
- inputs: bfloat16 [8, 1024, 1536], P('dp'), may hold values from -6 to 6
- lengths: int32 [8, 4], P('dp'), may hold values from 0 to 1024, as said below
- q_weight: bfloat16 [1536, 1536], P(None, 'mp'), may hold values from -0.3125 to 0.3125
- k_weight: bfloat16 [1536, 768], P(None, 'mp'), may hold values from -0.15625 to 0.15625
- v_weight: bfloat16 [1536, 768], P(None, 'mp'), may hold values from -0.15625 to 0.15625
- o_weight: bfloat16 [1536, 1536], P('mp'), may hold values from -0.625 to 0.625
- gate_weight: bfloat16 [1536, 4096], P(None, 'mp'), may hold values from -0.15625 to 0.15625
- up_weight: bfloat16 [1536, 4096], P(None, 'mp'), may hold values from -0.15625 to 0.15625
- down_weight: bfloat16 [4096, 1536], P('mp'), may hold values from -0.09375 to 0.09375
- attn_gain: bfloat16 [1536], replicated, may hold values from 0.5 to 1.5
- mlp_gain: bfloat16 [1536], replicated, may hold values from 0.5 to 1.5
- cotangent: bfloat16 [8, 1024, 1536], P('dp'), may hold values from -6 to 6
Outputs:
- output: bfloat16 [8, 1024, 1536], P('dp')
- input_grad: bfloat16 [8, 1024, 1536], P('dp')
- q_grad: float32 [1536, 1536], P('dp', 'mp')
- k_grad: float32 [1536, 768], P('dp', 'mp')
- v_grad: float32 [1536, 768], P('dp', 'mp')
- o_grad: float32 [1536, 1536], P('mp', 'dp')
- gate_grad: float32 [1536, 4096], P('dp', 'mp')
- up_grad: float32 [1536, 4096], P('dp', 'mp')
- down_grad: float32 [4096, 1536], P('mp', 'dp')
- attn_gain_grad: float32 [1536], P('dp')
- mlp_gain_grad: float32 [1536], P('dp')
Inputs may be any that keep to these rules, and one draw needn't show every extreme that they name: Each row's 4 lengths sum to 1024 (a length may be 0); in every draw at least a quarter of the rows hold a single sequence of 1024 tokens.
All inputs are finite; a program needn't handle non-finite values.
Results may differ from a plain program's by a relative error of at most 0.023.
Values may be sent and summed in bfloat16 or wider, within the bound.
A program may use at most 192 MiB of HBM per device.

v0:
```python
import jax
import jax.numpy as jnp
from jax import lax
from jax.sharding import PartitionSpec as P

D = 1536
HD = 96
ROW = 1024
SEGS = 4


eps = 1e-05
rope_base = 100000.0


def layout(lengths):
    finish = jnp.cumsum(lengths, axis=1)
    starts = finish - lengths
    places = jnp.arange(ROW, dtype=jnp.int32)
    segment = jnp.sum((places[None, :, None] >= finish[:, None, :]).astype(jnp.int32), axis=2)
    chosen = segment[:, :, None] == jnp.arange(SEGS, dtype=jnp.int32)[None, None, :]
    offsets = jnp.sum(jnp.where(chosen, starts[:, None, :], 0), axis=2)
    return (segment, places[None, :] - offsets)


def angles_of(positions):
    freqs = rope_base ** (-(jnp.arange(HD // 2, dtype=jnp.float32) * 2.0) / HD)
    angles = positions.astype(jnp.float32)[..., None] * freqs
    return (jnp.cos(angles), jnp.sin(angles))


def rotate(tensor, cosine, sine):
    middle = tensor.shape[-1] // 2
    leading = tensor[..., :middle]
    trailing = tensor[..., middle:]
    cos_wide = cosine[..., None, :]
    sin_wide = sine[..., None, :]
    return jnp.concatenate(
        [leading * cos_wide - trailing * sin_wide, trailing * cos_wide + leading * sin_wide],
        axis=-1,
    )


def unrotate(tensor, cosine, sine):
    middle = tensor.shape[-1] // 2
    leading = tensor[..., :middle]
    trailing = tensor[..., middle:]
    cos_wide = cosine[..., None, :]
    sin_wide = sine[..., None, :]
    return jnp.concatenate(
        [leading * cos_wide + trailing * sin_wide, trailing * cos_wide - leading * sin_wide],
        axis=-1,
    )


def masked_scores(query_block, key_rows, segment, begin, stop):
    scores = jnp.einsum(
        "qgpe,kge->gpqk", query_block, key_rows, preferred_element_type=jnp.float32
    ) * HD ** (-0.5)
    rows_here = begin + jnp.arange(stop - begin, dtype=jnp.int32)
    columns = jnp.arange(stop, dtype=jnp.int32)
    allowed = (segment[begin:stop][:, None] == segment[:stop][None, :]) & (
        columns[None, :] <= rows_here[:, None]
    )
    return jnp.where(allowed, scores, -1e30)


def norm_back(grad_normed, normed, factor):
    return factor * (grad_normed - normed * jnp.mean(grad_normed * normed, axis=-1, keepdims=True))


def body(
    inputs,
    lengths,
    q_weight,
    k_weight,
    v_weight,
    o_weight,
    gate_weight,
    up_weight,
    down_weight,
    attn_gain,
    mlp_gain,
    cotangent,
):
    f32 = jnp.float32
    bf16 = jnp.bfloat16
    rows = inputs.shape[0]
    tokens = rows * ROW
    heads = q_weight.shape[1] // HD
    groups = k_weight.shape[1] // HD
    pair = heads // groups
    scale = HD ** (-0.5)
    block = min(512, ROW)
    segment, positions = layout(lengths)
    cosine, sine = angles_of(positions.reshape(tokens))
    resid = inputs.reshape(tokens, D).astype(f32)
    factor1 = lax.rsqrt(jnp.mean(resid * resid, axis=-1, keepdims=True) + eps)
    normed1 = resid * factor1
    hidden1 = (normed1 * attn_gain.astype(f32)).astype(bf16)
    q_pre = jnp.dot(hidden1, q_weight, preferred_element_type=f32)
    k_pre = jnp.dot(hidden1, k_weight, preferred_element_type=f32)
    v_pre = jnp.dot(hidden1, v_weight, preferred_element_type=f32)
    queries = (
        rotate(q_pre.reshape(tokens, heads, HD), cosine, sine)
        .astype(bf16)
        .reshape(tokens, groups, pair, HD)
    )
    keys = rotate(k_pre.reshape(tokens, groups, HD), cosine, sine).astype(bf16)
    values = v_pre.astype(bf16).reshape(tokens, groups, HD)
    outputs = []
    logsums = []
    row = 0
    base = row * ROW
    for begin in range(0, ROW, block):
        stop = begin + block
        scores = masked_scores(
            queries[base + begin : base + stop], keys[base : base + stop], segment[row], begin, stop
        )
        top = jnp.max(scores, axis=-1, keepdims=True)
        weights = jnp.exp(scores - top)
        total = jnp.sum(weights, axis=-1, keepdims=True)
        logsums.append(top + jnp.log(total))
        probs = (weights / total).astype(bf16)
        outputs.append(
            jnp.einsum(
                "gpqk,kge->qgpe", probs, values[base : base + stop], preferred_element_type=f32
            )
        )
    heads_out = jnp.concatenate(outputs, axis=0).astype(bf16).reshape(tokens, heads * HD)
    attn_term = jnp.dot(heads_out, o_weight, preferred_element_type=f32).astype(bf16)
    attn_out = lax.psum(attn_term, "mp").astype(jnp.float32)
    mid = resid + attn_out
    factor2 = lax.rsqrt(jnp.mean(mid * mid, axis=-1, keepdims=True) + eps)
    normed2 = mid * factor2
    hidden2 = (normed2 * mlp_gain.astype(f32)).astype(bf16)
    gate = jnp.dot(hidden2, gate_weight, preferred_element_type=f32)
    upper = jnp.dot(hidden2, up_weight, preferred_element_type=f32)
    sigma = jax.nn.sigmoid(gate)
    act = (gate * sigma * upper).astype(bf16)
    mlp_term = jnp.dot(act, down_weight, preferred_element_type=f32).astype(bf16)
    mlp_out = lax.psum(mlp_term, "mp").astype(jnp.float32)
    output = (mid + mlp_out).astype(bf16).reshape(rows, ROW, D)
    grad_out = cotangent.reshape(tokens, D)
    down_grad = jnp.einsum("tf,td->fd", act, grad_out, preferred_element_type=f32)
    grad_act = jnp.einsum("td,fd->tf", grad_out, down_weight, preferred_element_type=f32)
    grad_gate = (grad_act * upper * sigma * (1.0 + gate * (1.0 - sigma))).astype(bf16)
    grad_up = (grad_act * gate * sigma).astype(bf16)
    gate_grad = jnp.einsum("td,tf->df", hidden2, grad_gate, preferred_element_type=f32)
    up_grad = jnp.einsum("td,tf->df", hidden2, grad_up, preferred_element_type=f32)
    back_term2 = jnp.einsum("tf,df->td", grad_gate, gate_weight, preferred_element_type=f32)
    back_term2 = back_term2 + jnp.einsum(
        "tf,df->td", grad_up, up_weight, preferred_element_type=f32
    )
    grad_hidden2 = lax.psum(back_term2.astype(bf16), "mp").astype(jnp.float32)
    mlp_gain_local = jnp.sum(grad_hidden2 * normed2, axis=0)
    grad_mid = grad_out.astype(f32) + norm_back(
        grad_hidden2 * mlp_gain.astype(f32), normed2, factor2
    )
    grad_mid_low = grad_mid.astype(bf16)
    o_grad = jnp.einsum("te,td->ed", heads_out, grad_mid_low, preferred_element_type=f32)
    grad_heads = (
        jnp.einsum("td,ed->te", grad_mid_low, o_weight, preferred_element_type=f32)
        .astype(bf16)
        .reshape(tokens, groups, pair, HD)
    )
    grad_query_parts = []
    grad_keys = jnp.zeros((tokens, groups, HD), f32)
    grad_values = jnp.zeros((tokens, groups, HD), f32)
    counter = 0
    row = 0
    base = row * ROW
    for begin in range(0, ROW, block):
        stop = begin + block
        query_block = queries[base + begin : base + stop]
        scores = masked_scores(query_block, keys[base : base + stop], segment[row], begin, stop)
        probs = jnp.exp(scores - logsums[counter])
        counter = counter + 1
        probs_low = probs.astype(bf16)
        grad_block = grad_heads[base + begin : base + stop]
        grad_probs = jnp.einsum(
            "qgpe,kge->gpqk", grad_block, values[base : base + stop], preferred_element_type=f32
        )
        delta = jnp.sum(probs * grad_probs, axis=-1, keepdims=True)
        grad_scores = (probs * (grad_probs - delta)).astype(bf16)
        grad_query_parts.append(
            jnp.einsum(
                "gpqk,kge->qgpe", grad_scores, keys[base : base + stop], preferred_element_type=f32
            )
            * scale
        )
        grad_keys = grad_keys.at[base : base + stop].add(
            jnp.einsum("gpqk,qgpe->kge", grad_scores, query_block, preferred_element_type=f32)
            * scale
        )
        grad_values = grad_values.at[base : base + stop].add(
            jnp.einsum("gpqk,qgpe->kge", probs_low, grad_block, preferred_element_type=f32)
        )
    grad_queries = jnp.concatenate(grad_query_parts, axis=0).reshape(tokens, heads, HD)
    grad_q = unrotate(grad_queries, cosine, sine).astype(bf16).reshape(tokens, heads * HD)
    grad_k = unrotate(grad_keys, cosine, sine).astype(bf16).reshape(tokens, groups * HD)
    grad_v = grad_values.astype(bf16).reshape(tokens, groups * HD)
    q_grad = jnp.einsum("td,te->de", hidden1, grad_q, preferred_element_type=f32)
    k_grad = jnp.einsum("td,te->de", hidden1, grad_k, preferred_element_type=f32)
    v_grad = jnp.einsum("td,te->de", hidden1, grad_v, preferred_element_type=f32)
    back_term1 = jnp.einsum("te,de->td", grad_q, q_weight, preferred_element_type=f32)
    back_term1 = back_term1 + jnp.einsum("te,de->td", grad_k, k_weight, preferred_element_type=f32)
    back_term1 = back_term1 + jnp.einsum("te,de->td", grad_v, v_weight, preferred_element_type=f32)
    grad_hidden1 = lax.psum(back_term1.astype(bf16), "mp").astype(jnp.float32)
    attn_gain_local = jnp.sum(grad_hidden1 * normed1, axis=0)
    grad_input = grad_mid + norm_back(grad_hidden1 * attn_gain.astype(f32), normed1, factor1)
    input_grad = grad_input.astype(bf16).reshape(rows, ROW, D)
    summed = (
        lax.psum_scatter(q_grad, "dp", scatter_dimension=0, tiled=True),
        lax.psum_scatter(k_grad, "dp", scatter_dimension=0, tiled=True),
        lax.psum_scatter(v_grad, "dp", scatter_dimension=0, tiled=True),
        lax.psum_scatter(o_grad, "dp", scatter_dimension=1, tiled=True),
        lax.psum_scatter(gate_grad, "dp", scatter_dimension=0, tiled=True),
        lax.psum_scatter(up_grad, "dp", scatter_dimension=0, tiled=True),
        lax.psum_scatter(down_grad, "dp", scatter_dimension=1, tiled=True),
        lax.psum_scatter(attn_gain_local, "dp", scatter_dimension=0, tiled=True),
        lax.psum_scatter(mlp_gain_local, "dp", scatter_dimension=0, tiled=True),
    )
    return (
        output,
        input_grad,
        summed[0],
        summed[1],
        summed[2],
        summed[3],
        summed[4],
        summed[5],
        summed[6],
        summed[7],
        summed[8],
    )


def solution(mesh):
    in_specs = (
        P("dp", None, None),
        P("dp", None),
        P(None, "mp"),
        P(None, "mp"),
        P(None, "mp"),
        P("mp", None),
        P(None, "mp"),
        P(None, "mp"),
        P("mp", None),
        P(),
        P(),
        P("dp", None, None),
    )
    out_specs = (
        P("dp", None, None),
        P("dp", None, None),
        P("dp", "mp"),
        P("dp", "mp"),
        P("dp", "mp"),
        P("mp", "dp"),
        P("dp", "mp"),
        P("dp", "mp"),
        P("mp", "dp"),
        P("dp"),
        P("dp"),
    )
    return jax.shard_map(body, mesh=mesh, in_specs=in_specs, out_specs=out_specs, check_vma=False)
```

profile of v0, /device:TPU:0, one launch (start us, length us, event | category | flops | bytes accessed | tf_op | source)
XLA Modules:
  0.0 958.6 jit_solution(4923154159564604458)
XLA Ops:
  13.9 3.4 fusion.84
  23.7 3.8 fusion.46
  40.4 3.5 convolution_convert_fusion
  44.5 123.3 %all-reduce.10.cloned.1.call-done = bf16[1024,1536]{1,0:T(8,128)(2,1)} async-done(((bf16[1024,1536]{1,0:T(8,128)(2,1)}), bf16[1024,1536]{1,0:T(8,128)(2,1)}) %all-reduce.10.cloned.1.call-update) | async-done | bytes 3145744 | tf_op jit(solution)/shard_map/psum | solution.py:132
  167.8 4.1 multiply_reduce_fusion
  174.4 3.4 fusion.119
  177.9 5.0 fusion.118
  182.9 8.3 multiply_convert_fusion.1
  191.2 3.5 fusion.120
  194.7 4.9 add_convert_fusion.1
  201.3 6.4 convolution_convert_fusion.1
  207.7 112.2 %all-reduce.12.cloned.1.call-done = bf16[1024,1536]{1,0:T(8,128)(2,1)} async-done(((bf16[1024,1536]{1,0:T(8,128)(2,1)}), bf16[1024,1536]{1,0:T(8,128)(2,1)}) %all-reduce.12.cloned.1.call-update) | async-done | bytes 3145744 | tf_op jit(solution)/shard_map/psum | solution.py:155
  319.9 5.8 fusion.21
  325.7 4.1 fusion.20
  343.3 2.6 fusion.2
  352.6 2.7 add_convert_fusion
  356.0 3.4 fusion.52
  362.1 6.3 fusion.63
  368.9 4.7 fusion.50
  373.6 8.6 fusion.42
  382.3 8.6 fusion.124
  391.2 8.7 fusion.123
  401.7 176.0 %all-reduce.14.cloned.1.call-done = (bf16[1024,1536]{1,0:T(8,128)(2,1)}, bf16[1024,1536]{1,0:T(8,128)(2,1)}) async-done(((bf16[1024,1536]{1,0:T(8,128)(2,1)}, bf16[1024,1536]{1,0:T(8,128)(2,1)}), (bf16[1024,1536]{1,0:T(8,128)(2,1)}, bf16[1024,1536]{1,0:T(8,128)(2,1)})) %all-reduce.14.cloned.1.call-update) | async-done | bytes 6291472 | tf_op jit(solution)/shard_map/psum | solution.py:142
  577.8 3.8 fusion.24
  581.6 24.2 %all-reduce.4 = (f32[1536]{0:T(1024)S(1)}, f32[1536]{0:T(1024)S(1)}) all-reduce(f32[1536]{0:T(1024)S(1)} %get-tuple-element.77, f32[1536]{0:T(1024)S(1)} %copy-done.48), channel_id=9, replica_groups=mesh['dp'=8,'mp'=4] {'dp'}, use_global_device_ids=true, to_apply=%region_25.26.clone | all-reduce | flops 3072 | bytes 24576
  607.1 10.5 %fusion.41 = (bf16[1,1024,1536]{2,1,0:T(8,128)(2,1)}, bf16[1,1024,1536]{2,1,0:T(8,128)(2,1)}) fusion(f32[1024,1536]{1,0:T(8,128)} %copy-done.10, bf16[1,1024,1536]{2,1,0:T(8,128)(2,1)} %param.24, bf16[1024,1536]{1,0:T(8,128)(2,1)} %get-tuple-element.82, f32[1024]{0:T(1024)S(1)} %broadcast_multiply_fusion, f32[1536]{0:T(1024)S(1)} %copy-done.38, ...), kind=kLoop, calls=%fused_computation.67 | loop fusion | flops 22020096 | bytes 25180160 | tf_op jit(solution)/shard_map/reshape | solution.py:212
  618.9 42.2 %reduce-scatter.10.cloned.1.call-done = f32[192,192]{1,0:T(8,128)} async-done(((f32[1536,192]{1,0:T(8,128)}), f32[192,192]{1,0:T(8,128)}) %reduce-scatter.10.cloned.1.call-update) | async-done | bytes 147472 | tf_op jit(solution)/shard_map/reduce_scatter | solution.py:215
  661.1 46.3 %reduce-scatter.14.cloned.1.call-done = f32[384,192]{0,1:T(8,128)} async-done(((f32[384,1536]{0,1:T(8,128)}), f32[384,192]{0,1:T(8,128)}) %reduce-scatter.14.cloned.1.call-update) | async-done | bytes 294928 | tf_op jit(solution)/shard_map/reduce_scatter | solution.py:217
  707.4 46.8 %reduce-scatter.8.cloned.1.call-done = f32[192,384]{1,0:T(8,128)} async-done(((f32[1536,384]{1,0:T(8,128)}), f32[192,384]{1,0:T(8,128)}) %reduce-scatter.8.cloned.1.call-update) | async-done | bytes 294928 | tf_op jit(solution)/shard_map/reduce_scatter | solution.py:214
  754.2 65.7 %reduce-scatter.20.cloned.1.call-done = f32[1024,192]{0,1:T(8,128)} async-done(((f32[1024,1536]{0,1:T(8,128)}), f32[1024,192]{0,1:T(8,128)}) %reduce-scatter.20.cloned.1.call-update) | async-done | bytes 786448 | tf_op jit(solution)/shard_map/reduce_scatter | solution.py:220
  819.9 66.1 %reduce-scatter.18.cloned.1.call-done = f32[192,1024]{1,0:T(8,128)} async-done(((f32[1536,1024]{1,0:T(8,128)}), f32[192,1024]{1,0:T(8,128)}) %reduce-scatter.18.cloned.1.call-update) | async-done | bytes 786448 | tf_op jit(solution)/shard_map/reduce_scatter | solution.py:219
  886.0 65.6 %reduce-scatter.16.cloned.1.call-done = f32[192,1024]{1,0:T(8,128)} async-done(((f32[1536,1024]{1,0:T(8,128)}), f32[192,1024]{1,0:T(8,128)}) %reduce-scatter.16.cloned.1.call-update) | async-done | bytes 786448 | tf_op jit(solution)/shard_map/reduce_scatter | solution.py:218
  (201 shorter events, 58.3 us)
Async XLA Ops:
  7.2 175.7 %copy-start = (bf16[1024,1536]{1,0:T(8,128)(2,1)S(1)}, bf16[1024,1536]{1,0:T(8,128)(2,1)}, u32[]{:S(2)}) copy-start(bf16[1024,1536]{1,0:T(8,128)(2,1)} %param.32) | copy-start | bytes 9437188
  7.2 160.6 %all-reduce.10.cloned.1.call-start = ((), (), s32[]{:S(2)}) async-start(), calls=%async_computation.7 | async-start | bytes 6291456 | tf_op jit(solution)/shard_map/psum | solution.py:132
  12.3 11.3 %copy-start.41 = (f32[1024]{0:T(1024)}, f32[1024]{0:T(1024)S(1)}, u32[]{:S(2)}) copy-start(f32[1024]{0:T(1024)S(1)} %add_rsqrt_fusion.1) | copy-start | bytes 12292
  13.0 10.6 %copy-start.37 = (f32[1536]{0:T(1024)}, f32[1536]{0:T(1024)S(1)}, u32[]{:S(2)}) copy-start(f32[1536]{0:T(1024)S(1)} %convert_element_type.160) | copy-start | bytes 18436
  13.9 4.9 copy-start.2
  13.9 4.9 copy-start.32
  23.6 4.6 copy-start.28
  28.4 4.5 copy-start.16
  28.4 4.5 copy-start.18
  32.9 6.7 copy-start.55
  43.9 276.0 %all-reduce.12.cloned.1.call-start = ((), (), s32[]{:S(2)}) async-start(), calls=%async_computation.8 | async-start | bytes 6291456 | tf_op jit(solution)/shard_map/psum | solution.py:155
  44.5 129.2 %copy-start.35 = (f32[1536]{0:T(1024)}, f32[1536]{0:T(1024)S(1)}, u32[]{:S(2)}) copy-start(f32[1536]{0:T(1024)S(1)} %convert_element_type.172) | copy-start | bytes 18436
  167.8 4.7 copy-start.6
  177.9 5.0 copy-start.15
  194.7 5.2 copy-start.44
  199.6 378.1 %all-reduce.14.cloned.1.call-start = ((), (), s32[]{:S(2)}) async-start(), calls=%async_computation.16 | async-start | bytes 12582912 | tf_op jit(solution)/shard_map/psum | solution.py:142
  207.7 118.0 %copy-start.4 = (bf16[1,1024,1536]{2,1,0:T(8,128)(2,1)S(1)}, bf16[1,1024,1536]{2,1,0:T(8,128)(2,1)}, u32[]{:S(2)}) copy-start(bf16[1,1024,1536]{2,1,0:T(8,128)(2,1)} %param.24) | copy-start | bytes 9437188
  319.9 5.8 copy-start.7
  319.9 5.8 copy-start.11
  319.9 5.8 copy-start.36
  319.9 5.8 copy-start.40
  329.8 4.5 copy-start.9
  343.3 9.3 copy-start.20
  355.4 263.6 %reduce-scatter.12.cloned.1.call-start = ((), (), s32[]{:S(2)}) async-start(), calls=%async_computation.11 | async-start | bytes 1769472 | tf_op jit(solution)/shard_map/reduce_scatter | solution.py:216
  359.5 301.6 %reduce-scatter.10.cloned.1.call-start = ((), (), s32[]{:S(2)}) async-start(), calls=%async_computation.10 | async-start | bytes 1769472 | tf_op jit(solution)/shard_map/reduce_scatter | solution.py:215
  362.0 345.4 %reduce-scatter.14.cloned.1.call-start = ((), (), s32[]{:S(2)}) async-start(), calls=%async_computation.12 | async-start | bytes 2654208 | tf_op jit(solution)/shard_map/reduce_scatter | solution.py:217
  368.4 385.8 %reduce-scatter.8.cloned.1.call-start = ((), (), s32[]{:S(2)}) async-start(), calls=%async_computation.9 | async-start | bytes 2654208 | tf_op jit(solution)/shard_map/reduce_scatter | solution.py:214
  373.6 446.3 %reduce-scatter.20.cloned.1.call-start = ((), (), s32[]{:S(2)}) async-start(), calls=%async_computation.15 | async-start | bytes 7077888 | tf_op jit(solution)/shard_map/reduce_scatter | solution.py:220
  382.3 503.7 %reduce-scatter.18.cloned.1.call-start = ((), (), s32[]{:S(2)}) async-start(), calls=%async_computation.14 | async-start | bytes 7077888 | tf_op jit(solution)/shard_map/reduce_scatter | solution.py:219
  390.9 560.7 %reduce-scatter.16.cloned.1.call-start = ((), (), s32[]{:S(2)}) async-start(), calls=%async_computation.13 | async-start | bytes 7077888 | tf_op jit(solution)/shard_map/reduce_scatter | solution.py:218
  399.9 181.7 %copy-start.48 = (f32[1536]{0:T(1024)S(1)}, f32[1536]{0:T(1024)}, u32[]{:S(2)}) copy-start(f32[1536]{0:T(1024)} %get-tuple-element.75) | copy-start | bytes 18436
  607.1 344.5 %copy-start.1 = (bf16[1024,1536]{1,0:T(8,128)(2,1)S(1)}, bf16[1024,1536]{1,0:T(8,128)(2,1)}, u32[]{:S(2)}) copy-start(bf16[1024,1536]{1,0:T(8,128)(2,1)} %param.32) | copy-start | bytes 9437188
  (40 other events, 93.7 us)
Sparse Core Ops, SparseCore 0:
  44.0 123.7 all-reduce.9
  199.8 120.0 all-reduce.11
  355.5 222.2 all-reduce.13
  581.5 37.4 reduce-scatter.11
  622.6 38.4 reduce-scatter.9
  664.9 42.4 reduce-scatter.13
  711.7 42.4 reduce-scatter.7
  758.1 61.7 reduce-scatter.19
  824.2 61.7 reduce-scatter.17
  889.8 61.7 reduce-scatter.15
where the time goes:
time: 962 us; the launch traced here: 959 us
  waiting for transfers between devices  746 us (78%)
  matrix products  108 us (11%)
  other arithmetic  45.3 us (5%)
  blocking collectives  24.2 us (3%)
  local copies, waits for them, and re-layouts  18 us (2%)
  between operations  15.8 us (2%)
    psum x1, waiting for transfers between devices, body(): mlp_out = lax.psum(mlp_term, 'mp').astype(jnp.float32)  176 us
    psum x1, waiting for transfers between devices, body(): attn_out = lax.psum(attn_term, 'mp').astype(jnp.float32)  123 us
    psum x1, waiting for transfers between devices, body(): grad_hidden2 = lax.psum(back_term2.astype(bf16), 'mp').astype(jnp.float32)  112 us
    reduce_scatter x1, waiting for transfers between devices, body(): lax.psum_scatter(up_grad, 'dp', scatter_dimension=0, tiled=True)  66.1 us
    reduce_scatter x1, waiting for transfers between devices, body(): lax.psum_scatter(down_grad, 'dp', scatter_dimension=1, tiled=True)  65.7 us
    reduce_scatter x1, waiting for transfers between devices, body(): lax.psum_scatter(gate_grad, 'dp', scatter_dimension=0, tiled=True)  65.6 us
    reduce_scatter x1, waiting for transfers between devices, body(): lax.psum_scatter(q_grad, 'dp', scatter_dimension=0, tiled=True)  46.8 us
    reduce_scatter x1, waiting for transfers between devices, body(): lax.psum_scatter(o_grad, 'dp', scatter_dimension=1, tiled=True)  46.3 us
  transfers between devices with their start and end apart: 10, of which 10 were waited for; matrix products, arithmetic and copies ran while one was open for 7% of the time, Pallas kernels for 0%

commit v1 on v0

v1 whole, which is shorter than its diff:
```python
import functools

import jax
import jax.numpy as jnp
from jax import lax
from jax.experimental import pallas as pl
from jax.experimental.pallas import tpu as pltpu
from jax.sharding import PartitionSpec as P

D = 1536
HD = 96
ROW = 1024
SEGS = 4
NZ = 4
CH = 256
TB = 128
HQ_OWN = 4
KV_OWN = 2
QR = HQ_OWN * HD
KR = KV_OWN * HD
QKV = QR + 2 * KR
WR = QKV + QR
SCALE = HD ** -0.5
C2 = SCALE * 1.4426950408889634
NEG = -1e30
eps = 1e-05
rope_base = 100000.0
f32 = jnp.float32
bf16 = jnp.bfloat16
MESH = pl.DeviceIdType.MESH
ANY = pl.BlockSpec(memory_space=pl.ANY)
VM = pl.BlockSpec(memory_space=pltpu.VMEM)
DMA = pltpu.SemaphoreType.DMA
sds = jax.ShapeDtypeStruct


def nt(a, b):
    return lax.dot_general(a, b, (((1,), (1,)), ((), ())), preferred_element_type=f32)


def nn(a, b):
    return lax.dot_general(a, b, (((1,), (0,)), ((), ())), preferred_element_type=f32)


def tn(a, b):
    return lax.dot_general(a, b, (((0,), (0,)), ((), ())), preferred_element_type=f32)


def chunk(c, size=CH):
    return pl.ds(pl.multiple_of(c * size, size), size)


def places():
    dp = lax.axis_index("dp")
    z = lax.axis_index("mp")
    low = lax.rem(dp, 8)
    return dp, z, low


def partner(low, dp, bit):
    on = lax.rem(low // bit, 2)
    return dp + bit - 2 * bit * on


def greet(dp, z, low):
    barrier = pltpu.get_barrier_semaphore()
    for bit in (1, 2, 4):
        pl.semaphore_signal(barrier, inc=1, device_id={"dp": partner(low, dp, bit)}, device_id_type=MESH)
    for other in (1, 2, 3):
        pl.semaphore_signal(barrier, inc=1, device_id={"mp": lax.rem(z + other, NZ)}, device_id_type=MESH)
    pl.semaphore_wait(barrier, 6)


def put(src, dst, ssem, rsem, dev):
    return pltpu.make_async_remote_copy(
        src_ref=src, dst_ref=dst, send_sem=ssem, recv_sem=rsem, device_id=dev, device_id_type=MESH)


def split3(v):
    hi = v.astype(bf16).astype(f32)
    rest = v - hi
    mid = rest.astype(bf16).astype(f32)
    return hi, mid, rest - mid


def extra_rows(base, v, first):
    row = lax.broadcasted_iota(jnp.int32, base.shape, 0)
    out = base
    for i, part in enumerate(split3(v)):
        out = jnp.where(row == first + i, part, out)
    return out.astype(bf16)


def project(w, hid, qt, kt, kk, vt, vv, cos, sin, qaug, kaug, s, c):
    cols = chunk(c)
    t = nt(w[s, 0:QKV], hid[cols])
    co = cos[:, cols]
    si = sin[:, cols]

    def rot(u):
        a = u[0:HD // 2]
        b = u[HD // 2:HD]
        return jnp.concatenate([a * co - b * si, b * co + a * si], axis=0).astype(bf16)

    for h in range(HQ_OWN):
        qt[HQ_OWN * s + h, 0:HD, cols] = rot(t[HD * h:HD * h + HD])
        qt[HQ_OWN * s + h, HD:128, cols] = qaug[:, cols]
    for h in range(KV_OWN):
        g = KV_OWN * s + h
        k = jnp.concatenate([rot(t[QR + HD * h:QR + HD * h + HD]), kaug[:, cols]], axis=0)
        kt[g, :, cols] = k
        kk[g, cols, :] = k.T
        v = t[QR + KR + HD * h:QR + KR + HD * h + HD].astype(bf16)
        v = jnp.concatenate([v, jnp.ones((128 - HD, CH), bf16)], axis=0)
        vt[g, :, cols] = v
        vv[g, cols, :] = v.T


def attend(qt, kk, vt, ho, qaug, g):
    for qb in range(ROW // CH):
        lo = qb * CH
        nk = lo + CH
        q = jnp.concatenate([qt[2 * g, :, lo:nk], qt[2 * g + 1, :, lo:nk]], axis=1)
        st = nn(kk[g, 0:nk, :], q)
        ki = lax.broadcasted_iota(jnp.int32, (CH, CH), 0)
        qi = lax.broadcasted_iota(jnp.int32, (CH, CH), 1)
        keep = jnp.concatenate([ki <= qi, ki <= qi], axis=1)
        dg = jnp.where(keep, st[lo:nk], NEG)
        m = jnp.max(dg, axis=0, keepdims=True)
        if qb:
            m = jnp.maximum(m, jnp.max(st[0:lo], axis=0, keepdims=True))
        mc = m * C2
        o = nn(vt[g, :, lo:nk], jnp.exp2(dg * C2 - mc).astype(bf16))
        if qb:
            o = o + nn(vt[g, :, 0:lo], jnp.exp2(st[0:lo] * C2 - mc).astype(bf16))
        total = o[HD:HD + 1]
        r = (o[0:HD] / total).astype(bf16)
        back = (mc + jnp.log2(total)) * (-1.0 / C2)
        for h in range(2):
            part = slice(h * CH, (h + 1) * CH)
            ho[pl.ds(pl.multiple_of(g * 2 * HD + h * HD, 32), HD), lo:nk] = r[:, part]
            base = qaug[:, lo:nk].astype(f32)
            qt[2 * g + h, HD:128, lo:nk] = extra_rows(base, back[:, part], SEGS)


def order(z, j):
    right = (0, 1, 2, 3), (1, 0, 2, 3), (2, 3, 1, 0), (3, 2, 1, 0)
    s = jnp.int32(0)
    for i in range(NZ):
        s = s + jnp.where(z == i, right[i][j], 0)
    return s


GPARTS = ((0, QKV // 8, 48), (QKV, QR // 8, 32))


def forward_kernel(x, gain, gain2, cos, sin, qaug, kaug, own,
                   mid_o, hid2_o, ho_o, qt_o, kt_o, kk_o, vv_o, w_o, hid_o,
                   w, hid, ho, qt, kt, kk, vt, vv, midb, hidb,
                   zsend, zrecv, xsend, xrecv, ysend, yrecv, csend, crecv, osem, wsem, msem):
    dp, z, low = places()
    pc, px, py = (partner(low, dp, bit) for bit in (1, 2, 4))
    lx = px - dp + low
    ly = py - dp + low
    lxy = ly + lx - low
    load = pltpu.make_async_copy(own, w.at[z], wsem.at[0])
    load.start()
    greet(dp, z, low)
    load.wait()

    def rows(part, where, lo, hi):
        base, size, _ = GPARTS[part]
        return pl.ds(pl.multiple_of(base + where * size + lo, 16), hi - lo)

    def zcopy(part, d, s):
        r = rows(part, low, 0, GPARTS[part][1])
        to = lax.rem(z + d, NZ)
        return put(w.at[s, r], w.at[s, r], zsend.at[part, d - 1], zrecv.at[part, s], {"mp": to})

    for part in range(2):
        for hop in (1, 2, 3):
            for sign in (1, -1):
                to = z + sign * hop

                @pl.when((to >= 0) & (to < NZ))
                def _(part=part, hop=hop, sign=sign):
                    zcopy(part, (sign * hop) % NZ, z).start()

    def copies(part, j, kind):
        s = order(z, j)
        base, size, cut = GPARTS[part]
        a, b, both = (0, cut), (cut, size), (0, size)
        if part == 1:
            a, b = (0, size - 32), (size - 32, size)

        def c(where, half, sems, semr, i, dev):
            r = rows(part, where, *half)
            return put(w.at[s, r], w.at[s, r], sems.at[part, j - 1, i], semr.at[part, j - 1, i], {"dp": dev})

        if kind == 1:
            return [c(low, a, xsend, xrecv, 0, px), c(low, b, ysend, yrecv, 0, py)]
        if kind == 2:
            return [c(low, a, ysend, yrecv, 1, py), c(lx, a, ysend, yrecv, 2, py),
                    c(low, b, xsend, xrecv, 1, px), c(ly, b, xsend, xrecv, 2, px)]
        return [c(at, both, csend, crecv, i, pc) for i, at in enumerate((low, lx, ly, lxy))]

    def stage(part, j, k):
        if k == 1:
            zcopy(part, 1, order(z, j)).wait_recv()
        else:
            for c in copies(part, j, k - 1):
                c.wait_recv()
        if k < 4:
            for c in copies(part, j, k):
                c.start()

    def norm(c, _):
        r = chunk(c)
        xx = x[r].astype(f32)
        f = lax.rsqrt(jnp.mean(xx * xx, axis=1, keepdims=True) + eps)
        hid[r] = (xx * f * gain[...].astype(f32)).astype(bf16)
        return 0

    lax.fori_loop(0, ROW // CH, norm, 0)

    def projections(s):
        def one(c, _):
            project(w, hid, qt, kt, kk, vt, vv, cos, sin, qaug, kaug, s, c)
            return 0

        lax.fori_loop(0, ROW // CH, one, 0)

    def attends(s):
        def one(g, _):
            attend(qt, kk, vt, ho, qaug, KV_OWN * s + g)
            return 0

        lax.fori_loop(0, KV_OWN, one, 0)

    events = {
        "0a": ((0, 1, 1),),
        "0b": ((0, 1, 2), (0, 2, 1), (0, 1, 3), (0, 2, 2), (0, 3, 1), (0, 1, 4)),
        "1a": ((0, 2, 3), (0, 3, 2), (1, 1, 1)),
        "1b": ((0, 2, 4), (0, 3, 3), (1, 1, 2), (1, 2, 1)),
        "2a": ((0, 3, 4), (1, 1, 3), (1, 2, 2), (1, 3, 1)),
        "2b": ((1, 1, 4), (1, 2, 3), (1, 3, 2)),
        "3a": ((1, 2, 4), (1, 3, 3)),
        "3b": ((1, 3, 4),),
    }
    for j in range(NZ):
        s = order(z, j)
        projections(s)
        for e in events[f"{j}a"]:
            stage(*e)
        attends(s)
        for e in events[f"{j}b"]:
            stage(*e)
    outs = [(w, w_o), (qt, qt_o), (kt, kt_o), (kk, kk_o), (vv, vv_o), (ho, ho_o), (hid, hid_o)]
    writes = [pltpu.make_async_copy(a, b, osem.at[i]) for i, (a, b) in enumerate(outs)]
    for c in writes:
        c.start()

    def mid_copies(c, slot):
        return (pltpu.make_async_copy(midb.at[slot], mid_o.at[chunk(c)], msem.at[0, slot]),
                pltpu.make_async_copy(hidb.at[slot], hid2_o.at[chunk(c)], msem.at[1, slot]))

    def out_proj(c, _):
        r = chunk(c)
        slot = lax.rem(c, 2)

        @pl.when(c >= 2)
        def _():
            for m in mid_copies(c - 2, slot):
                m.wait()

        acc = x[r].astype(f32)
        for s in range(NZ):
            acc = acc + tn(ho[QR * s:QR * s + QR, r], w[s, QKV:WR])
        midb[slot] = acc
        f = lax.rsqrt(jnp.mean(acc * acc, axis=1, keepdims=True) + eps)
        hidb[slot] = (acc * f * gain2[...].astype(f32)).astype(bf16)
        for m in mid_copies(c, slot):
            m.start()
        return 0

    n = ROW // CH
    lax.fori_loop(0, n, out_proj, 0)
    for c in range(max(n - 2, 0), n):
        for m in mid_copies(c, c % 2):
            m.wait()
    for c in writes:
        c.wait()
    for part in range(2):
        for d in (1, 2, 3):
            zcopy(part, d, z).wait_send()
        for j in (1, 2, 3):
            for kind in (1, 2, 3):
                for c in copies(part, j, kind):
                    c.wait_send()


def forward(x, gain, gain2, cos, sin, qaug, kaug, own):
    heads = NZ * HQ_OWN
    kv = NZ * KV_OWN
    vm = pltpu.VMEM
    return pl.pallas_call(
        forward_kernel,
        out_shape=(sds((ROW, D), f32), sds((ROW, D), bf16), sds((heads * HD, ROW), bf16),
                   sds((heads, 128, ROW), bf16), sds((kv, 128, ROW), bf16), sds((kv, ROW, 128), bf16),
                   sds((kv, ROW, 128), bf16), sds((NZ, WR, D), bf16), sds((ROW, D), bf16)),
        in_specs=[VM] * 7 + [ANY],
        out_specs=(ANY,) * 9,
        scratch_shapes=[
            vm((NZ, WR, D), bf16), vm((ROW, D), bf16), vm((heads * HD, ROW), bf16),
            vm((heads, 128, ROW), bf16), vm((kv, 128, ROW), bf16), vm((kv, ROW, 128), bf16),
            vm((kv, 128, ROW), bf16), vm((kv, ROW, 128), bf16), vm((2, CH, D), f32), vm((2, CH, D), bf16),
            DMA((2, 3)), DMA((2, NZ)), DMA((2, 3, 3)), DMA((2, 3, 3)), DMA((2, 3, 3)), DMA((2, 3, 3)),
            DMA((2, 3, 4)), DMA((2, 3, 4)), DMA((7,)), DMA((1,)), DMA((2, 2))],
        compiler_params=pltpu.CompilerParams(
            collective_id=1, has_side_effects=True, vmem_limit_bytes=60 * 2**20),
        name="attention_forward",
    )(x, gain, gain2, cos, sin, qaug, kaug, own)


def tables(lengths):
    finish = jnp.cumsum(lengths)
    starts = finish - lengths
    place = jnp.arange(ROW, dtype=jnp.int32)
    segment = jnp.sum((place[None, :] >= finish[:, None]).astype(jnp.int32), axis=0)
    chosen = segment[None, :] == jnp.arange(SEGS, dtype=jnp.int32)[:, None]
    offsets = jnp.sum(jnp.where(chosen, starts[:, None], 0), axis=0)
    positions = (place - offsets).astype(f32)
    freqs = rope_base ** (-(jnp.arange(HD // 2, dtype=f32) * 2.0) / HD)
    angles = freqs[:, None] * positions[None, :]
    rest = 128 - HD - SEGS
    qaug = jnp.concatenate([jnp.where(chosen, 0.0, NEG), jnp.zeros((rest, ROW))], axis=0).astype(bf16)
    kaug = jnp.concatenate([chosen.astype(f32), jnp.ones((3, ROW)), jnp.zeros((rest - 3, ROW))], axis=0).astype(bf16)
    return jnp.cos(angles), jnp.sin(angles), qaug, kaug


def unrotate(u, co, si):
    a = u[0:HD // 2]
    b = u[HD // 2:HD]
    return jnp.concatenate([a * co + b * si, b * co - a * si], axis=0).astype(bf16)


def attend_back(qt, kt, kk, vv, dot, ho, dk, dv, gt, cos, sin, g, qb):
    lo = qb * CH
    hi = lo + CH
    q = jnp.concatenate([qt[2 * g, :, lo:hi], qt[2 * g + 1, :, lo:hi]], axis=1)
    heads = []
    for h in range(2):
        at = pl.ds(pl.multiple_of(g * 2 * HD + h * HD, 32), HD)
        do = dot[at, :]
        delta = jnp.sum(do.astype(f32) * ho[at, lo:hi].astype(f32), axis=0, keepdims=True)
        extra = extra_rows(jnp.zeros((128 - HD, CH), f32), -delta, 0)
        heads.append(jnp.concatenate([do, extra], axis=0))
    do = jnp.concatenate(heads, axis=1)
    do_t = do.T
    q_t = q.T
    dq = jnp.zeros((128, 2 * CH), f32)
    for kb in range(qb + 1):
        ks = slice(kb * CH, (kb + 1) * CH)
        p = jnp.exp2(nn(kk[g, ks, :], q) * C2)
        if kb == qb:
            ki = lax.broadcasted_iota(jnp.int32, (CH, CH), 0)
            qi = lax.broadcasted_iota(jnp.int32, (CH, CH), 1)
            keep = jnp.concatenate([ki <= qi, ki <= qi], axis=1)
            p = jnp.where(keep, p, 0.0)
        ds = (p * nn(vv[g, ks, :], do)).astype(bf16)
        dvb = nn(p.astype(bf16), do_t)
        dkb = nn(ds, q_t)
        if kb == qb:
            dv[g, ks, :] = dvb
            dk[g, ks, :] = dkb
        else:
            dv[g, ks, :] += dvb
            dk[g, ks, :] += dkb
        dq = dq + nn(kt[g, :, ks], ds)
    co = cos[:, lo:hi]
    si = sin[:, lo:hi]
    s = g // KV_OWN
    first = s * QKV + lax.rem(g, KV_OWN) * 2 * HD
    for h in range(2):
        at = pl.ds(pl.multiple_of(first + h * HD, 32), HD)
        gt[at, lo:hi] = unrotate(dq[0:HD, h * CH:(h + 1) * CH] * SCALE, co, si)


def backward_kernel(gain, gain2, cos, sin, x, cot, mid, gh2, hid1, ho_i, qt_i, kt_i, kk_i, vv_i, w_i,
                    xg_o, grad_o, gain_o, gain2_o, gm_o,
                    w, ho, qt, kt, kk, vv, dk, dv, gt, gml, dot, h1, xb, cb, mb, gb, gmb, ob,
                    lsem, bsem, wsem, psem):
    z = lax.axis_index("mp")
    loads = [pltpu.make_async_copy(a, b, lsem.at[i]) for i, (a, b) in enumerate(
        ((w_i, w), (ho_i, ho), (qt_i, qt), (kt_i, kt), (kk_i, kk), (vv_i, vv), (hid1, h1)))]
    for c in loads:
        c.start()
    nb = ROW // TB

    def block_loads(b, slot):
        r = chunk(b, TB)
        return [pltpu.make_async_copy(src.at[r], dst.at[slot], bsem.at[i, slot])
                for i, (src, dst) in enumerate(((mid, mb), (cot, cb), (gh2, gb)))]

    def gm_copy(b, slot):
        return pltpu.make_async_copy(gmb.at[slot], gm_o.at[chunk(b, TB)], wsem.at[slot])

    for c in block_loads(0, 0):
        c.start()
    gain2_o[...] = jnp.zeros_like(gain2_o)
    gain_o[...] = jnp.zeros_like(gain_o)

    def grad_mid(b, _):
        slot = lax.rem(b, 2)

        @pl.when(b + 1 < nb)
        def _():
            for c in block_loads(b + 1, 1 - slot):
                c.start()

        for c in block_loads(b, slot):
            c.wait()

        @pl.when(b >= 2)
        def _():
            gm_copy(b - 2, slot).wait()

        m = mb[slot]
        f = lax.rsqrt(jnp.mean(m * m, axis=1, keepdims=True) + eps)
        n = m * f
        g = gb[slot].astype(f32)
        gn = g * n
        gain2_o[...] += jnp.sum(gn, axis=0, keepdims=True)
        ga = gain2[...].astype(f32)
        gm = cb[slot].astype(f32) + f * (g * ga - n * jnp.mean(gn * ga, axis=1, keepdims=True))
        gmb[slot] = gm
        gml[chunk(b, TB)] = gm.astype(bf16)
        gm_copy(b, slot).start()
        return 0

    for qb in range(ROW // CH):
        lax.fori_loop(qb * (CH // TB), (qb + 1) * (CH // TB), grad_mid, 0)
        if qb == 0:
            for c in loads:
                c.wait()

        def heads(s, _, qb=qb):
            t = nt(w[s, QKV:WR], gml[qb * CH:(qb + 1) * CH])
            dot[pl.ds(pl.multiple_of(s * QR, 32), QR), :] = t.astype(bf16)
            return 0

        lax.fori_loop(0, NZ, heads, 0)

        def one(g, _, qb=qb):
            attend_back(qt, kt, kk, vv, dot, ho, dk, dv, gt, cos, sin, g, qb)
            return 0

        lax.fori_loop(0, NZ * KV_OWN, one, 0)
    for b in range(nb - 2, nb):
        gm_copy(b, b % 2).wait()

    def keys(g, _):
        s = g // KV_OWN
        first = s * QKV + QR + lax.rem(g, KV_OWN) * HD
        gt[pl.ds(pl.multiple_of(first, 32), HD), :] = unrotate(dk[g].T[0:HD] * SCALE, cos[...], sin[...])
        gt[pl.ds(pl.multiple_of(first + KR, 32), HD), :] = dv[g].T[0:HD].astype(bf16)
        return 0

    lax.fori_loop(0, NZ * KV_OWN, keys, 0)

    def own_grads(i, _):
        at = pl.ds(pl.multiple_of(z * QKV + i * 192, 32), 192)
        grad_o[pl.ds(pl.multiple_of(i * 192, 32), 192), :] = nn(gt[at, :], h1[...]).astype(bf16)
        return 0

    lax.fori_loop(0, QKV // 192, own_grads, 0)

    def own_o(i, _):
        at = pl.ds(pl.multiple_of(z * QR + i * 192, 32), 192)
        grad_o[pl.ds(pl.multiple_of(QKV + i * 192, 32), 192), :] = nn(ho[at, :], gml[...]).astype(bf16)
        return 0

    lax.fori_loop(0, QR // 192, own_o, 0)

    def tail_loads(b, slot):
        r = chunk(b, TB)
        return [pltpu.make_async_copy(x.at[r], cb.at[slot], bsem.at[0, slot]),
                pltpu.make_async_copy(gm_o.at[r], mb.at[slot], bsem.at[1, slot])]

    def out_copy(b, slot):
        return pltpu.make_async_copy(ob.at[slot], xg_o.at[chunk(b, TB)], psem.at[slot])

    for c in tail_loads(0, 0):
        c.start()

    def tail(b, _):
        slot = lax.rem(b, 2)

        @pl.when(b + 1 < nb)
        def _():
            for c in tail_loads(b + 1, 1 - slot):
                c.start()

        r = chunk(b, TB)
        acc = jnp.zeros((TB, D), f32)
        for s in range(NZ):
            acc = acc + tn(gt[QKV * s:QKV * s + QKV, r], w[s, 0:QKV])
        for c in tail_loads(b, slot):
            c.wait()

        @pl.when(b >= 2)
        def _():
            out_copy(b - 2, slot).wait()

        xx = cb[slot].astype(f32)
        f = lax.rsqrt(jnp.mean(xx * xx, axis=1, keepdims=True) + eps)
        n = xx * f
        gn = acc * n
        gain_o[...] += jnp.sum(gn, axis=0, keepdims=True)
        ga = gain[...].astype(f32)
        out = mb[slot] + f * (acc * ga - n * jnp.mean(gn * ga, axis=1, keepdims=True))
        ob[slot] = out.astype(bf16)
        out_copy(b, slot).start()
        return 0

    lax.fori_loop(0, nb, tail, 0)
    for b in range(nb - 2, nb):
        out_copy(b, b % 2).wait()


def backward(gain, gain2, cos, sin, x, cot, mid, gh2, hid1, ho, qt, kt, kk, vv, w):
    vm = pltpu.VMEM
    heads = NZ * HQ_OWN
    kv = NZ * KV_OWN
    return pl.pallas_call(
        backward_kernel,
        out_shape=(sds((ROW, D), bf16), sds((WR, D), bf16), sds((1, D), f32), sds((1, D), f32), sds((ROW, D), f32)),
        in_specs=[VM] * 4 + [ANY] * 11,
        out_specs=(ANY, VM, VM, VM, ANY),
        scratch_shapes=[
            vm((NZ, WR, D), bf16), vm((heads * HD, ROW), bf16), vm((heads, 128, ROW), bf16),
            vm((kv, 128, ROW), bf16), vm((kv, ROW, 128), bf16), vm((kv, ROW, 128), bf16),
            vm((kv, ROW, 128), f32), vm((kv, ROW, 128), f32), vm((NZ * QKV, ROW), bf16),
            vm((ROW, D), bf16), vm((heads * HD, CH), bf16), vm((ROW, D), bf16),
            vm((2, TB, D), bf16), vm((2, TB, D), bf16), vm((2, TB, D), f32), vm((2, TB, D), bf16),
            vm((2, TB, D), f32), vm((2, TB, D), bf16),
            DMA((7,)), DMA((3, 2)), DMA((2,)), DMA((2,))],
        compiler_params=pltpu.CompilerParams(vmem_limit_bytes=63 * 2**20),
        name="attention_backward",
    )(gain, gain2, cos, sin, x, cot, mid, gh2, hid1, ho, qt, kt, kk, vv, w)


def body(inputs, lengths, q_weight, k_weight, v_weight, o_weight, gate_weight, up_weight, down_weight,
         attn_gain, mlp_gain, cotangent):
    x = inputs.reshape(ROW, D)
    cot = cotangent.reshape(ROW, D)
    gain = attn_gain.reshape(1, D)
    gain2 = mlp_gain.reshape(1, D)
    cos, sin, qaug, kaug = tables(lengths[0])
    own = jnp.concatenate([q_weight.T, k_weight.T, v_weight.T, o_weight], axis=0)
    mid, hidden2, ho, qt, kt, kk, vv, w, hid1 = forward(x, gain, gain2, cos, sin, qaug, kaug, own)
    gate = jnp.dot(hidden2, gate_weight, preferred_element_type=f32)
    upper = jnp.dot(hidden2, up_weight, preferred_element_type=f32)
    sigma = jax.nn.sigmoid(gate)
    act = (gate * sigma * upper).astype(bf16)
    mlp_term = jnp.dot(act, down_weight, preferred_element_type=f32).astype(bf16)
    grad_act = jnp.einsum("td,fd->tf", cot, down_weight, preferred_element_type=f32)
    grad_gate = (grad_act * upper * sigma * (1.0 + gate * (1.0 - sigma))).astype(bf16)
    grad_up = (grad_act * gate * sigma).astype(bf16)
    back_term2 = jnp.einsum("tf,df->td", grad_gate, gate_weight, preferred_element_type=f32)
    back_term2 = back_term2 + jnp.einsum("tf,df->td", grad_up, up_weight, preferred_element_type=f32)
    grad_hidden2 = lax.psum(back_term2.astype(bf16), "mp")
    mlp_out = lax.psum(mlp_term, "mp").astype(f32)
    output = (mid + mlp_out).astype(bf16).reshape(1, ROW, D)
    down_grad = jnp.einsum("td,tf->df", cot, act, preferred_element_type=f32)
    gate_grad = jnp.einsum("td,tf->df", hidden2, grad_gate, preferred_element_type=f32)
    up_grad = jnp.einsum("td,tf->df", hidden2, grad_up, preferred_element_type=f32)
    input_grad, grads, gain_local, gain2_local, _ = backward(
        gain, gain2, cos, sin, x, cot, mid, grad_hidden2, hid1, ho, qt, kt, kk, vv, w)

    def scatter(v, dim=0):
        return lax.psum_scatter(v, "dp", scatter_dimension=dim, tiled=True).astype(f32)

    mlp = scatter(jnp.concatenate([gate_grad, up_grad, down_grad], axis=1).astype(bf16))
    ff = gate_weight.shape[1]
    att = scatter(grads.T)
    return (output, input_grad.reshape(1, ROW, D), att[:, 0:QR], att[:, QR:QR + KR], att[:, QR + KR:QKV],
            att[:, QKV:WR].T, mlp[:, 0:ff], mlp[:, ff:2 * ff], mlp[:, 2 * ff:].T,
            scatter(gain_local[0]), scatter(gain2_local[0]))


def solution(mesh):
    row = P("dp", None, None)
    in_specs = (row, P("dp", None), P(None, "mp"), P(None, "mp"), P(None, "mp"), P("mp", None),
                P(None, "mp"), P(None, "mp"), P("mp", None), P(), P(), row)
    out_specs = (row, row, P("dp", "mp"), P("dp", "mp"), P("dp", "mp"), P("mp", "dp"),
                 P("dp", "mp"), P("dp", "mp"), P("mp", "dp"), P("dp"), P("dp"))
    return jax.shard_map(body, mesh=mesh, in_specs=in_specs, out_specs=out_specs, check_vma=False)
```

time: 962 us -> 619 us (0.64)
  waiting for transfers between devices: 746 us -> 278 us
  Pallas kernels: 0 us -> 189 us
  matrix products: 108 us -> 41.9 us
  other arithmetic: 45.3 us -> 19.7 us
  local copies, waits for them, and re-layouts: 18 us -> 42.3 us
    reduce_scatter x7 -> x0, waiting for transfers between devices: 334 us -> none  [the longest x1 66.1 us: body(): lax.psum_scatter(up_grad, 'dp', scatter_dimension=0, tiled=True)]
    psum x3 -> x1, waiting for transfers between devices: 412 us -> 222 us  [body(): mlp_out = lax.psum(mlp_term, 'mp').astype(f32)]
    pallas_call x0 -> x2, Pallas kernels: none -> 189 us  [the longest x1 108 us: forward(): pl.pallas_call(forward_kernel, out_shape=(sds((ROW, D), f32), sds((ROW, D...]
    dot_general x26 -> x2, matrix products: 67.4 us -> 10.2 us  [the longest x1 6.34 us: body(): jnp.einsum('td,fd->tf', cot, down_weight, preferred_element_type=f32)]
    unnamed x10 -> x5, waiting for transfers between devices: 0.16 us -> 56.1 us
    unnamed x128 -> x55, local copies, waits for them, and re-layouts: 17.3 us -> 35.4 us
    reduce_sum x8 -> x2, other arithmetic: 18.1 us -> 0.16 us  [the longest x1 0.08 us: tables(): jnp.sum((place[None, :] >= finish[:, None]).astype(jnp.int32), axis=0)]
  transfers between devices with their start and end apart: 10 -> 3, of which waited for: 10 -> 2; matrix products, arithmetic and copies ran while one was open for 7% -> 7% of each run, Pallas kernels for 0% -> 0%
where the time goes in v1:
time: 619 us; the launch traced here: 611 us
  waiting for transfers between devices  278 us (45%)
  Pallas kernels  189 us (31%)
  local copies, waits for them, and re-layouts  42.3 us (7%)
  matrix products  41.9 us (7%)
  blocking collectives  24.3 us (4%)
  other arithmetic  19.7 us (3%)
  between operations  15.2 us (2%)
    psum x1, waiting for transfers between devices, body(): mlp_out = lax.psum(mlp_term, 'mp').astype(f32)  222 us
    pallas_call x1, Pallas kernels, forward(): pl.pallas_call(forward_kernel, out_shape=(sds((ROW, D), f32), sds((ROW, D...  108 us
    pallas_call x1, Pallas kernels, backward(): pl.pallas_call(backward_kernel, out_shape=(sds((ROW, D), bf16), sds((WR,...  81 us
    unnamed x5, waiting for transfers between devices  56.1 us
    unnamed x55, local copies, waits for them, and re-layouts  35.4 us
    unnamed x1, blocking collectives  24.3 us
  transfers between devices with their start and end apart: 3, of which 2 were waited for; matrix products, arithmetic and copies ran while one was open for 7% of the time, Pallas kernels for 0%

profile of v1, /device:TPU:0, one launch (start us, length us, event | category | flops | bytes accessed | tf_op | source)
XLA Modules:
  0.0 610.9 jit_solution(709188985237132409)
XLA Ops:
  10.3 1.3 reshape.83.gain
  11.6 1.3 reshape.84.gain2
  13.5 1.6 copy.39
  15.1 1.5 multiply_sine_fusion
  16.6 1.4 maximum_maximum_fusion.kaug
  18.0 2.0 pad_maximum_fusion.1.own
  20.0 108.3 %attention_forward.1 = (f32[1024,1536]{1,0:T(8,128)}, bf16[1024,1536]{1,0:T(8,128)(2,1)}, bf16[1536,1024]{1,0:T(8,128)(2,1)}, bf16[16,128,1024]{2,1,0:T(8,128)(2...) custom-call(bf16[1024,1536]{1,0:T(8,128)(2,1)} %bitcast.45, ...), custom_call_target="tpu_custom_call" | custom-call | tf_op jit(solution)/shard_map/attention_forward/pallas_call | solution.py:306
  128.3 5.4 fusion.8
  133.8 3.4 fusion.7
  137.2 6.3 %multiply_convert_fusion = (bf16[1024,1024]{1,0:T(8,128)(2,1)}, bf16[1024,1024]{1,0:T(8,128)(2,1)S(1)}, bf16[1024,1024]{1,0:T(8,128)(2,1)S(1)}) fusion(f32[1024,1024]{1,0:T(8,128)S(1)} %fusion.7, f32[1024,1024]{1,0:T(8,128)S(1)} %fusion.8, bf16[1024,1536]{1,0:T(8,128)(2,1)S(1)} %copy-done.8, bf16[1,1024,1536]{2,1,0:T(8,128)(2,1)S(1)} %copy-done), kind=kOutput, calls=%fused_computation.3 | convolution fusion | flops 3238002688 | bytes 20971520 | tf_op jit(solution)/shard_map/td,fd->tf/dot_general | solution.py:567
  143.6 4.9 convolution_convert_fusion.3
  148.6 3.5 fusion.9
  152.1 4.9 add_convert_fusion
  157.0 221.9 %all-reduce.7.cloned.1.call-done = (bf16[1024,1536]{1,0:T(8,128)(2,1)}, bf16[1024,1536]{1,0:T(8,128)(2,1)}) async-done(((bf16[1024,1536]{1,0:T(8,128)(2,1)}, bf16[1024,1536]{1,0:T(8,128)(2,1)}), (bf16[1024,1536]{1,0:T(8,128)(2,1)}, bf16[1024,1536]{1,0:T(8,128)(2,1)})) %all-reduce.7.cloned.1.call-update) | async-done | bytes 6291472 | tf_op jit(solution)/shard_map/psum | solution.py:573
  378.9 81.0 %attention_backward.1 = (bf16[1024,1536]{1,0:T(8,128)(2,1)}, bf16[1152,1536]{1,0:T(8,128)(2,1)}, f32[1,1536]{1,0:T(1,128)}, f32[1,1536]{1,0:T(1,128)}, f32[1024,1536]{1,0:T(8,128)}) custom-call(bf16[1,1536]{1,0:T(2,128)(2,1)} %reshape.83.gain, bf16[1,1536]{1,0:T(2,128)(2,1)} %reshape.84.gain2, f32[48,1024]{1,0:T(8,128)} %get-tuple-element.82.cos, ...), custom_call_target="tpu_custom_call" | custom-call | tf_op jit(solution)/shard_map/attention_backward/pallas_call | solution.py:535
  459.9 5.8 copy.47
  465.8 1.8 copy-done.13
  467.6 5.7 convolution_convert_fusion.1
  473.4 3.8 convolution_convert_fusion.2
  477.2 3.8 fusion
  481.1 4.3 pad_maximum_fusion
  485.3 12.6 %copy.49 = bf16[1536,3072]{1,0:T(8,128)(2,1)} copy(bf16[1536,3072]{0,1:T(8,128)(2,1)} %pad_maximum_fusion) | data formatting | bytes 18874368
  499.9 24.3 %all-reduce.3 = (f32[1536]{0:T(1024)S(1)}, f32[1536]{0:T(1024)S(1)}) all-reduce(f32[1536]{0:T(1024)S(1)} %reduce, f32[1536]{0:T(1024)S(1)} %reduce.1), channel_id=4, replica_groups=mesh['dp'=8,'mp'=4] {'dp'}, use_global_device_ids=true, to_apply=%region_7.8.clone | all-reduce | flops 3072 | bytes 24576
  525.5 6.7 %fusion.1 = bf16[1,1024,1536]{2,1,0:T(8,128)(2,1)} fusion(f32[1024,1536]{1,0:T(8,128)} %get-tuple-element.24.mid, bf16[1024,1536]{1,0:T(8,128)(2,1)S(1)} %copy-done.2), kind=kLoop, calls=%fused_computation.13 | loop fusion | flops 4718592 | bytes 12582912 | tf_op jit(solution)/shard_map/reshape | solution.py:574
  532.3 1.3 copy.48
  537.1 56.0 %reduce-scatter.9.cloned.1.call-done = bf16[192,3072]{1,0:T(8,128)(2,1)} async-done(((bf16[1536,3072]{1,0:T(8,128)(2,1)}), bf16[192,3072]{1,0:T(8,128)(2,1)}) %reduce-scatter.9.cloned.1.call-update) | async-done | bytes 1179664
  593.1 1.6 copy.50
  595.9 1.9 convert_element_type.54
  597.8 2.4 copy.45
  600.2 1.2 copy.44
  601.4 1.3 slice_bitcast_fusion
  602.7 1.2 copy.46
  (73 shorter events, 11.1 us)
Async XLA Ops:
  7.2 10.8 %copy-start.3 = (bf16[384,1536]{1,0:T(8,128)(2,1)S(1)}, bf16[384,1536]{1,0:T(8,128)(2,1)}, u32[]{:S(2)}) copy-start(bf16[384,1536]{1,0:T(8,128)(2,1)} %param.17) | copy-start | bytes 3538948
  7.2 10.8 %copy-start.4 = (bf16[1536,192]{0,1:T(8,128)(2,1)S(1)}, bf16[1536,192]{0,1:T(8,128)(2,1)}, u32[]{:S(2)}) copy-start(bf16[1536,192]{0,1:T(8,128)(2,1)} %param.16) | copy-start | bytes 1769476
  7.2 10.8 %copy-start.5 = (bf16[1536,192]{0,1:T(8,128)(2,1)S(1)}, bf16[1536,192]{0,1:T(8,128)(2,1)}, u32[]{:S(2)}) copy-start(bf16[1536,192]{0,1:T(8,128)(2,1)} %param.15) | copy-start | bytes 1769476
  7.2 371.7 %all-reduce.7.cloned.1.call-start = ((), (), s32[]{:S(2)}) async-start(), calls=%async_computation.4 | async-start | bytes 12582912 | tf_op jit(solution)/shard_map/psum | solution.py:573
  20.0 108.3 %copy-start.10 = (bf16[1536,1024]{1,0:T(8,128)(2,1)S(1)}, bf16[1536,1024]{1,0:T(8,128)(2,1)}, u32[]{:S(2)}) copy-start(bf16[1536,1024]{1,0:T(8,128)(2,1)} %param.19) | copy-start | bytes 9437188
  128.3 5.5 copy-start.9
  128.3 5.5 copy-start.12
  133.8 3.4 copy-start
  133.8 3.4 copy-start.8
  143.6 5.0 copy-start.17
  143.6 5.0 copy-start.15
  148.6 3.5 copy-start.11
  148.6 3.5 copy-start.19
  157.0 375.3 %reduce-scatter.7.cloned.1.call-start = ((), (), s32[]{:S(2)}) async-start(), calls=%async_computation.2 | async-start | bytes 3981312
  465.7 1.9 copy-start.13
  465.7 127.3 %reduce-scatter.9.cloned.1.call-start = ((), (), s32[]{:S(2)}) async-start(), calls=%async_computation.3 | async-start | bytes 10616832
  467.6 5.8 copy-start.16
  473.4 3.8 copy-start.1
  473.4 3.8 copy-start.18
  498.0 0.7 copy-start.14
  498.0 1.9 copy-start.7
  498.0 1.9 copy-start.6
  498.0 27.6 %copy-start.2 = (bf16[1024,1536]{1,0:T(8,128)(2,1)S(1)}, bf16[1024,1536]{1,0:T(8,128)(2,1)}, u32[]{:S(2)}) copy-start(bf16[1024,1536]{1,0:T(8,128)(2,1)} %get-tuple-element.72) | copy-start | bytes 9437188
Sparse Core Ops, SparseCore 0:
  157.1 221.7 all-reduce.6
  465.9 47.1 reduce-scatter.6
  516.6 76.4 reduce-scatter.8

commit v2 on v1

v2 whole, which is shorter than its diff:
```python
import functools

import jax
import jax.numpy as jnp
from jax import lax
from jax.experimental import pallas as pl
from jax.experimental.pallas import tpu as pltpu
from jax.sharding import PartitionSpec as P

D = 1536
HD = 96
ROW = 1024
SEGS = 4
NZ = 4
CH = 256
TB = 128
BL = 64
LAG = 2
RING = 10
HQ_OWN = 4
KV_OWN = 2
QR = HQ_OWN * HD
KR = KV_OWN * HD
QKV = QR + 2 * KR
WR = QKV + QR
SCALE = HD ** -0.5
C2 = SCALE * 1.4426950408889634
NEG = -1e30
eps = 1e-05
rope_base = 100000.0
f32 = jnp.float32
bf16 = jnp.bfloat16
MESH = pl.DeviceIdType.MESH
ANY = pl.BlockSpec(memory_space=pl.ANY)
VM = pl.BlockSpec(memory_space=pltpu.VMEM)
DMA = pltpu.SemaphoreType.DMA
sds = jax.ShapeDtypeStruct


def nt(a, b):
    return lax.dot_general(a, b, (((1,), (1,)), ((), ())), preferred_element_type=f32)


def nn(a, b):
    return lax.dot_general(a, b, (((1,), (0,)), ((), ())), preferred_element_type=f32)


def tn(a, b):
    return lax.dot_general(a, b, (((0,), (0,)), ((), ())), preferred_element_type=f32)


def chunk(c, size=CH):
    return pl.ds(pl.multiple_of(c * size, size), size)


def places():
    dp = lax.axis_index("dp")
    z = lax.axis_index("mp")
    low = lax.rem(dp, 8)
    return dp, z, low


def partner(low, dp, bit):
    on = lax.rem(low // bit, 2)
    return dp + bit - 2 * bit * on


def greet(dp, z, low):
    barrier = pltpu.get_barrier_semaphore()
    for bit in (1, 2, 4):
        pl.semaphore_signal(barrier, inc=1, device_id={"dp": partner(low, dp, bit)}, device_id_type=MESH)
    for other in (1, 2, 3):
        pl.semaphore_signal(barrier, inc=1, device_id={"mp": lax.rem(z + other, NZ)}, device_id_type=MESH)
    pl.semaphore_wait(barrier, 6)


def put(src, dst, ssem, rsem, dev):
    return pltpu.make_async_remote_copy(
        src_ref=src, dst_ref=dst, send_sem=ssem, recv_sem=rsem, device_id=dev, device_id_type=MESH)


def split3(v):
    hi = v.astype(bf16).astype(f32)
    rest = v - hi
    mid = rest.astype(bf16).astype(f32)
    return hi, mid, rest - mid


def extra_rows(base, v, first):
    row = lax.broadcasted_iota(jnp.int32, base.shape, 0)
    out = base
    for i, part in enumerate(split3(v)):
        out = jnp.where(row == first + i, part, out)
    return out.astype(bf16)


def project(w, hid, qt, kt, kk, vt, vv, cos, sin, qaug, kaug, s, c):
    cols = chunk(c)
    t = nt(w[s, 0:QKV], hid[cols])
    co = cos[:, cols]
    si = sin[:, cols]

    def rot(u):
        a = u[0:HD // 2]
        b = u[HD // 2:HD]
        return jnp.concatenate([a * co - b * si, b * co + a * si], axis=0).astype(bf16)

    for h in range(HQ_OWN):
        qt[HQ_OWN * s + h, 0:HD, cols] = rot(t[HD * h:HD * h + HD])
        qt[HQ_OWN * s + h, HD:128, cols] = qaug[:, cols]
    for h in range(KV_OWN):
        g = KV_OWN * s + h
        k = jnp.concatenate([rot(t[QR + HD * h:QR + HD * h + HD]), kaug[:, cols]], axis=0)
        kt[g, :, cols] = k
        kk[g, cols, :] = k.T
        v = t[QR + KR + HD * h:QR + KR + HD * h + HD].astype(bf16)
        v = jnp.concatenate([v, jnp.ones((128 - HD, CH), bf16)], axis=0)
        vt[g, :, cols] = v
        vv[g, cols, :] = v.T


def attend(qt, kk, vt, ho, qaug, g):
    for qb in range(ROW // CH):
        lo = qb * CH
        nk = lo + CH
        q = jnp.concatenate([qt[2 * g, :, lo:nk], qt[2 * g + 1, :, lo:nk]], axis=1)
        st = nn(kk[g, 0:nk, :], q)
        ki = lax.broadcasted_iota(jnp.int32, (CH, CH), 0)
        qi = lax.broadcasted_iota(jnp.int32, (CH, CH), 1)
        keep = jnp.concatenate([ki <= qi, ki <= qi], axis=1)
        dg = jnp.where(keep, st[lo:nk], NEG)
        m = jnp.max(dg, axis=0, keepdims=True)
        if qb:
            m = jnp.maximum(m, jnp.max(st[0:lo], axis=0, keepdims=True))
        mc = m * C2
        o = nn(vt[g, :, lo:nk], jnp.exp2(dg * C2 - mc).astype(bf16))
        if qb:
            o = o + nn(vt[g, :, 0:lo], jnp.exp2(st[0:lo] * C2 - mc).astype(bf16))
        total = o[HD:HD + 1]
        r = (o[0:HD] / total).astype(bf16)
        back = (mc + jnp.log2(total)) * (-1.0 / C2)
        for h in range(2):
            part = slice(h * CH, (h + 1) * CH)
            ho[pl.ds(pl.multiple_of(g * 2 * HD + h * HD, 32), HD), lo:nk] = r[:, part]
            base = qaug[:, lo:nk].astype(f32)
            qt[2 * g + h, HD:128, lo:nk] = extra_rows(base, back[:, part], SEGS)


def order(z, j):
    right = (0, 1, 2, 3), (1, 0, 2, 3), (2, 3, 1, 0), (3, 2, 1, 0)
    s = jnp.int32(0)
    for i in range(NZ):
        s = s + jnp.where(z == i, right[i][j], 0)
    return s


GPARTS = ((0, QKV // 8, 48), (QKV, QR // 8, 32))


def forward_kernel(x, gain, gain2, cos, sin, qaug, kaug, own, cot,
                   mid_o, hid2_o, ho_o, qt_o, kt_o, kk_o, vv_o, w_o, hid1t_o, hid2t_o, cott_o,
                   w, hid, ho, qt, kt, kk, vt, vv, midb, hidb, hidtb, cb, ctb,
                   zsend, zrecv, xsend, xrecv, ysend, yrecv, csend, crecv, osem, wsem, msem, tsem):
    dp, z, low = places()
    pc, px, py = (partner(low, dp, bit) for bit in (1, 2, 4))
    lx = px - dp + low
    ly = py - dp + low
    lxy = ly + lx - low
    load = pltpu.make_async_copy(own, w.at[z], wsem.at[0])
    load.start()
    greet(dp, z, low)
    load.wait()

    def rows(part, where, lo, hi):
        base, size, _ = GPARTS[part]
        return pl.ds(pl.multiple_of(base + where * size + lo, 16), hi - lo)

    def zcopy(part, d, s):
        r = rows(part, low, 0, GPARTS[part][1])
        to = lax.rem(z + d, NZ)
        return put(w.at[s, r], w.at[s, r], zsend.at[part, d - 1], zrecv.at[part, s], {"mp": to})

    for part in range(2):
        for hop in (1, 2, 3):
            for sign in (1, -1):
                to = z + sign * hop

                @pl.when((to >= 0) & (to < NZ))
                def _(part=part, hop=hop, sign=sign):
                    zcopy(part, (sign * hop) % NZ, z).start()

    def copies(part, j, kind):
        s = order(z, j)
        base, size, cut = GPARTS[part]
        a, b, both = (0, cut), (cut, size), (0, size)
        if part == 1:
            a, b = (0, size - 32), (size - 32, size)

        def c(where, half, sems, semr, i, dev):
            r = rows(part, where, *half)
            return put(w.at[s, r], w.at[s, r], sems.at[part, j - 1, i], semr.at[part, j - 1, i], {"dp": dev})

        if kind == 1:
            return [c(low, a, xsend, xrecv, 0, px), c(low, b, ysend, yrecv, 0, py)]
        if kind == 2:
            return [c(low, a, ysend, yrecv, 1, py), c(lx, a, ysend, yrecv, 2, py),
                    c(low, b, xsend, xrecv, 1, px), c(ly, b, xsend, xrecv, 2, px)]
        return [c(at, both, csend, crecv, i, pc) for i, at in enumerate((low, lx, ly, lxy))]

    def stage(part, j, k):
        if k == 1:
            zcopy(part, 1, order(z, j)).wait_recv()
        else:
            for c in copies(part, j, k - 1):
                c.wait_recv()
        if k < 4:
            for c in copies(part, j, k):
                c.start()

    def norm(c, _):
        r = chunk(c)
        xx = x[r].astype(f32)
        f = lax.rsqrt(jnp.mean(xx * xx, axis=1, keepdims=True) + eps)
        h = (xx * f * gain[...].astype(f32)).astype(bf16)
        hid[r] = h
        turned(c, h, hid1t_o)
        return 0

    def turn_copy(c, dst):
        return pltpu.make_async_copy(ctb.at[lax.rem(c, 2)], dst.at[:, chunk(c)], tsem.at[0, lax.rem(c, 2)])

    def turned(c, v, dst):
        pl.when(c >= 2)(lambda: turn_copy(c - 2, dst).wait())
        ctb[lax.rem(c, 2)] = v.T
        turn_copy(c, dst).start()

    def turn_end(dst):
        for c in (ROW // CH - 2, ROW // CH - 1):
            turn_copy(c, dst).wait()

    def cot_load(c):
        return pltpu.make_async_copy(cot.at[chunk(c)], cb.at[lax.rem(c, 2)], tsem.at[1, lax.rem(c, 2)])

    def turn_cot(c, _):
        pl.when(c + 1 < ROW // CH)(lambda: cot_load(c + 1).start())
        cot_load(c).wait()
        turned(c, cb[lax.rem(c, 2)], cott_o)
        return 0

    cot_load(0).start()
    lax.fori_loop(0, ROW // CH, norm, 0)
    turn_end(hid1t_o)

    def projections(s):
        def one(c, _):
            project(w, hid, qt, kt, kk, vt, vv, cos, sin, qaug, kaug, s, c)
            return 0

        lax.fori_loop(0, ROW // CH, one, 0)

    def attends(s):
        def one(g, _):
            attend(qt, kk, vt, ho, qaug, KV_OWN * s + g)
            return 0

        lax.fori_loop(0, KV_OWN, one, 0)

    events = {
        "0a": ((0, 1, 1),),
        "0b": ((0, 1, 2), (0, 2, 1), (0, 1, 3), (0, 2, 2), (0, 3, 1), (0, 1, 4)),
        "1a": ((0, 2, 3), (0, 3, 2), (1, 1, 1)),
        "1b": ((0, 2, 4), (0, 3, 3), (1, 1, 2), (1, 2, 1)),
        "2a": ((0, 3, 4), (1, 1, 3), (1, 2, 2), (1, 3, 1)),
        "2b": ((1, 1, 4), (1, 2, 3), (1, 3, 2)),
        "3a": ((1, 2, 4), (1, 3, 3)),
        "3b": ((1, 3, 4),),
    }
    for j in range(NZ):
        s = order(z, j)
        if j == 1:
            lax.fori_loop(0, ROW // CH, turn_cot, 0)
            turn_end(cott_o)
        projections(s)
        for e in events[f"{j}a"]:
            stage(*e)
        attends(s)
        for e in events[f"{j}b"]:
            stage(*e)
    outs = [(w, w_o), (qt, qt_o), (kt, kt_o), (kk, kk_o), (vv, vv_o), (ho, ho_o)]
    writes = [pltpu.make_async_copy(a, b, osem.at[i]) for i, (a, b) in enumerate(outs)]
    for c in writes:
        c.start()

    def mid_copies(c, slot):
        return (pltpu.make_async_copy(midb.at[slot], mid_o.at[chunk(c)], msem.at[0, slot]),
                pltpu.make_async_copy(hidb.at[slot], hid2_o.at[chunk(c)], msem.at[1, slot]),
                pltpu.make_async_copy(hidtb.at[slot], hid2t_o.at[:, chunk(c)], msem.at[2, slot]))

    def out_proj(c, _):
        r = chunk(c)
        slot = lax.rem(c, 2)

        @pl.when(c >= 2)
        def _():
            for m in mid_copies(c - 2, slot):
                m.wait()

        acc = x[r].astype(f32)
        for s in range(NZ):
            acc = acc + tn(ho[QR * s:QR * s + QR, r], w[s, QKV:WR])
        midb[slot] = acc
        f = lax.rsqrt(jnp.mean(acc * acc, axis=1, keepdims=True) + eps)
        h = (acc * f * gain2[...].astype(f32)).astype(bf16)
        hidb[slot] = h
        hidtb[slot] = h.T
        for m in mid_copies(c, slot):
            m.start()
        return 0

    n = ROW // CH
    lax.fori_loop(0, n, out_proj, 0)
    for c in range(max(n - 2, 0), n):
        for m in mid_copies(c, c % 2):
            m.wait()
    for c in writes:
        c.wait()
    for part in range(2):
        for d in (1, 2, 3):
            zcopy(part, d, z).wait_send()
        for j in (1, 2, 3):
            for kind in (1, 2, 3):
                for c in copies(part, j, kind):
                    c.wait_send()


def forward(x, gain, gain2, cos, sin, qaug, kaug, own, cot):
    heads = NZ * HQ_OWN
    kv = NZ * KV_OWN
    vm = pltpu.VMEM
    return pl.pallas_call(
        forward_kernel,
        out_shape=(sds((ROW, D), f32), sds((ROW, D), bf16), sds((heads * HD, ROW), bf16),
                   sds((heads, 128, ROW), bf16), sds((kv, 128, ROW), bf16), sds((kv, ROW, 128), bf16),
                   sds((kv, ROW, 128), bf16), sds((NZ, WR, D), bf16), sds((D, ROW), bf16), sds((D, ROW), bf16),
                   sds((D, ROW), bf16)),
        in_specs=[VM] * 7 + [ANY] * 2,
        out_specs=(ANY,) * 11,
        scratch_shapes=[
            vm((NZ, WR, D), bf16), vm((ROW, D), bf16), vm((heads * HD, ROW), bf16),
            vm((heads, 128, ROW), bf16), vm((kv, 128, ROW), bf16), vm((kv, ROW, 128), bf16),
            vm((kv, 128, ROW), bf16), vm((kv, ROW, 128), bf16), vm((2, CH, D), f32), vm((2, CH, D), bf16),
            vm((2, D, CH), bf16), vm((2, CH, D), bf16), vm((2, D, CH), bf16),
            DMA((2, 3)), DMA((2, NZ)), DMA((2, 3, 3)), DMA((2, 3, 3)), DMA((2, 3, 3)), DMA((2, 3, 3)),
            DMA((2, 3, 4)), DMA((2, 3, 4)), DMA((6,)), DMA((1,)), DMA((3, 2)), DMA((2, 2))],
        compiler_params=pltpu.CompilerParams(
            collective_id=1, has_side_effects=True, vmem_limit_bytes=60 * 2**20),
        name="attention_forward",
    )(x, gain, gain2, cos, sin, qaug, kaug, own, cot)


def tables(lengths):
    finish = jnp.cumsum(lengths)
    starts = finish - lengths
    place = jnp.arange(ROW, dtype=jnp.int32)
    segment = jnp.sum((place[None, :] >= finish[:, None]).astype(jnp.int32), axis=0)
    chosen = segment[None, :] == jnp.arange(SEGS, dtype=jnp.int32)[:, None]
    offsets = jnp.sum(jnp.where(chosen, starts[:, None], 0), axis=0)
    positions = (place - offsets).astype(f32)
    freqs = rope_base ** (-(jnp.arange(HD // 2, dtype=f32) * 2.0) / HD)
    angles = freqs[:, None] * positions[None, :]
    rest = 128 - HD - SEGS
    qaug = jnp.concatenate([jnp.where(chosen, 0.0, NEG), jnp.zeros((rest, ROW))], axis=0).astype(bf16)
    kaug = jnp.concatenate([chosen.astype(f32), jnp.ones((3, ROW)), jnp.zeros((rest - 3, ROW))], axis=0).astype(bf16)
    return jnp.cos(angles), jnp.sin(angles), qaug, kaug


class RowSum:
    def __init__(self, z, own, rend, rmid, out, ssem, esem, msem, osem, ring, lag):
        self.z, self.own, self.ring, self.lag = z, own, ring, lag
        self.rend, self.rmid, self.out = rend, rmid, out
        self.ssem, self.esem, self.msem, self.osem = ssem, esem, msem, osem

    def who(self, i):
        odd = lax.rem(i, 2)
        return 3 * odd, 1 + odd, 2 - odd, 3 - 3 * odd

    def copy(self, kind, i, to, sem=0):
        s = lax.rem(i, self.ring)
        src, dst, rsem = {
            "end": (self.own(i), self.rend.at[s], self.esem),
            "mid": (self.rmid.at[s], self.rmid.at[s], self.msem),
            "out": (self.out.at[s], self.out.at[s], self.osem)}[kind]
        return put(src, dst, self.ssem.at[sem, s], rsem.at[s], {"mp": to})

    def on(self, place, f):
        pl.when(self.z == place)(f)

    def step1(self, i):
        e, o, m, f = self.who(i)
        self.on(e, lambda: self.copy("end", i, o).start())
        self.on(f, lambda: self.copy("end", i, m).start())

    def step2(self, i):
        e, o, m, f = self.who(i)
        s = lax.rem(i, self.ring)

        def go():
            self.copy("end", i, o).wait_recv()
            self.rmid[s] = (self.own(i)[...].astype(f32) + self.rend[s].astype(f32)).astype(bf16)
            self.copy("mid", i, o).start()

        self.on(m, go)

    def step3(self, i):
        e, o, m, f = self.who(i)
        s = lax.rem(i, self.ring)

        def go():
            self.copy("end", i, e).wait_recv()
            self.copy("mid", i, e).wait_recv()
            self.out[s] = (self.own(i)[...].astype(f32) + self.rend[s].astype(f32)
                           + self.rmid[s].astype(f32)).astype(bf16)
            self.copy("out", i, m, 1).start()
            self.copy("out", i, e).start()

        self.on(o, go)

    def step4(self, i):
        e, o, m, f = self.who(i)

        def go():
            self.copy("out", i, o).wait_recv()
            self.copy("out", i, f, 1).start()

        self.on(m, go)

    def arrive(self, i):
        e, o, m, f = self.who(i)
        self.on(e, lambda: self.copy("out", i, o).wait_recv())
        self.on(f, lambda: self.copy("out", i, m).wait_recv())

    def drain(self, i):
        e, o, m, f = self.who(i)
        self.on(e, lambda: self.copy("end", i, o).wait_send())
        self.on(f, lambda: self.copy("end", i, m).wait_send())

        def middle():
            self.copy("mid", i, o).wait_send()
            self.copy("out", i, f, 1).wait_send()

        def owner():
            self.copy("out", i, m, 1).wait_send()
            self.copy("out", i, e).wait_send()

        self.on(m, middle)
        self.on(o, owner)

    def tick(self, t, count, finish):
        def last(i):
            self.arrive(i)
            finish(i)
            self.drain(i)

        for lag, step in ((4, last), (3, self.step4), (2, self.step3), (1, self.step2), (0, self.step1)):
            i = t - lag * self.lag
            pl.when((i >= 0) & (i < count))(functools.partial(step, i))


class GradSum:
    def __init__(self, dp, low, width, cut, g, c1, x1, y1, x2, y2, ssem, rsem, out, wide=False):
        self.pc, self.px, self.py = (partner(low, dp, bit) for bit in (1, 2, 4))
        self.c, self.x, self.y = lax.rem(low, 2), lax.rem(low // 2, 2), low // 4
        self.g, self.c1, self.x1, self.y1, self.x2, self.y2 = g, c1, x1, y1, x2, y2
        self.ssem, self.rsem, self.out = ssem, rsem, out
        self.width, self.cut, self.wide = width, cut, wide

    def cols(self, u, lo, hi):
        if self.wide:
            return (pl.ds(pl.multiple_of(u * self.width + lo, 128), hi - lo),)
        return (pl.ds(lo, hi - lo),)

    def part(self, u, *at, lo=None, hi=None):
        lo, hi = (0, self.width) if lo is None else (lo, hi)
        return (() if self.wide else (u,)) + at + self.cols(u, lo, hi)

    def put_block(self, u, k, res):
        self.put_part(u, k, 0, self.width, res)

    def put_part(self, u, k, lo, hi, res):
        self.g[self.part(u, k // 4, (k // 2) % 2, k % 2, slice(None), lo=lo, hi=hi)] = res.astype(bf16)

    def copies(self, u, k):
        g, c, x, y = self.g, self.c, self.x, self.y
        every = slice(None)
        a = dict(lo=0, hi=self.cut)
        b = dict(lo=self.cut, hi=self.width)

        def mk(i, src, dst, dev):
            return put(src, dst, self.ssem.at[u, i], self.rsem.at[u, i], {"dp": dev})

        if k == 0:
            return [mk(0, g.at[self.part(u, every, every, 1 - c, every)], self.c1.at[u], self.pc)]
        if k == 1:
            return [mk(1, g.at[self.part(u, every, 1 - x, c, every, **a)], self.x1.at[u], self.px),
                    mk(2, g.at[self.part(u, 1 - y, every, c, every, **b)], self.y1.at[u], self.py)]
        return [mk(3, g.at[self.part(u, 1 - y, x, c, every, **a)], self.y2.at[u], self.py),
                mk(4, g.at[self.part(u, y, 1 - x, c, every, **b)], self.x2.at[u], self.px)]

    def start(self, u):
        for c in self.copies(u, 0):
            c.start()

    def stage(self, k, u):
        width, cut = self.width, self.cut
        g, c, x, y = self.g, self.c, self.x, self.y
        for cp in self.copies(u, k - 1):
            cp.wait_recv()

        def at(i, j, lo, hi):
            return self.part(u, i, j, c, slice(None), lo=lo, hi=hi)

        def add(i, j, lo, hi, other):
            g[at(i, j, lo, hi)] = (g[at(i, j, lo, hi)].astype(f32) + other.astype(f32)).astype(bf16)

        if k == 1:
            for i in range(2):
                for j in range(2):
                    add(i, j, 0, width, self.c1[u, i, j])
        elif k == 2:
            for i in range(2):
                add(i, x, 0, cut, self.x1[u, i])
                add(y, i, cut, width, self.y1[u, i])
        else:
            self.out[:, pl.ds(pl.multiple_of(u * width, 128), cut)] = (
                g[at(y, x, 0, cut)].astype(f32) + self.y2[u].astype(f32))
            self.out[:, pl.ds(pl.multiple_of(u * width + cut, 128), width - cut)] = (
                g[at(y, x, cut, width)].astype(f32) + self.x2[u].astype(f32))
        if k < 3:
            for cp in self.copies(u, k):
                cp.start()

    def drain(self, u):
        for k in range(3):
            for cp in self.copies(u, k):
                cp.wait_send()


def sum_scratch(count, width, cut):
    vm = pltpu.VMEM
    rest = width - cut
    return [vm((count, 2, 2, 2, 192, width), bf16), vm((count, 2, 2, 192, width), bf16),
            vm((count, 2, 192, cut), bf16), vm((count, 2, 192, rest), bf16),
            vm((count, 192, rest), bf16), vm((count, 192, cut), bf16), DMA((count, 5)), DMA((count, 5))]


def ring_scratch(ring, rows):
    vm = pltpu.VMEM
    return [vm((ring, rows, D), bf16), vm((ring, rows, D), bf16), vm((ring, rows, D), bf16),
            DMA((2, ring)), DMA((ring,)), DMA((ring,)), DMA((ring,))]


MLP_UNITS = 6
MLP_WIDTH = 512


def feed_kernel(gain2, hid2, cot, mid, hid2t_i, cott_i, gw_i, uw_i, dw_i,
                mlp_o, gm_o, gml_o, gmlt_o, gain2_o, grad_o,
                gw, uw, dw, a3, side, own, hb, cb, tb, mb, cb2, gmb, gmlb, gmltb,
                rend, rmid, out, zs, ze, zm, zo,
                g, c1, x1, y1, x2, y2, gs, gr,
                lsem, bsem, tsem, msem, wsem):
    dp, z, low = places()
    loads = [pltpu.make_async_copy(a, b, lsem.at[i]) for i, (a, b) in enumerate(
        ((gw_i, gw), (uw_i, uw), (dw_i, dw), (hid2t_i, side), (cott_i, side)))]
    nc = ROW // CH
    nb = ROW // BL
    nj = ROW // 128
    pair = 128 // BL

    def chunk_loads(c):
        return [pltpu.make_async_copy(src.at[chunk(c)], dst.at[lax.rem(c, 2)], bsem.at[i, lax.rem(c, 2)])
                for i, (src, dst) in enumerate(((hid2, hb), (cot, cb)))]

    for c in chunk_loads(0):
        c.start()
    for c in loads[:4]:
        c.start()
    greet(dp, z, low)
    zsum = RowSum(z, lambda i: own.at[chunk(i, BL)], rend, rmid, out, zs, ze, zm, zo, RING, LAG)
    gsum = GradSum(dp, low, MLP_WIDTH, MLP_WIDTH // 2, g, c1, x1, y1, x2, y2, gs, gr, grad_o)
    gain2_o[...] = jnp.zeros_like(gain2_o)

    def gm_loads(j):
        r = chunk(j, 128)
        return [pltpu.make_async_copy(mid.at[r], mb, msem.at[0]),
                pltpu.make_async_copy(cot.at[r], cb2, msem.at[1])]

    def gm_writes(j):
        r = chunk(j, 128)
        s = lax.rem(j, 2)
        return [pltpu.make_async_copy(gmb.at[s], gm_o.at[r], wsem.at[0, s]),
                pltpu.make_async_copy(gmlb.at[s], gml_o.at[r], wsem.at[1, s]),
                pltpu.make_async_copy(gmltb.at[s], gmlt_o.at[:, r], wsem.at[2, s])]

    def finish_pair(j):
        s = lax.rem(j, 2)
        for c in gm_loads(j):
            c.wait()

        @pl.when(j >= 2)
        def _():
            for c in gm_writes(j - 2):
                c.wait()

        gh = jnp.concatenate([out[lax.rem(j * pair + k, RING)] for k in range(pair)], axis=0).astype(f32)
        m = mb[...]
        f = lax.rsqrt(jnp.mean(m * m, axis=1, keepdims=True) + eps)
        n = m * f
        gn = gh * n
        gain2_o[...] += jnp.sum(gn, axis=0, keepdims=True)
        ga = gain2[...].astype(f32)
        gm = cb2[...].astype(f32) + f * (gh * ga - n * jnp.mean(gn * ga, axis=1, keepdims=True))
        gmb[s] = gm
        low_gm = gm.astype(bf16)
        gmlb[s] = low_gm
        gmltb[s] = low_gm.T
        for c in gm_writes(j):
            c.start()

        @pl.when(j + 1 < nj)
        def _():
            for c in gm_loads(j + 1):
                c.start()

    def finish(i):
        pl.when(lax.rem(i, pair) == pair - 1)(lambda: finish_pair(i // pair))

    for c in gm_loads(0):
        c.start()

    def tick(t):
        zsum.tick(t, nb, finish)

    def mlp_write(c):
        return pltpu.make_async_copy(tb.at[lax.rem(c, 2)], mlp_o.at[chunk(c)], tsem.at[lax.rem(c, 2)])

    def mlp_chunk(c, _):
        r = chunk(c)
        s = lax.rem(c, 2)
        for cp in chunk_loads(c):
            cp.wait()

        @pl.when(c + 1 < nc)
        def _():
            for cp in chunk_loads(c + 1):
                cp.start()

        @pl.when(c == 0)
        def _():
            loads[0].wait()
            loads[1].wait()
            loads[2].wait()

        gate = nn(hb[s], gw[...])
        upper = nn(hb[s], uw[...])
        ga = nt(cb[s], dw[...])
        sigma = 1.0 / (1.0 + jnp.exp(-gate))
        silu = gate * sigma
        gg = (ga * upper * sigma * (1.0 + gate * (1.0 - sigma))).astype(bf16)
        gu = (ga * silu).astype(bf16)
        act = (silu * upper).astype(bf16)
        a3[0, r] = gg
        a3[1, r] = gu
        a3[2, r] = act
        own[r] = (nt(gg, gw[...]) + nt(gu, uw[...])).astype(bf16)
        tick(2 * c)

        @pl.when(c >= 2)
        def _():
            mlp_write(c - 2).wait()

        tb[s] = nn(act, dw[...]).astype(bf16)
        mlp_write(c).start()
        tick(2 * c + 1)
        return 0

    def unit(u):
        @pl.when(u == 0)
        def _():
            loads[3].wait()

        @pl.when(u == 4)
        def _():
            loads[4].start()
            loads[4].wait()

        which = u // 2
        cols = chunk(lax.rem(u, 2), MLP_WIDTH)
        rhs = a3[which, :, cols]
        for k in range(8):
            gsum.put_block(u, k, nn(side[k * 192:(k + 1) * 192], rhs))
        gsum.start(u)

    def beat(t, _):
        first = 2 * nc
        u = t - first
        pl.when(u < MLP_UNITS)(lambda: unit(u))
        tick(t)
        for k, lag in ((3, 9), (2, 5), (1, 1)):
            v = u - lag
            pl.when((v >= 0) & (v < MLP_UNITS))(functools.partial(gsum.stage, k, v))
        return 0

    lax.fori_loop(0, nc, mlp_chunk, 0)
    lax.fori_loop(2 * nc, nb + 4 * LAG, beat, 0)

    def drains(u, _):
        gsum.drain(u)
        return 0

    lax.fori_loop(0, MLP_UNITS, drains, 0)
    for c in range(max(nc - 2, 0), nc):
        mlp_write(c).wait()
    for j in range(nj - 2, nj):
        for c in gm_writes(j):
            c.wait()


def feed(gain2, hid2, cot, mid, hid2t, cott, gw, uw, dw):
    vm = pltpu.VMEM
    ff = gw.shape[1]
    return pl.pallas_call(
        feed_kernel,
        out_shape=(sds((ROW, D), bf16), sds((ROW, D), f32), sds((ROW, D), bf16), sds((D, ROW), bf16),
                   sds((1, D), f32), sds((D // 8, 3 * ff), f32)),
        in_specs=[VM] + [ANY] * 8,
        out_specs=(ANY, ANY, ANY, ANY, VM, VM),
        scratch_shapes=[
            vm((D, ff), bf16), vm((D, ff), bf16), vm((ff, D), bf16), vm((3, ROW, ff), bf16),
            vm((D, ROW), bf16), vm((ROW, D), bf16),
            vm((2, CH, D), bf16), vm((2, CH, D), bf16), vm((2, CH, D), bf16),
            vm((128, D), f32), vm((128, D), bf16), vm((2, 128, D), f32), vm((2, 128, D), bf16),
            vm((2, D, 128), bf16)]
        + ring_scratch(RING, BL) + sum_scratch(MLP_UNITS, MLP_WIDTH, MLP_WIDTH // 2)
        + [DMA((5,)), DMA((2, 2)), DMA((2,)), DMA((2,)), DMA((3, 2))],
        compiler_params=pltpu.CompilerParams(
            collective_id=2, has_side_effects=True, vmem_limit_bytes=63 * 2**20),
        name="feed_forward",
    )(gain2, hid2, cot, mid, hid2t, cott, gw, uw, dw)


BL3 = 32
RING3 = 10
LAG3 = 2
ATT_UNITS = 5
ATT_WIDTH = 256


def unrotate(u, co, si):
    a = u[0:HD // 2]
    b = u[HD // 2:HD]
    return jnp.concatenate([a * co + b * si, b * co - a * si], axis=0).astype(bf16)


def attend_back(qk, kk, vv, dot, ho, dk, dv, gt, cos, sin, g, gg, qb):
    lo = qb * CH
    hi = lo + CH
    heads = NZ * HQ_OWN * 128
    q = jnp.concatenate([qk[pl.ds(pl.multiple_of((2 * g + h) * 128, 128), 128), lo:hi] for h in range(2)], axis=1)
    parts = []
    for h in range(2):
        do = dot[pl.ds(pl.multiple_of((2 * gg + h) * HD, 32), HD), lo:hi]
        o = ho[pl.ds(pl.multiple_of((2 * g + h) * HD, 32), HD), lo:hi]
        delta = jnp.sum(do.astype(f32) * o.astype(f32), axis=0, keepdims=True)
        extra = extra_rows(jnp.zeros((128 - HD, CH), f32), -delta, 0)
        parts.append(jnp.concatenate([do, extra], axis=0))
    do = jnp.concatenate(parts, axis=1)
    do_t = do.T
    q_t = q.T
    dq = jnp.zeros((128, 2 * CH), f32)
    for kb in range(qb + 1):
        ks = slice(kb * CH, (kb + 1) * CH)
        p = jnp.exp2(nn(kk[g, ks, :], q) * C2)
        if kb == qb:
            ki = lax.broadcasted_iota(jnp.int32, (CH, CH), 0)
            qi = lax.broadcasted_iota(jnp.int32, (CH, CH), 1)
            keep = jnp.concatenate([ki <= qi, ki <= qi], axis=1)
            p = jnp.where(keep, p, 0.0)
        ds = (p * nn(vv[g, ks, :], do)).astype(bf16)
        dvb = nn(p.astype(bf16), do_t)
        dkb = nn(ds, q_t)
        if kb == qb:
            dv[ks, :] = dvb
            dk[ks, :] = dkb
        else:
            dv[ks, :] += dvb
            dk[ks, :] += dkb
        dq = dq + nn(qk[pl.ds(pl.multiple_of(heads + g * 128, 128), 128), ks], ds)
    first = (g // KV_OWN) * QKV + gg * 2 * HD
    for h in range(2):
        at = pl.ds(pl.multiple_of(first + h * HD, 32), HD)
        gt[at, lo:hi] = unrotate(dq[0:HD, h * CH:(h + 1) * CH] * SCALE, cos[:, lo:hi], sin[:, lo:hi])


def backward_kernel(groups, gain, cos, sin, gain2_i, x, mid, mlp, gm, gml_i, gmlt, hid1t, ho_i, qt_i, kt_i, kk_i, vv_i, w_i,
                    out_o, xg_o, grad_o,
                    w, wo, ho, qk, kk, vv, dk, dv, gt, gml, dot, ga1, own, mb2, ob2, xb, gb, ob,
                    rend, rmid, out, zs, ze, zm, zo,
                    c1, x1, y1, x2, y2, gs, gr,
                    lsem, bsem, wsem, psem, osem, isem):
    dp, z, low = places()
    qrows = NZ * HQ_OWN * 128
    loads = [pltpu.make_async_copy(gml_i, gml, lsem.at[0]),
             pltpu.make_async_copy(ho_i, ho, lsem.at[1]),
             pltpu.make_async_copy(kk_i, kk, lsem.at[2]),
             pltpu.make_async_copy(vv_i, vv, lsem.at[3])]
    loads += [pltpu.make_async_copy(w_i.at[s, pl.ds(QKV + 192 * h, 192)], wo.at[s // 2, s % 2, h], lsem.at[4 + 2 * s + h])
              for s in range(NZ) for h in range(2)]
    loads += [pltpu.make_async_copy(qt_i, qk.at[pl.ds(0, qrows)], lsem.at[12]),
              pltpu.make_async_copy(kt_i, qk.at[pl.ds(qrows, NZ * KV_OWN * 128)], lsem.at[13])]
    wloads = [pltpu.make_async_copy(w_i.at[s, pl.ds(0, QKV)], w.at[s], lsem.at[14 + s]) for s in range(NZ)]
    late = [pltpu.make_async_copy(hid1t, qk.at[pl.ds(0, D)], lsem.at[18]),
            pltpu.make_async_copy(gmlt, qk.at[pl.ds(D, D)], lsem.at[19])]
    nb = ROW // BL3
    nt_blocks = ROW // TB

    def own_load(i):
        s = lax.rem(i, RING3)
        return pltpu.make_async_copy(mlp.at[chunk(i, BL3)], own.at[s], isem.at[s])

    def mid_load(i):
        s = lax.rem(i, 2)
        return pltpu.make_async_copy(mid.at[chunk(i, BL3)], mb2.at[s], osem.at[0, s])

    def out_write(i):
        s = lax.rem(i, 2)
        return pltpu.make_async_copy(ob2.at[s], out_o.at[chunk(i, BL3)], osem.at[1, s])

    own_load(0).start()
    own_load(1).start()
    mid_load(0).start()
    for c in loads:
        c.start()
    greet(dp, z, low)
    zsum = RowSum(z, lambda i: own.at[lax.rem(i, RING3)], rend, rmid, out, zs, ze, zm, zo, RING3, LAG3)
    gsum = GradSum(dp, low, ATT_WIDTH, ATT_WIDTH // 2, wo, c1, x1, y1, x2, y2, gs, gr, grad_o, True)

    def finish(i):
        mid_load(i).wait()
        s = lax.rem(i, 2)

        @pl.when(i >= 2)
        def _():
            out_write(i - 2).wait()

        ob2[s] = (mb2[s] + out[lax.rem(i, RING3)].astype(f32)).astype(bf16)
        out_write(i).start()

        @pl.when(i + 1 < nb)
        def _():
            mid_load(i + 1).start()

    def tick(t):
        pl.when(t < nb)(lambda: own_load(t).wait())
        zsum.tick(t, nb, finish)
        pl.when(t + 2 < nb)(lambda: own_load(t + 2).start())

    def quarter(s, _):
        @pl.when(s == 0)
        def _():
            for c in loads:
                c.wait()
            for c in wloads:
                c.start()

        for h in range(2):
            t = nt(wo[s // 2, lax.rem(s, 2), h], gml[...])
            dot[h * 192:(h + 1) * 192, :] = t.astype(bf16)
        tick(s * (1 + KV_OWN * 4))

        def one(gg, _):
            g = KV_OWN * s + gg
            for qb in range(ROW // CH):
                attend_back(qk, kk, vv, dot, ho, dk, dv, gt, cos, sin, g, gg, qb)
                tick(s * (1 + KV_OWN * 4) + 1 + gg * 4 + qb)
            first = pl.multiple_of(s * QKV + QR + gg * HD, 32)
            gt[pl.ds(first, HD), :] = unrotate(dk[...].T[0:HD] * SCALE, cos[...], sin[...])
            gt[pl.ds(pl.multiple_of(first + KR, 32), HD), :] = dv[...].T[0:HD].astype(bf16)
            return 0

        lax.fori_loop(0, KV_OWN, one, 0)
        return 0

    lax.fori_loop(0, NZ, quarter, 0)
    beats = NZ * (1 + KV_OWN * 4)
    for c in late:
        c.start()
    for c in wloads + late:
        c.wait()

    def qkv_unit(u, _):
        rhs = gt[pl.ds(pl.multiple_of(z * QKV + u * ATT_WIDTH, 128), ATT_WIDTH), :]
        for k in range(8):
            gsum.put_block(u, k, nt(qk[k * 192:(k + 1) * 192, :], rhs))
        gsum.start(u)
        tick(beats + u)

        pl.when(u >= 1)(lambda: gsum.stage(1, u - 1))
        return 0

    lax.fori_loop(0, QKV // ATT_WIDTH, qkv_unit, 0)
    beats += QKV // ATT_WIDTH
    o_at = pl.multiple_of(z * QR, 128)
    for k in range(8):
        gsum.put_block(3, k, nt(qk[D + k * 192:D + (k + 1) * 192, :], ho[pl.ds(o_at, ATT_WIDTH), :]))
    gsum.start(3)
    for k in range(8):
        r = nt(qk[D + k * 192:D + (k + 1) * 192, :], ho[pl.ds(o_at + ATT_WIDTH, QR - ATT_WIDTH), :])
        gsum.put_part(4, k, 0, QR - ATT_WIDTH, r)
    gsum.stage(1, 2)

    def tail_loads(b, slot):
        r = chunk(b, TB)
        return [pltpu.make_async_copy(x.at[r], xb.at[slot], bsem.at[0, slot]),
                pltpu.make_async_copy(gm.at[r], gb.at[slot], bsem.at[1, slot])]

    def out_copy(b, slot):
        return pltpu.make_async_copy(ob.at[slot], xg_o.at[chunk(b, TB)], psem.at[slot])

    for c in tail_loads(0, 0):
        c.start()
    ga1[...] = jnp.zeros_like(ga1)

    def tail(b, _):
        slot = lax.rem(b, 2)

        @pl.when(b + 1 < nt_blocks)
        def _():
            for c in tail_loads(b + 1, 1 - slot):
                c.start()

        r = chunk(b, TB)
        acc = jnp.zeros((TB, D), f32)
        for s in range(NZ):
            acc = acc + tn(gt[QKV * s:QKV * s + QKV, r], w[s])
        for c in tail_loads(b, slot):
            c.wait()

        @pl.when(b >= 2)
        def _():
            out_copy(b - 2, slot).wait()

        xx = xb[slot].astype(f32)
        f = lax.rsqrt(jnp.mean(xx * xx, axis=1, keepdims=True) + eps)
        n = xx * f
        gn = acc * n
        ga1[...] += jnp.sum(gn, axis=0, keepdims=True)
        ga = gain[...].astype(f32)
        res = gb[slot] + f * (acc * ga - n * jnp.mean(gn * ga, axis=1, keepdims=True))
        ob[slot] = res.astype(bf16)
        out_copy(b, slot).start()
        tick(beats + b)
        pl.when(b == 0)(lambda: gsum.stage(1, 3))
        pl.when((b >= 1) & (b < 5))(lambda: gsum.stage(2, b - 1))
        pl.when(b >= 4)(lambda: gsum.stage(3, b - 4))
        return 0

    lax.fori_loop(0, nt_blocks, tail, 0)
    beats += nt_blocks
    row = lax.broadcasted_iota(jnp.int32, (128, D), 0)
    both = by_block(jnp.where(row == 0, ga1[...], jnp.where(row == 1, gain2_i[...], 0.0)).T, groups)
    for k in range(8):
        gsum.put_part(4, k, QR - ATT_WIDTH, ATT_WIDTH, both[k * 192:(k + 1) * 192])
    gsum.start(4)

    def rest(t, _):
        tick(t)
        return 0

    if beats < nb + 4 * LAG3:
        lax.fori_loop(beats, nb + 4 * LAG3, rest, 0)
    for k in (1, 2, 3):
        gsum.stage(k, 4)

    def drains(u, _):
        gsum.drain(u)
        return 0

    lax.fori_loop(0, ATT_UNITS, drains, 0)
    for b in range(nt_blocks - 2, nt_blocks):
        out_copy(b, b % 2).wait()
    for i in (nb - 2, nb - 1):
        out_write(i).wait()


def backward(groups, gain, cos, sin, gain2_sum, x, mid, mlp, gm, gml, gmlt, hid1t, ho, qt, kt, kk, vv, w):
    vm = pltpu.VMEM
    heads = NZ * HQ_OWN
    kv = NZ * KV_OWN
    return pl.pallas_call(
        functools.partial(backward_kernel, groups),
        out_shape=(sds((ROW, D), bf16), sds((ROW, D), bf16), sds((D // 8, ATT_UNITS * ATT_WIDTH), f32)),
        in_specs=[VM] * 4 + [ANY] * 13,
        out_specs=(ANY, ANY, VM),
        scratch_shapes=[
            vm((NZ, QKV, D), bf16), vm((2, 2, 2, 192, D), bf16), vm((heads * HD, ROW), bf16),
            vm(((heads + kv) * 128, ROW), bf16), vm((kv, ROW, 128), bf16), vm((kv, ROW, 128), bf16),
            vm((ROW, 128), f32), vm((ROW, 128), f32), vm((NZ * QKV, ROW), bf16),
            vm((ROW, D), bf16), vm((QR, ROW), bf16), vm((1, D), f32),
            vm((RING3, BL3, D), bf16), vm((2, BL3, D), f32), vm((2, BL3, D), bf16),
            vm((2, TB, D), bf16), vm((2, TB, D), f32), vm((2, TB, D), bf16)]
        + ring_scratch(RING3, BL3) + sum_scratch(ATT_UNITS, ATT_WIDTH, ATT_WIDTH // 2)[1:]
        + [DMA((20,)), DMA((2, 2)), DMA((2,)), DMA((2,)), DMA((2, 2)), DMA((RING3,))],
        compiler_params=pltpu.CompilerParams(
            collective_id=3, has_side_effects=True, vmem_limit_bytes=63 * 2**20),
        name="attention_backward",
    )(gain, cos, sin, gain2_sum, x, mid, mlp, gm, gml, gmlt, hid1t, ho, qt, kt, kk, vv, w)


def by_block(v, groups):
    if groups == 1:
        return v
    rows, cols = v.shape
    return v.reshape(groups, 8, rows // (8 * groups), cols).transpose(1, 0, 2, 3).reshape(rows, cols)


def body(groups, inputs, lengths, q_weight, k_weight, v_weight, o_weight, gate_weight, up_weight, down_weight,
         attn_gain, mlp_gain, cotangent):
    x = inputs.reshape(ROW, D)
    cot = cotangent.reshape(ROW, D)
    gain = attn_gain.reshape(1, D)
    gain2 = mlp_gain.reshape(1, D)
    ff = gate_weight.shape[1]
    cos, sin, qaug, kaug = tables(lengths[0])
    own = jnp.concatenate([q_weight.T, k_weight.T, v_weight.T, o_weight], axis=0)
    mid, hid2, ho, qt, kt, kk, vv, w, hid1t, hid2t, cott = forward(x, gain, gain2, cos, sin, qaug, kaug, own, cot)
    mlp, gm, gml, gmlt, gain2_sum, mlp_grad = feed(
        gain2, hid2, cot, mid, by_block(hid2t, groups), by_block(cott, groups), gate_weight, up_weight, down_weight)
    output, input_grad, att_grad = backward(
        groups, gain, cos, sin, gain2_sum, x, mid, mlp, gm, gml, by_block(gmlt, groups), by_block(hid1t, groups),
        ho, qt.reshape(-1, ROW), kt.reshape(-1, ROW), kk, vv, w)
    if groups > 1:
        n = 8 * groups
        same = [[g * 8 + low for g in range(groups)] for low in range(8)]

        def over(v):
            return lax.psum_scatter(v, "dp", scatter_dimension=0, axis_index_groups=same, tiled=True)

        mlp_grad, att_grad = over(mlp_grad), over(att_grad)
    return (output.reshape(1, ROW, D), input_grad.reshape(1, ROW, D), att_grad[:, 0:QR], att_grad[:, QR:QR + KR],
            att_grad[:, QR + KR:QKV], att_grad[:, QKV:WR].T, mlp_grad[:, 0:ff], mlp_grad[:, ff:2 * ff],
            mlp_grad[:, 2 * ff:].T, att_grad[:, WR], att_grad[:, WR + 1])


def solution(mesh):
    row = P("dp", None, None)
    in_specs = (row, P("dp", None), P(None, "mp"), P(None, "mp"), P(None, "mp"), P("mp", None),
                P(None, "mp"), P(None, "mp"), P("mp", None), P(), P(), row)
    out_specs = (row, row, P("dp", "mp"), P("dp", "mp"), P("dp", "mp"), P("mp", "dp"),
                 P("dp", "mp"), P("dp", "mp"), P("mp", "dp"), P("dp"), P("dp"))
    return jax.shard_map(functools.partial(body, mesh.shape["dp"] // 8), mesh=mesh, in_specs=in_specs,
                         out_specs=out_specs, check_vma=False)
```

time: 619 us -> 359 us (0.58); the launches traced: 611 us -> 359 us
  waiting for transfers between devices: 278 us -> 0 us
  Pallas kernels: 189 us -> 333 us
  matrix products: 41.9 us -> 0 us
  blocking collectives: 24.3 us -> 0 us
  local copies, waits for them, and re-layouts: 42.3 us -> 18.3 us
  between operations: 15.2 us -> 0.76 us
  other arithmetic: 19.7 us -> 6.04 us
    psum x1 -> x0, waiting for transfers between devices: 222 us -> none  [body(): mlp_out = lax.psum(mlp_term, 'mp').astype(f32)]
    pallas_call x1 -> x2, Pallas kernels: 81 us -> 225 us  [the longest x1 126 us: backward(): pl.pallas_call(functools.partial(backward_kernel, groups), out_shape=(sds...]
    unnamed x5 -> x0, waiting for transfers between devices: 56.1 us -> none
    dot_general x9 -> x0, matrix products: 41.9 us -> none  [the longest x1 6.34 us: body(): jnp.einsum('td,fd->tf', cot, down_weight, preferred_element_type=f32)]
    unnamed x55 -> x13, local copies, waits for them, and re-layouts: 35.4 us -> 6.27 us
    unnamed x1 -> x0, blocking collectives: 24.3 us -> none
    reshape x1 -> x0, other arithmetic: 6.73 us -> none  [body(): output = (mid + mlp_out).astype(bf16).reshape(1, ROW, D)]
  transfers between devices with their start and end apart: 3 -> 0, of which waited for: 2 -> 0; matrix products, arithmetic and copies ran while one was open for 7% -> 0% of each run, Pallas kernels for 0% -> 0%
where the time goes in v2:
time: 359 us
  Pallas kernels  333 us (93%)
  local copies, waits for them, and re-layouts  18.3 us (5%)
  other arithmetic  6.04 us (2%)
    pallas_call x1, Pallas kernels, backward(): pl.pallas_call(functools.partial(backward_kernel, groups), out_shape=(sds...  126 us
    pallas_call x1, Pallas kernels, forward(): pl.pallas_call(forward_kernel, out_shape=(sds((ROW, D), f32), sds((ROW, D...  108 us
    pallas_call x1, Pallas kernels, feed(): pl.pallas_call(feed_kernel, out_shape=(sds((ROW, D), bf16), sds((ROW, D),...  99.1 us

profile of v2, /device:TPU:0, one launch (start us, length us, event | category | flops | bytes accessed | tf_op | source)
XLA Modules:
  0.0 358.6 jit_solution(15807064256279388904)
XLA Ops:
  0.6 0.0 copy-start.2
  0.7 0.0 copy-start.3
  0.7 0.0 copy-start.4
  0.7 1.0 reduce-window.7
  1.7 0.7 bitcast_subtract_fusion
  2.3 0.1 pad.8.clone
  2.4 0.1 pad.7.clone
  2.5 0.1 convert_reduce_fusion
  2.6 0.1 select_reduce_fusion
  2.7 1.3 reshape.88.gain
  4.0 1.3 reshape.92.gain2
  5.3 0.7 maximum_maximum_fusion.kaug
  6.0 0.6 concatenate.10.qaug
  6.6 1.5 multiply_sine_fusion
  8.1 1.6 copy.25
  9.7 0.0 copy-done.2
  9.7 0.0 copy-done.3
  9.7 0.0 copy-done.4
  9.7 2.0 pad_maximum_fusion.own
  11.7 108.1 %attention_forward.1 = (f32[1024,1536]{1,0:T(8,128)}, bf16[1024,1536]{1,0:T(8,128)(2,1)}, bf16[1536,1024]{1,0:T(8,128)(2,1)}, bf16[16,128,1024]{2,1,0:T(8,128)(2...) custom-call(bf16[1024,1536]{1,0:T(8,128)(2,1)} %bitcast.20, ...), custom_call_target="tpu_custom_call" | custom-call | tf_op jit(solution)/shard_map/attention_forward/pallas_call | solution.py:340
  119.8 99.1 %feed_forward.1 = (bf16[1024,1536]{1,0:T(8,128)(2,1)}, f32[1024,1536]{1,0:T(8,128)}, bf16[1024,1536]{1,0:T(8,128)(2,1)}, bf16[1536,1024]{1,0:T(8,128)(2,1)}, f32[1,1536]{1,0:T(1,128)}, /*index=5*/f32[192,3072]{1,0:T(8,128)}) custom-call(bf16[1,1536]{1,0:T(2,128)(2,1)} %reshape.92.gain2, bf16[1024,1536]{1,0:T(8,128)(2,1)} %get-tuple-element.31.hid2, ...), custom_call_target="tpu_custom_call" | custom-call | tf_op jit(solution)/shard_map/feed_forward/pallas_call | solution.py:732
  218.9 126.2 %attention_backward.1 = (bf16[1024,1536]{1,0:T(8,128)(2,1)}, bf16[1024,1536]{1,0:T(8,128)(2,1)}, f32[192,1280]{1,0:T(8,128)}) custom-call(bf16[1,1536]{1,0:T(2,128)(2,1)} %reshape.88.gain, f32[48,1024]{1,0:T(8,128)} %get-tuple-element.61.cos, f32[48,1024]{1,0:T(8,128)} %get-tuple-element.60.sin, f32[1,1536]{1,0:T(1,128)} %get-tuple-element.35.gain2_i, ...), custom_call_target="tpu_custom_call" | custom-call | tf_op jit(solution)/shard_map/attention_backward/pallas_call | solution.py:1000
  345.2 1.8 slice_reduce_fusion
  346.9 1.8 fusion
  348.7 0.0 copy-start.1
  348.7 2.1 slice_bitcast_fusion.1
  350.8 3.1 slice_bitcast_fusion
  353.9 0.0 copy-done.1
  353.9 0.0 copy-start
  353.9 1.7 copy.28
  355.5 1.4 copy-done
  356.9 1.7 copy.29
  (6 shorter events, 0.0 us)
Async XLA Ops:
  0.6 9.1 %copy-start.2 = (bf16[384,1536]{1,0:T(8,128)(2,1)S(1)}, bf16[384,1536]{1,0:T(8,128)(2,1)}, u32[]{:S(2)}) copy-start(bf16[384,1536]{1,0:T(8,128)(2,1)} %param.17) | copy-start | bytes 3538948
  0.7 9.1 %copy-start.3 = (bf16[1536,192]{0,1:T(8,128)(2,1)S(1)}, bf16[1536,192]{0,1:T(8,128)(2,1)}, u32[]{:S(2)}) copy-start(bf16[1536,192]{0,1:T(8,128)(2,1)} %param.16) | copy-start | bytes 1769476
  0.7 9.1 %copy-start.4 = (bf16[1536,192]{0,1:T(8,128)(2,1)S(1)}, bf16[1536,192]{0,1:T(8,128)(2,1)}, u32[]{:S(2)}) copy-start(bf16[1536,192]{0,1:T(8,128)(2,1)} %param.15) | copy-start | bytes 1769476
  348.7 5.1 %copy-start.1 = (bf16[1024,1536]{1,0:T(8,128)(2,1)S(1)}, bf16[1024,1536]{1,0:T(8,128)(2,1)}, u32[]{:S(2)}) copy-start(bf16[1024,1536]{1,0:T(8,128)(2,1)} %get-tuple-element.47) | copy-start | bytes 9437188
  353.9 3.0 copy-start

commit v3 on v2

--- a/solution.py
+++ b/solution.py
@@ -65,13 +65,20 @@
     return dp + bit - 2 * bit * on
 
 
-def greet(dp, z, low):
+def flip(low, mask):
+    for bit in (1, 2, 4):
+        if mask & bit:
+            low = low + bit - 2 * bit * lax.rem(low // bit, 2)
+    return low
+
+
+def greet(dp, z, low, masks=(1, 2, 4)):
     barrier = pltpu.get_barrier_semaphore()
-    for bit in (1, 2, 4):
-        pl.semaphore_signal(barrier, inc=1, device_id={"dp": partner(low, dp, bit)}, device_id_type=MESH)
+    for mask in masks:
+        pl.semaphore_signal(barrier, inc=1, device_id={"dp": dp - low + flip(low, mask)}, device_id_type=MESH)
     for other in (1, 2, 3):
         pl.semaphore_signal(barrier, inc=1, device_id={"mp": lax.rem(z + other, NZ)}, device_id_type=MESH)
-    pl.semaphore_wait(barrier, 6)
+    pl.semaphore_wait(barrier, len(masks) + 3)
 
 
 def put(src, dst, ssem, rsem, dev):
@@ -119,7 +126,7 @@
         vv[g, cols, :] = v.T
 
 
-def attend(qt, kk, vt, ho, qaug, g):
+def attend(qt, kk, vt, ho, qaug, g, between):
     for qb in range(ROW // CH):
         lo = qb * CH
         nk = lo + CH
@@ -144,151 +151,241 @@
             ho[pl.ds(pl.multiple_of(g * 2 * HD + h * HD, 32), HD), lo:nk] = r[:, part]
             base = qaug[:, lo:nk].astype(f32)
             qt[2 * g + h, HD:128, lo:nk] = extra_rows(base, back[:, part], SEGS)
+        if qb % 2:
+            between(qb // 2)
 
 
 def order(z, j):
-    right = (0, 1, 2, 3), (1, 0, 2, 3), (2, 3, 1, 0), (3, 2, 1, 0)
+    places_of = (0, 1, 2, 3), (1, 0, 2, 3), (2, 3, 1, 0), (3, 2, 1, 0)
     s = jnp.int32(0)
-    for i in range(NZ):
-        s = s + jnp.where(z == i, right[i][j], 0)
+    for i, of in enumerate(places_of):
+        for k, quarter in enumerate(of):
+            if quarter:
+                s = s + jnp.where((z == i) & (j == k), quarter, 0)
     return s
 
 
-GPARTS = ((0, QKV // 8, 48), (QKV, QR // 8, 32))
-
-
-def forward_kernel(x, gain, gain2, cos, sin, qaug, kaug, own, cot,
+EVENTS = {
+    3: (("f", 0, 1), ("f", 0, 2), (1, 0, 1)),
+    6: ((2, 0, 1),),
+    7: (("f", 0, 3), ("s", 1, 0), (1, 0, 2)),
+    ("before", 1): ((3, 0, 1), (1, 0, 3), (4, 0, 1)),
+    8: ((2, 0, 2), ("f", 1, 1), ("f", 1, 2)),
+    11: ((2, 0, 3),),
+    13: ((1, 1, 1),),
+    15: (("f", 1, 3),),
+    ("before", 2): ((3, 0, 2), (4, 0, 2)),
+    16: ((1, 1, 2),),
+    20: ((3, 0, 3),),
+    22: ((1, 1, 3), (2, 1, 1)),
+    ("before", 3): ((4, 0, 3),),
+    26: ((2, 1, 2),),
+    27: ((3, 1, 1),),
+    29: ((2, 1, 3), (3, 1, 2)),
+    ("before", 4): ((3, 1, 3),),
+}
+QSLICE = QKV // 8
+OSLICE = QR // 8
+
+
+def forward_kernel(lengths, gains, cos, sin, x_i, qw_i, kw, vw, ow, cot,
                    mid_o, hid2_o, ho_o, qt_o, kt_o, kk_o, vv_o, w_o, hid1t_o, hid2t_o, cott_o,
-                   w, hid, ho, qt, kt, kk, vt, vv, midb, hidb, hidtb, cb, ctb,
+                   x, qw, w, hid, ho, qt, kt, kk, vt, vv, qaug, kaug, midb, hidb, hidtb, cb, ctb,
                    zsend, zrecv, xsend, xrecv, ysend, yrecv, csend, crecv, osem, wsem, msem, tsem):
     dp, z, low = places()
     pc, px, py = (partner(low, dp, bit) for bit in (1, 2, 4))
     lx = px - dp + low
     ly = py - dp + low
     lxy = ly + lx - low
-    load = pltpu.make_async_copy(own, w.at[z], wsem.at[0])
-    load.start()
+    c_at, x_at, y_at = lax.rem(low, 2), lax.rem(low // 2, 2), low // 4
+    own = [pltpu.make_async_copy(qw_i, qw, wsem.at[0])]
+    own += [pltpu.make_async_copy(src, w.at[z, pl.ds(at, n)], wsem.at[i + 1])
+            for i, (src, at, n) in enumerate(((kw, QR, KR), (vw, QR + KR, KR), (ow, QKV, QR)))]
+    own += [pltpu.make_async_copy(x_i, x, wsem.at[4])]
+    for c in own:
+        c.start()
     greet(dp, z, low)
-    load.wait()
-
-    def rows(part, where, lo, hi):
-        base, size, _ = GPARTS[part]
-        return pl.ds(pl.multiple_of(base + where * size + lo, 16), hi - lo)
-
-    def zcopy(part, d, s):
-        r = rows(part, low, 0, GPARTS[part][1])
-        to = lax.rem(z + d, NZ)
-        return put(w.at[s, r], w.at[s, r], zsend.at[part, d - 1], zrecv.at[part, s], {"mp": to})
-
-    for part in range(2):
-        for hop in (1, 2, 3):
-            for sign in (1, -1):
-                to = z + sign * hop
-
-                @pl.when((to >= 0) & (to < NZ))
-                def _(part=part, hop=hop, sign=sign):
-                    zcopy(part, (sign * hop) % NZ, z).start()
+    own[0].wait()
+    w[z, 0:QR] = qw[...].T
+    own[1].wait()
+    own[2].wait()
+
+    def qrows(at, lo=0, hi=QSLICE):
+        return pl.ds(pl.multiple_of(at * QSLICE + lo, 16), hi - lo)
+
+    def orows(half, at, core):
+        return pl.ds(pl.multiple_of(QKV + half * (QR // 2) + (2 * at + core) * OSLICE, 16), OSLICE)
+
+    def zcopies(part, s, side):
+        to = jnp.clip(z + 2 * side - 1, 0, NZ - 1)
+        if part == 0:
+            slices = ((0, qrows(low)),)
+        else:
+            slices = ((1, orows(0, y_at, c_at)), (2, orows(1, x_at, c_at)))
+        return [put(w.at[s, r], w.at[s, r], zsend.at[i, s, side], zrecv.at[i, s], {"mp": to}) for i, r in slices]
+
+    def send_own(part):
+        def go(side):
+            for c in zcopies(part, z, side):
+                c.start()
+
+        for side in (0, 1):
+            pl.when((z < NZ - 1) if side else (z > 0))(functools.partial(go, side))
+
+    send_own(0)
+    own[3].wait()
+    own[4].wait()
 
     def copies(part, j, kind):
         s = order(z, j)
-        base, size, cut = GPARTS[part]
-        a, b, both = (0, cut), (cut, size), (0, size)
+
+        def c(r, sems, semr, i, dev):
+            return put(w.at[s, r], w.at[s, r], sems.at[part, j - 1, i], semr.at[part, j - 1, i], {"dp": dev})
+
         if part == 1:
-            a, b = (0, size - 32), (size - 32, size)
-
-        def c(where, half, sems, semr, i, dev):
-            r = rows(part, where, *half)
-            return put(w.at[s, r], w.at[s, r], sems.at[part, j - 1, i], semr.at[part, j - 1, i], {"dp": dev})
-
+            if kind == 1:
+                return [c(orows(0, y_at, c_at), ysend, yrecv, 0, py), c(orows(1, x_at, c_at), xsend, xrecv, 0, px)]
+            return [c(orows(half, at, c_at), csend, crecv, 2 * half + at, pc) for half in (0, 1) for at in (0, 1)]
+        cut = QSLICE // 2
         if kind == 1:
-            return [c(low, a, xsend, xrecv, 0, px), c(low, b, ysend, yrecv, 0, py)]
+            return [c(qrows(low, 0, cut), xsend, xrecv, 0, px), c(qrows(low, cut), ysend, yrecv, 0, py)]
         if kind == 2:
-            return [c(low, a, ysend, yrecv, 1, py), c(lx, a, ysend, yrecv, 2, py),
-                    c(low, b, xsend, xrecv, 1, px), c(ly, b, xsend, xrecv, 2, px)]
-        return [c(at, both, csend, crecv, i, pc) for i, at in enumerate((low, lx, ly, lxy))]
-
-    def stage(part, j, k):
-        if k == 1:
-            zcopy(part, 1, order(z, j)).wait_recv()
+            return [c(qrows(low, 0, cut), ysend, yrecv, 1, py), c(qrows(lx, 0, cut), ysend, yrecv, 2, py),
+                    c(qrows(low, cut), xsend, xrecv, 1, px), c(qrows(ly, cut), xsend, xrecv, 2, px)]
+        return [c(qrows(at), csend, crecv, i, pc) for i, at in enumerate((low, lx, ly, lxy))]
+
+    def kinds(part):
+        return range(1, 3 if part else 4)
+
+    inner = (z > 0) & (z < NZ - 1)
+
+    def pass_on(part, j):
+        s = order(z, j)
+        return s, jnp.where(s < z, 1, 0)
+
+    def do(kind, part, j):
+        if kind == "s":
+            send_own(part)
+        elif kind == "f":
+            @pl.when(inner)
+            def _():
+                s, side = pass_on(part, j)
+                for c in zcopies(part, s, side):
+                    c.wait_recv()
+                    c.start()
         else:
-            for c in copies(part, j, k - 1):
-                c.wait_recv()
-        if k < 4:
-            for c in copies(part, j, k):
-                c.start()
+            if kind == 1:
+                @pl.when(jnp.logical_not(inner))
+                def _():
+                    for c in zcopies(part, order(z, j), 0):
+                        c.wait_recv()
+            else:
+                for c in copies(part, j, kind - 1):
+                    c.wait_recv()
+            if kind in kinds(part):
+                for c in copies(part, j, kind):
+                    c.start()
+
+    def beat(step):
+        for at, events in EVENTS.items():
+            if isinstance(at, int):
+                @pl.when(step == at)
+                def _(events=events):
+                    for e in events:
+                        do(*e)
+
+    def before(j):
+        for e in EVENTS.get(("before", j), ()):
+            do(*e)
+
+    place = lax.broadcasted_iota(jnp.int32, (1, ROW), 1)
+    row = lax.broadcasted_iota(jnp.int32, (128 - HD, ROW), 0)
+    segment = jnp.zeros((1, ROW), jnp.int32)
+    finish = jnp.int32(0)
+    for i in range(SEGS):
+        finish = finish + lengths[0, i]
+        segment = segment + jnp.where(place >= finish, 1, 0)
+    same = row == segment
+    qaug[...] = jnp.where(same | (row >= SEGS), 0.0, NEG).astype(bf16)
+    kaug[...] = jnp.where(same | ((row >= SEGS) & (row < SEGS + 3)), 1.0, 0.0).astype(bf16)
 
     def norm(c, _):
         r = chunk(c)
         xx = x[r].astype(f32)
         f = lax.rsqrt(jnp.mean(xx * xx, axis=1, keepdims=True) + eps)
-        h = (xx * f * gain[...].astype(f32)).astype(bf16)
-        hid[r] = h
-        turned(c, h, hid1t_o)
+        hid[r] = (xx * f * gains[0:1, :].astype(f32)).astype(bf16)
         return 0
 
-    def turn_copy(c, dst):
-        return pltpu.make_async_copy(ctb.at[lax.rem(c, 2)], dst.at[:, chunk(c)], tsem.at[0, lax.rem(c, 2)])
-
-    def turned(c, v, dst):
-        pl.when(c >= 2)(lambda: turn_copy(c - 2, dst).wait())
-        ctb[lax.rem(c, 2)] = v.T
-        turn_copy(c, dst).start()
-
-    def turn_end(dst):
-        for c in (ROW // CH - 2, ROW // CH - 1):
-            turn_copy(c, dst).wait()
+    def turn_copy(i):
+        s = lax.rem(i, 2)
+        n = ROW // CH
+        cols = chunk(lax.rem(i, n))
+        return (pltpu.make_async_copy(ctb.at[s], hid1t_o.at[:, cols], tsem.at[0, s]),
+                pltpu.make_async_copy(ctb.at[s], cott_o.at[:, cols], tsem.at[0, s]))
 
     def cot_load(c):
-        return pltpu.make_async_copy(cot.at[chunk(c)], cb.at[lax.rem(c, 2)], tsem.at[1, lax.rem(c, 2)])
+        s = lax.rem(c, 2)
+        return pltpu.make_async_copy(cot.at[chunk(c)], cb.at[s], tsem.at[1, s])
+
+    def turn_hid(c, _):
+        pl.when(c >= 2)(lambda: turn_copy(c - 2)[0].wait())
+        ctb[lax.rem(c, 2)] = hid[chunk(c)].T
+        turn_copy(c)[0].start()
+        return 0
 
     def turn_cot(c, _):
-        pl.when(c + 1 < ROW // CH)(lambda: cot_load(c + 1).start())
         cot_load(c).wait()
-        turned(c, cb[lax.rem(c, 2)], cott_o)
+        turn_copy(c + 2)[0].wait()
+        ctb[lax.rem(c, 2)] = cb[lax.rem(c, 2)].T
+        turn_copy(c)[1].start()
+        pl.when(c + 2 < ROW // CH)(lambda: cot_load(c + 2).start())
         return 0
 
     cot_load(0).start()
+    cot_load(1).start()
     lax.fori_loop(0, ROW // CH, norm, 0)
-    turn_end(hid1t_o)
-
-    def projections(s):
+
+    def results(j):
+        s = order(z, j)
+        h = pl.ds(s * HQ_OWN, HQ_OWN)
+        g = pl.ds(s * KV_OWN, KV_OWN)
+        r = pl.ds(0, QKV)
+        pairs = [(w.at[s, r], w_o.at[s, r]), (qt.at[h], qt_o.at[h]), (kt.at[g], kt_o.at[g]),
+                 (kk.at[g], kk_o.at[g]), (vv.at[g], vv_o.at[g])]
+        return [pltpu.make_async_copy(a, b, osem.at[j, i]) for i, (a, b) in enumerate(pairs)]
+
+    def quarter(j, _):
+        s = order(z, j)
+        for i in range(1, NZ):
+            @pl.when(j == i)
+            def _(i=i):
+                if i == 1:
+                    lax.fori_loop(0, ROW // CH, turn_hid, 0)
+                    lax.fori_loop(0, ROW // CH, turn_cot, 0)
+                before(i)
+
         def one(c, _):
             project(w, hid, qt, kt, kk, vt, vv, cos, sin, qaug, kaug, s, c)
+            beat(8 * j + c)
             return 0
 
         lax.fori_loop(0, ROW // CH, one, 0)
 
-    def attends(s):
-        def one(g, _):
-            attend(qt, kk, vt, ho, qaug, KV_OWN * s + g)
+        def two(g, _):
+            attend(qt, kk, vt, ho, qaug, KV_OWN * s + g, lambda half: beat(8 * j + 4 + 2 * g + half))
             return 0
 
-        lax.fori_loop(0, KV_OWN, one, 0)
-
-    events = {
-        "0a": ((0, 1, 1),),
-        "0b": ((0, 1, 2), (0, 2, 1), (0, 1, 3), (0, 2, 2), (0, 3, 1), (0, 1, 4)),
-        "1a": ((0, 2, 3), (0, 3, 2), (1, 1, 1)),
-        "1b": ((0, 2, 4), (0, 3, 3), (1, 1, 2), (1, 2, 1)),
-        "2a": ((0, 3, 4), (1, 1, 3), (1, 2, 2), (1, 3, 1)),
-        "2b": ((1, 1, 4), (1, 2, 3), (1, 3, 2)),
-        "3a": ((1, 2, 4), (1, 3, 3)),
-        "3b": ((1, 3, 4),),
-    }
-    for j in range(NZ):
-        s = order(z, j)
-        if j == 1:
-            lax.fori_loop(0, ROW // CH, turn_cot, 0)
-            turn_end(cott_o)
-        projections(s)
-        for e in events[f"{j}a"]:
-            stage(*e)
-        attends(s)
-        for e in events[f"{j}b"]:
-            stage(*e)
-    outs = [(w, w_o), (qt, qt_o), (kt, kt_o), (kk, kk_o), (vv, vv_o), (ho, ho_o)]
-    writes = [pltpu.make_async_copy(a, b, osem.at[i]) for i, (a, b) in enumerate(outs)]
-    for c in writes:
+        lax.fori_loop(0, KV_OWN, two, 0)
+        for c in results(j):
+            c.start()
+        return 0
+
+    lax.fori_loop(0, NZ, quarter, 0)
+    before(NZ)
+    last = [pltpu.make_async_copy(ho, ho_o, osem.at[NZ, 0])]
+    last += [pltpu.make_async_copy(w.at[s, pl.ds(QKV, QR)], w_o.at[s, pl.ds(QKV, QR)], osem.at[NZ, 1 + s])
+             for s in range(NZ)]
+    for c in last:
         c.start()
 
     def mid_copies(c, slot):
@@ -310,7 +407,7 @@
             acc = acc + tn(ho[QR * s:QR * s + QR, r], w[s, QKV:WR])
         midb[slot] = acc
         f = lax.rsqrt(jnp.mean(acc * acc, axis=1, keepdims=True) + eps)
-        h = (acc * f * gain2[...].astype(f32)).astype(bf16)
+        h = (acc * f * gains[1:2, :].astype(f32)).astype(bf16)
         hidb[slot] = h
         hidtb[slot] = h.T
         for m in mid_copies(c, slot):
@@ -322,18 +419,27 @@
     for c in range(max(n - 2, 0), n):
         for m in mid_copies(c, c % 2):
             m.wait()
-    for c in writes:
+        turn_copy(c)[1].wait()
+    for j in range(NZ):
+        for c in results(j):
+            c.wait()
+    for c in last:
         c.wait()
     for part in range(2):
-        for d in (1, 2, 3):
-            zcopy(part, d, z).wait_send()
+        def sent(s, side, part=part):
+            for c in zcopies(part, s, side):
+                c.wait_send()
+
+        for side in (0, 1):
+            pl.when((z < NZ - 1) if side else (z > 0))(functools.partial(sent, z, side))
         for j in (1, 2, 3):
-            for kind in (1, 2, 3):
+            pl.when(inner)(functools.partial(lambda j: sent(*pass_on(part, j)), j))
+            for kind in kinds(part):
                 for c in copies(part, j, kind):
                     c.wait_send()
 
 
-def forward(x, gain, gain2, cos, sin, qaug, kaug, own, cot):
+def forward(lengths, x, gains, cos, sin, qw, kw, vw, ow, cot):
     heads = NZ * HQ_OWN
     kv = NZ * KV_OWN
     vm = pltpu.VMEM
@@ -343,35 +449,33 @@
                    sds((heads, 128, ROW), bf16), sds((kv, 128, ROW), bf16), sds((kv, ROW, 128), bf16),
                    sds((kv, ROW, 128), bf16), sds((NZ, WR, D), bf16), sds((D, ROW), bf16), sds((D, ROW), bf16),
                    sds((D, ROW), bf16)),
-        in_specs=[VM] * 7 + [ANY] * 2,
+        in_specs=[pl.BlockSpec(memory_space=pltpu.SMEM)] + [VM] * 3 + [ANY] * 6,
         out_specs=(ANY,) * 11,
         scratch_shapes=[
-            vm((NZ, WR, D), bf16), vm((ROW, D), bf16), vm((heads * HD, ROW), bf16),
+            vm((ROW, D), bf16), vm((D, QR), bf16), vm((NZ, WR, D), bf16), vm((ROW, D), bf16), vm((heads * HD, ROW), bf16),
             vm((heads, 128, ROW), bf16), vm((kv, 128, ROW), bf16), vm((kv, ROW, 128), bf16),
-            vm((kv, 128, ROW), bf16), vm((kv, ROW, 128), bf16), vm((2, CH, D), f32), vm((2, CH, D), bf16),
+            vm((kv, 128, ROW), bf16), vm((kv, ROW, 128), bf16),
+            vm((128 - HD, ROW), bf16), vm((128 - HD, ROW), bf16), vm((2, CH, D), f32), vm((2, CH, D), bf16),
             vm((2, D, CH), bf16), vm((2, CH, D), bf16), vm((2, D, CH), bf16),
-            DMA((2, 3)), DMA((2, NZ)), DMA((2, 3, 3)), DMA((2, 3, 3)), DMA((2, 3, 3)), DMA((2, 3, 3)),
-            DMA((2, 3, 4)), DMA((2, 3, 4)), DMA((6,)), DMA((1,)), DMA((3, 2)), DMA((2, 2))],
+            DMA((3, NZ, 2)), DMA((3, NZ)), DMA((2, 3, 3)), DMA((2, 3, 3)), DMA((2, 3, 3)), DMA((2, 3, 3)),
+            DMA((2, 3, 4)), DMA((2, 3, 4)), DMA((NZ + 1, 5)), DMA((5,)), DMA((3, 2)), DMA((2, 2))],
         compiler_params=pltpu.CompilerParams(
             collective_id=1, has_side_effects=True, vmem_limit_bytes=60 * 2**20),
         name="attention_forward",
-    )(x, gain, gain2, cos, sin, qaug, kaug, own, cot)
-
-
-def tables(lengths):
-    finish = jnp.cumsum(lengths)
-    starts = finish - lengths
+    )(lengths, gains, cos, sin, x, qw, kw, vw, ow, cot)
+
+
+def angles_of(lengths):
     place = jnp.arange(ROW, dtype=jnp.int32)
-    segment = jnp.sum((place[None, :] >= finish[:, None]).astype(jnp.int32), axis=0)
-    chosen = segment[None, :] == jnp.arange(SEGS, dtype=jnp.int32)[:, None]
-    offsets = jnp.sum(jnp.where(chosen, starts[:, None], 0), axis=0)
-    positions = (place - offsets).astype(f32)
+    start = jnp.zeros((ROW,), jnp.int32)
+    finish = jnp.int32(0)
+    for i in range(SEGS - 1):
+        finish = finish + lengths[i]
+        start = jnp.where(place >= finish, finish, start)
+    positions = (place - start).astype(f32)
     freqs = rope_base ** (-(jnp.arange(HD // 2, dtype=f32) * 2.0) / HD)
     angles = freqs[:, None] * positions[None, :]
-    rest = 128 - HD - SEGS
-    qaug = jnp.concatenate([jnp.where(chosen, 0.0, NEG), jnp.zeros((rest, ROW))], axis=0).astype(bf16)
-    kaug = jnp.concatenate([chosen.astype(f32), jnp.ones((3, ROW)), jnp.zeros((rest - 3, ROW))], axis=0).astype(bf16)
-    return jnp.cos(angles), jnp.sin(angles), qaug, kaug
+    return jnp.cos(angles), jnp.sin(angles)
 
 
 class RowSum:
@@ -467,11 +571,11 @@
 
 
 class GradSum:
-    def __init__(self, dp, low, width, cut, g, c1, x1, y1, x2, y2, ssem, rsem, out, wide=False):
+    def __init__(self, dp, low, width, cut, g, c1, x1, y1, x2, y2, ssem, rsem, emit, wide=False):
         self.pc, self.px, self.py = (partner(low, dp, bit) for bit in (1, 2, 4))
         self.c, self.x, self.y = lax.rem(low, 2), lax.rem(low // 2, 2), low // 4
         self.g, self.c1, self.x1, self.y1, self.x2, self.y2 = g, c1, x1, y1, x2, y2
-        self.ssem, self.rsem, self.out = ssem, rsem, out
+        self.ssem, self.rsem, self.emit = ssem, rsem, emit
         self.width, self.cut, self.wide = width, cut, wide
 
     def cols(self, u, lo, hi):
@@ -531,10 +635,8 @@
                 add(i, x, 0, cut, self.x1[u, i])
                 add(y, i, cut, width, self.y1[u, i])
         else:
-            self.out[:, pl.ds(pl.multiple_of(u * width, 128), cut)] = (
-                g[at(y, x, 0, cut)].astype(f32) + self.y2[u].astype(f32))
-            self.out[:, pl.ds(pl.multiple_of(u * width + cut, 128), width - cut)] = (
-                g[at(y, x, cut, width)].astype(f32) + self.x2[u].astype(f32))
+            self.emit(u, 0, cut, g[at(y, x, 0, cut)].astype(f32) + self.y2[u].astype(f32))
+            self.emit(u, cut, width, g[at(y, x, cut, width)].astype(f32) + self.x2[u].astype(f32))
         if k < 3:
             for cp in self.copies(u, k):
                 cp.start()
@@ -563,8 +665,8 @@
 MLP_WIDTH = 512
 
 
-def feed_kernel(gain2, hid2, cot, mid, hid2t_i, cott_i, gw_i, uw_i, dw_i,
-                mlp_o, gm_o, gml_o, gmlt_o, gain2_o, grad_o,
+def feed_kernel(gains, hid2, cot, mid, hid2t_i, cott_i, gw_i, uw_i, dw_i,
+                mlp_o, gm_o, gml_o, gmlt_o, gain2_o, gate_o, up_o, down_o,
                 gw, uw, dw, a3, side, own, hb, cb, tb, mb, cb2, gmb, gmlb, gmltb,
                 rend, rmid, out, zs, ze, zm, zo,
                 g, c1, x1, y1, x2, y2, gs, gr,
@@ -586,8 +688,16 @@
     for c in loads[:4]:
         c.start()
     greet(dp, z, low)
+    def emit(u, lo, hi, v):
+        half = lax.rem(u, 2) * MLP_WIDTH
+        at = pl.ds(pl.multiple_of(half + lo, 128), hi - lo)
+        for i, ref in enumerate((gate_o, up_o, down_o)):
+            @pl.when(u // 2 == i)
+            def _(ref=ref):
+                ref[:, at] = v
+
     zsum = RowSum(z, lambda i: own.at[chunk(i, BL)], rend, rmid, out, zs, ze, zm, zo, RING, LAG)
-    gsum = GradSum(dp, low, MLP_WIDTH, MLP_WIDTH // 2, g, c1, x1, y1, x2, y2, gs, gr, grad_o)
+    gsum = GradSum(dp, low, MLP_WIDTH, MLP_WIDTH // 2, g, c1, x1, y1, x2, y2, gs, gr, emit)
     gain2_o[...] = jnp.zeros_like(gain2_o)
 
     def gm_loads(j):
@@ -618,7 +728,7 @@
         n = m * f
         gn = gh * n
         gain2_o[...] += jnp.sum(gn, axis=0, keepdims=True)
-        ga = gain2[...].astype(f32)
+        ga = gains[1:2, :].astype(f32)
         gm = cb2[...].astype(f32) + f * (gh * ga - n * jnp.mean(gn * ga, axis=1, keepdims=True))
         gmb[s] = gm
         low_gm = gm.astype(bf16)
@@ -726,15 +836,15 @@
             c.wait()
 
 
-def feed(gain2, hid2, cot, mid, hid2t, cott, gw, uw, dw):
+def feed(gains, hid2, cot, mid, hid2t, cott, gw, uw, dw):
     vm = pltpu.VMEM
     ff = gw.shape[1]
     return pl.pallas_call(
         feed_kernel,
         out_shape=(sds((ROW, D), bf16), sds((ROW, D), f32), sds((ROW, D), bf16), sds((D, ROW), bf16),
-                   sds((1, D), f32), sds((D // 8, 3 * ff), f32)),
+                   sds((1, D), f32), sds((D // 8, ff), f32), sds((D // 8, ff), f32), sds((D // 8, ff), f32)),
         in_specs=[VM] + [ANY] * 8,
-        out_specs=(ANY, ANY, ANY, ANY, VM, VM),
+        out_specs=(ANY, ANY, ANY, ANY, VM, VM, VM, VM),
         scratch_shapes=[
             vm((D, ff), bf16), vm((D, ff), bf16), vm((ff, D), bf16), vm((3, ROW, ff), bf16),
             vm((D, ROW), bf16), vm((ROW, D), bf16),
@@ -746,14 +856,14 @@
         compiler_params=pltpu.CompilerParams(
             collective_id=2, has_side_effects=True, vmem_limit_bytes=63 * 2**20),
         name="feed_forward",
-    )(gain2, hid2, cot, mid, hid2t, cott, gw, uw, dw)
-
-
-BL3 = 32
+    )(gains, hid2, cot, mid, hid2t, cott, gw, uw, dw)
+
+
+BL3 = 64
 RING3 = 10
 LAG3 = 2
-ATT_UNITS = 5
-ATT_WIDTH = 256
+WIDTH = QR
+CUT = 128
 
 
 def unrotate(u, co, si):
@@ -802,16 +912,16 @@
         gt[at, lo:hi] = unrotate(dq[0:HD, h * CH:(h + 1) * CH] * SCALE, cos[:, lo:hi], sin[:, lo:hi])
 
 
-def backward_kernel(groups, gain, cos, sin, gain2_i, x, mid, mlp, gm, gml_i, gmlt, hid1t, ho_i, qt_i, kt_i, kk_i, vv_i, w_i,
-                    out_o, xg_o, grad_o,
+def backward_kernel(groups, gains, cos, sin, gain2_i, x, mid, mlp, gm, gml_i, gmlt, hid1t, ho_i, qt_i, kt_i, kk_i, vv_i, w_i,
+                    out_o, xg_o, qg_o, kg_o, vg_o, og_o, gains_o,
                     w, wo, ho, qk, kk, vv, dk, dv, gt, gml, dot, ga1, own, mb2, ob2, xb, gb, ob,
                     rend, rmid, out, zs, ze, zm, zo,
-                    c1, x1, y1, x2, y2, gs, gr,
-                    lsem, bsem, wsem, psem, osem, isem):
+                    c1, x1, y1, x2, y2, gs, gr, og, oc1, ox1, oy1, ox2, oy2, ogs, ogr, tb, gsend, grecv,
+                    lsem, bsem, wsem, psem, osem, isem, tsem, ssem, rsem):
     dp, z, low = places()
     qrows = NZ * HQ_OWN * 128
-    loads = [pltpu.make_async_copy(gml_i, gml, lsem.at[0]),
-             pltpu.make_async_copy(ho_i, ho, lsem.at[1]),
+    loads = [pltpu.make_async_copy(ho_i, ho, lsem.at[1]),
+             pltpu.make_async_copy(gml_i, gml, lsem.at[0]),
              pltpu.make_async_copy(kk_i, kk, lsem.at[2]),
              pltpu.make_async_copy(vv_i, vv, lsem.at[3])]
     loads += [pltpu.make_async_copy(w_i.at[s, pl.ds(QKV + 192 * h, 192)], wo.at[s // 2, s % 2, h], lsem.at[4 + 2 * s + h])
@@ -819,8 +929,7 @@
     loads += [pltpu.make_async_copy(qt_i, qk.at[pl.ds(0, qrows)], lsem.at[12]),
               pltpu.make_async_copy(kt_i, qk.at[pl.ds(qrows, NZ * KV_OWN * 128)], lsem.at[13])]
     wloads = [pltpu.make_async_copy(w_i.at[s, pl.ds(0, QKV)], w.at[s], lsem.at[14 + s]) for s in range(NZ)]
-    late = [pltpu.make_async_copy(hid1t, qk.at[pl.ds(0, D)], lsem.at[18]),
-            pltpu.make_async_copy(gmlt, qk.at[pl.ds(D, D)], lsem.at[19])]
+    late = [pltpu.make_async_copy(hid1t, qk.at[pl.ds(0, D)], lsem.at[18])]
     nb = ROW // BL3
     nt_blocks = ROW // TB
 
@@ -836,14 +945,33 @@
         s = lax.rem(i, 2)
         return pltpu.make_async_copy(ob2.at[s], out_o.at[chunk(i, BL3)], osem.at[1, s])
 
+    def turned_load(k):
+        return pltpu.make_async_copy(gmlt.at[pl.ds(k * 192, 192)], tb.at[k % 2], tsem.at[k % 2])
+
     own_load(0).start()
     own_load(1).start()
     mid_load(0).start()
+    turned_load(0).start()
+    turned_load(1).start()
     for c in loads:
         c.start()
-    greet(dp, z, low)
+    greet(dp, z, low, range(1, 8))
     zsum = RowSum(z, lambda i: own.at[lax.rem(i, RING3)], rend, rmid, out, zs, ze, zm, zo, RING3, LAG3)
-    gsum = GradSum(dp, low, ATT_WIDTH, ATT_WIDTH // 2, wo, c1, x1, y1, x2, y2, gs, gr, grad_o, True)
+
+    def emit(u, lo, hi, v):
+        if u == 0:
+            qg_o[:, lo:hi] = v
+            return
+        for ref, first in ((kg_o, 0), (vg_o, KR)):
+            a, b = max(lo, first), min(hi, first + KR)
+            if a < b:
+                ref[:, a - first:b - first] = v[:, a - lo:b - lo]
+
+    def emit_o(u, lo, hi, v):
+        og_o[:, lo:hi] = v
+
+    gsum = GradSum(dp, low, WIDTH, CUT, wo, c1, x1, y1, x2, y2, gs, gr, emit, True)
+    osum = GradSum(dp, low, WIDTH, CUT, og, oc1, ox1, oy1, ox2, oy2, ogs, ogr, emit_o)
 
     def finish(i):
         mid_load(i).wait()
@@ -860,64 +988,70 @@
         def _():
             mid_load(i + 1).start()
 
-    def tick(t):
-        pl.when(t < nb)(lambda: own_load(t).wait())
-        zsum.tick(t, nb, finish)
-        pl.when(t + 2 < nb)(lambda: own_load(t + 2).start())
+    per = 64 // BL3
+
+    def tick(beat):
+        for k in range(per):
+            t = beat * per + k
+            pl.when(t < nb)(functools.partial(lambda t: own_load(t).wait(), t))
+            zsum.tick(t, nb, finish)
+            pl.when(t + 2 < nb)(functools.partial(lambda t: own_load(t + 2).start(), t))
+
+    tick(0)
+    loads[0].wait()
+    o_rows = ho[pl.ds(pl.multiple_of(z * QR, 128), QR), :]
+    for k in range(8):
+        turned_load(k).wait()
+        osum.put_block(0, k, nt(tb[k % 2], o_rows))
+        if k + 2 < 8:
+            turned_load(k + 2).start()
+    osum.start(0)
+    tick(1)
+    for c in loads[1:]:
+        c.wait()
+    for c in wloads:
+        c.start()
+
+    def extra(g):
+        return (5 * g + 4) // 8
 
     def quarter(s, _):
-        @pl.when(s == 0)
-        def _():
-            for c in loads:
-                c.wait()
-            for c in wloads:
-                c.start()
-
         for h in range(2):
             t = nt(wo[s // 2, lax.rem(s, 2), h], gml[...])
             dot[h * 192:(h + 1) * 192, :] = t.astype(bf16)
-        tick(s * (1 + KV_OWN * 4))
 
         def one(gg, _):
             g = KV_OWN * s + gg
             for qb in range(ROW // CH):
                 attend_back(qk, kk, vv, dot, ho, dk, dv, gt, cos, sin, g, gg, qb)
-                tick(s * (1 + KV_OWN * 4) + 1 + gg * 4 + qb)
+                if qb == 2:
+                    pl.when(extra(g + 1) > extra(g))(lambda: tick(2 + g + extra(g)))
+                if qb == 3:
+                    tick(2 + g + extra(g + 1))
             first = pl.multiple_of(s * QKV + QR + gg * HD, 32)
             gt[pl.ds(first, HD), :] = unrotate(dk[...].T[0:HD] * SCALE, cos[...], sin[...])
             gt[pl.ds(pl.multiple_of(first + KR, 32), HD), :] = dv[...].T[0:HD].astype(bf16)
             return 0
 
         lax.fori_loop(0, KV_OWN, one, 0)
+        for k in (1, 2, 3):
+            pl.when(s == k - 1)(functools.partial(osum.stage, k, 0))
         return 0
 
     lax.fori_loop(0, NZ, quarter, 0)
-    beats = NZ * (1 + KV_OWN * 4)
+    beats = 2 + 13
     for c in late:
         c.start()
     for c in wloads + late:
         c.wait()
 
-    def qkv_unit(u, _):
-        rhs = gt[pl.ds(pl.multiple_of(z * QKV + u * ATT_WIDTH, 128), ATT_WIDTH), :]
+    for u in range(2):
+        rhs = gt[pl.ds(pl.multiple_of(z * QKV + u * WIDTH, 128), WIDTH), :]
         for k in range(8):
             gsum.put_block(u, k, nt(qk[k * 192:(k + 1) * 192, :], rhs))
         gsum.start(u)
         tick(beats + u)
-
-        pl.when(u >= 1)(lambda: gsum.stage(1, u - 1))
-        return 0
-
-    lax.fori_loop(0, QKV // ATT_WIDTH, qkv_unit, 0)
-    beats += QKV // ATT_WIDTH
-    o_at = pl.multiple_of(z * QR, 128)
-    for k in range(8):
-        gsum.put_block(3, k, nt(qk[D + k * 192:D + (k + 1) * 192, :], ho[pl.ds(o_at, ATT_WIDTH), :]))
-    gsum.start(3)
-    for k in range(8):
-        r = nt(qk[D + k * 192:D + (k + 1) * 192, :], ho[pl.ds(o_at + ATT_WIDTH, QR - ATT_WIDTH), :])
-        gsum.put_part(4, k, 0, QR - ATT_WIDTH, r)
-    gsum.stage(1, 2)
+    beats += 2
 
     def tail_loads(b, slot):
         r = chunk(b, TB)
@@ -955,53 +1089,66 @@
         n = xx * f
         gn = acc * n
         ga1[...] += jnp.sum(gn, axis=0, keepdims=True)
-        ga = gain[...].astype(f32)
+        ga = gains[0:1, :].astype(f32)
         res = gb[slot] + f * (acc * ga - n * jnp.mean(gn * ga, axis=1, keepdims=True))
         ob[slot] = res.astype(bf16)
         out_copy(b, slot).start()
-        tick(beats + b)
-        pl.when(b == 0)(lambda: gsum.stage(1, 3))
-        pl.when((b >= 1) & (b < 5))(lambda: gsum.stage(2, b - 1))
-        pl.when(b >= 4)(lambda: gsum.stage(3, b - 4))
+        pl.when(lax.rem(b, 2) == 1)(lambda: tick(beats + b // 2))
+        pl.when(b == 0)(lambda: (gsum.stage(1, 0), gsum.stage(1, 1)) and None)
+        pl.when(b == 2)(lambda: gsum.stage(2, 0))
+        pl.when(b == 4)(lambda: gsum.stage(2, 1))
+        pl.when(b == 6)(lambda: gsum.stage(3, 0))
         return 0
 
     lax.fori_loop(0, nt_blocks, tail, 0)
-    beats += nt_blocks
-    row = lax.broadcasted_iota(jnp.int32, (128, D), 0)
-    both = by_block(jnp.where(row == 0, ga1[...], jnp.where(row == 1, gain2_i[...], 0.0)).T, groups)
+    beats += nt_blocks // 2
+
+    def gains_copy(mask):
+        to = flip(low, mask)
+        return put(gsend.at[to], grecv.at[low], ssem.at[mask], rsem.at[mask], {"dp": dp - low + to})
+
+    share = D // 8 // groups
     for k in range(8):
-        gsum.put_part(4, k, QR - ATT_WIDTH, ATT_WIDTH, both[k * 192:(k + 1) * 192])
-    gsum.start(4)
+        for i, v in enumerate((ga1, gain2_i)):
+            gsend[k, i:i + 1, 0:D // 8] = jnp.concatenate(
+                [v[:, (g * 8 + k) * share:(g * 8 + k + 1) * share] for g in range(groups)], axis=1)
+    for mask in range(1, 8):
+        gains_copy(mask).start()
 
     def rest(t, _):
         tick(t)
         return 0
 
-    if beats < nb + 4 * LAG3:
-        lax.fori_loop(beats, nb + 4 * LAG3, rest, 0)
-    for k in (1, 2, 3):
-        gsum.stage(k, 4)
-
-    def drains(u, _):
+    ends = (nb + 4 * LAG3 + per - 1) // per
+    if beats < ends:
+        lax.fori_loop(beats, ends, rest, 0)
+    gsum.stage(3, 1)
+    total = gsend[low]
+    for mask in range(1, 8):
+        gains_copy(mask).wait_recv()
+        total = total + grecv[flip(low, mask)]
+    gains_o[...] = total
+    for mask in range(1, 8):
+        gains_copy(mask).wait_send()
+    for u in range(2):
         gsum.drain(u)
-        return 0
-
-    lax.fori_loop(0, ATT_UNITS, drains, 0)
+    osum.drain(0)
     for b in range(nt_blocks - 2, nt_blocks):
         out_copy(b, b % 2).wait()
     for i in (nb - 2, nb - 1):
         out_write(i).wait()
 
 
-def backward(groups, gain, cos, sin, gain2_sum, x, mid, mlp, gm, gml, gmlt, hid1t, ho, qt, kt, kk, vv, w):
+def backward(groups, gains, cos, sin, gain2_sum, x, mid, mlp, gm, gml, gmlt, hid1t, ho, qt, kt, kk, vv, w):
     vm = pltpu.VMEM
     heads = NZ * HQ_OWN
     kv = NZ * KV_OWN
     return pl.pallas_call(
         functools.partial(backward_kernel, groups),
-        out_shape=(sds((ROW, D), bf16), sds((ROW, D), bf16), sds((D // 8, ATT_UNITS * ATT_WIDTH), f32)),
+        out_shape=(sds((ROW, D), bf16), sds((ROW, D), bf16), sds((D // 8, QR), f32), sds((D // 8, KR), f32),
+                   sds((D // 8, KR), f32), sds((D // 8, QR), f32), sds((8, 256), f32)),
         in_specs=[VM] * 4 + [ANY] * 13,
-        out_specs=(ANY, ANY, VM),
+        out_specs=(ANY, ANY) + (VM,) * 5,
         scratch_shapes=[
             vm((NZ, QKV, D), bf16), vm((2, 2, 2, 192, D), bf16), vm((heads * HD, ROW), bf16),
             vm(((heads + kv) * 128, ROW), bf16), vm((kv, ROW, 128), bf16), vm((kv, ROW, 128), bf16),
@@ -1009,12 +1156,13 @@
             vm((ROW, D), bf16), vm((QR, ROW), bf16), vm((1, D), f32),
             vm((RING3, BL3, D), bf16), vm((2, BL3, D), f32), vm((2, BL3, D), bf16),
             vm((2, TB, D), bf16), vm((2, TB, D), f32), vm((2, TB, D), bf16)]
-        + ring_scratch(RING3, BL3) + sum_scratch(ATT_UNITS, ATT_WIDTH, ATT_WIDTH // 2)[1:]
-        + [DMA((20,)), DMA((2, 2)), DMA((2,)), DMA((2,)), DMA((2, 2)), DMA((RING3,))],
+        + ring_scratch(RING3, BL3) + sum_scratch(2, WIDTH, CUT)[1:] + sum_scratch(1, WIDTH, CUT)
+        + [vm((2, 192, ROW), bf16), vm((8, 8, 256), f32), vm((8, 8, 256), f32),
+           DMA((19,)), DMA((2, 2)), DMA((2,)), DMA((2,)), DMA((2, 2)), DMA((RING3,)), DMA((2,)), DMA((8,)), DMA((8,))],
         compiler_params=pltpu.CompilerParams(
             collective_id=3, has_side_effects=True, vmem_limit_bytes=63 * 2**20),
         name="attention_backward",
-    )(gain, cos, sin, gain2_sum, x, mid, mlp, gm, gml, gmlt, hid1t, ho, qt, kt, kk, vv, w)
+    )(gains, cos, sin, gain2_sum, x, mid, mlp, gm, gml, gmlt, hid1t, ho, qt, kt, kk, vv, w)
 
 
 def by_block(v, groups):
@@ -1028,28 +1176,56 @@
          attn_gain, mlp_gain, cotangent):
     x = inputs.reshape(ROW, D)
     cot = cotangent.reshape(ROW, D)
-    gain = attn_gain.reshape(1, D)
-    gain2 = mlp_gain.reshape(1, D)
-    ff = gate_weight.shape[1]
-    cos, sin, qaug, kaug = tables(lengths[0])
-    own = jnp.concatenate([q_weight.T, k_weight.T, v_weight.T, o_weight], axis=0)
-    mid, hid2, ho, qt, kt, kk, vv, w, hid1t, hid2t, cott = forward(x, gain, gain2, cos, sin, qaug, kaug, own, cot)
-    mlp, gm, gml, gmlt, gain2_sum, mlp_grad = feed(
-        gain2, hid2, cot, mid, by_block(hid2t, groups), by_block(cott, groups), gate_weight, up_weight, down_weight)
-    output, input_grad, att_grad = backward(
-        groups, gain, cos, sin, gain2_sum, x, mid, mlp, gm, gml, by_block(gmlt, groups), by_block(hid1t, groups),
+    first = lax.broadcasted_iota(jnp.int32, (2, D), 0) == 0
+    gains = jnp.where(first, attn_gain[None, :], mlp_gain[None, :])
+    cos, sin = angles_of(lengths[0])
+    mid, hid2, ho, qt, kt, kk, vv, w, hid1t, hid2t, cott = forward(
+        lengths, x, gains, cos, sin, q_weight, k_weight.T, v_weight.T, o_weight, cot)
+    mlp, gm, gml, gmlt, gain2_sum, gate_g, up_g, down_g = feed(
+        gains, hid2, cot, mid, by_block(hid2t, groups), by_block(cott, groups), gate_weight, up_weight, down_weight)
+    output, input_grad, q_g, k_g, v_g, o_g, gain_sums = backward(
+        groups, gains, cos, sin, gain2_sum, x, mid, mlp, gm, gml, by_block(gmlt, groups), by_block(hid1t, groups),
         ho, qt.reshape(-1, ROW), kt.reshape(-1, ROW), kk, vv, w)
+    grads = [q_g, k_g, v_g, o_g, gate_g, up_g, down_g, gain_sums]
     if groups > 1:
-        n = 8 * groups
         same = [[g * 8 + low for g in range(groups)] for low in range(8)]
-
-        def over(v):
-            return lax.psum_scatter(v, "dp", scatter_dimension=0, axis_index_groups=same, tiled=True)
-
-        mlp_grad, att_grad = over(mlp_grad), over(att_grad)
-    return (output.reshape(1, ROW, D), input_grad.reshape(1, ROW, D), att_grad[:, 0:QR], att_grad[:, QR:QR + KR],
-            att_grad[:, QR + KR:QKV], att_grad[:, QKV:WR].T, mlp_grad[:, 0:ff], mlp_grad[:, ff:2 * ff],
-            mlp_grad[:, 2 * ff:].T, att_grad[:, WR], att_grad[:, WR + 1])
+        grads = [lax.psum_scatter(v, "dp", scatter_dimension=int(i == 7), axis_index_groups=same, tiled=True)
+                 for i, v in enumerate(grads[:7] + [gain_sums[:, 0:D // 8]])]
+    output, input_grad, *grads = hand_over(output, input_grad, *grads)
+    grads[3], grads[6] = grads[3].T, grads[6].T
+    grads[7:] = grads[7][0, 0:D // 8 // groups], grads[7][1, 0:D // 8 // groups]
+    return (output.reshape(1, ROW, D), input_grad.reshape(1, ROW, D), *grads)
+
+
+def hand_over_kernel(n, *refs):
+    held, load, store = refs[2 * n:3 * n], refs[3 * n], refs[3 * n + 1]
+    pieces = []
+    for i in range(n):
+        rows = held[i].shape[0]
+        parts = 4 if rows % 64 == 0 and rows > 512 else 1
+        pieces += [(i, pl.ds(p * (rows // parts), rows // parts)) for p in range(parts)]
+    first = [pltpu.make_async_copy(refs[i].at[r], held[i].at[r], load.at[k]) for k, (i, r) in enumerate(pieces)]
+    then = [pltpu.make_async_copy(held[i].at[r], refs[n + i].at[r], store.at[k]) for k, (i, r) in enumerate(pieces)]
+    for c in first:
+        c.start()
+    for a, b in zip(first, then):
+        a.wait()
+        b.start()
+    for c in then:
+        c.wait()
+
+
+def hand_over(*arrays):
+    n = len(arrays)
+    return pl.pallas_call(
+        functools.partial(hand_over_kernel, n),
+        out_shape=tuple(sds(v.shape, v.dtype) for v in arrays),
+        in_specs=[ANY] * n,
+        out_specs=(ANY,) * n,
+        scratch_shapes=[pltpu.VMEM(v.shape, v.dtype) for v in arrays] + [DMA((4 * n,)), DMA((4 * n,))],
+        compiler_params=pltpu.CompilerParams(vmem_limit_bytes=63 * 2**20),
+        name="hand_over",
+    )(*arrays)
 
 
 def solution(mesh):

time: 359 us -> 300 us (0.84)
  Pallas kernels: 333 us -> 291 us
  local copies, waits for them, and re-layouts: 18.3 us -> 2.7 us
    pallas_call x1, Pallas kernels: 108 us -> 78.2 us  [forward(): pl.pallas_call(forward_kernel, out_shape=(sds((ROW, D), f32), sds((ROW, D...]
    pallas_call x1, Pallas kernels: 126 us -> 101 us  [backward(): pl.pallas_call(functools.partial(backward_kernel, groups), out_shape=(sds...]
    pallas_call x0 -> x1, Pallas kernels: none -> 7.97 us  [hand_over(): pl.pallas_call(functools.partial(hand_over_kernel, n), out_shape=tuple((s...]
    unnamed x13 -> x0, local copies, waits for them, and re-layouts: 6.27 us -> none
    transpose x2 -> x0, local copies, waits for them, and re-layouts: 5.13 us -> none  [the longest x1 3.08 us: body(): mlp_grad[:, 2 * ff:]]
    pallas_call x1, Pallas kernels: 99.1 us -> 103 us  [feed(): pl.pallas_call(feed_kernel, out_shape=(sds((ROW, D), bf16), sds((ROW, D),...]
where the time goes in v3:
time: 300 us; the launch traced here: 299 us
  Pallas kernels  291 us (97%)
  other arithmetic  3.55 us (1%)
    pallas_call x1, Pallas kernels, feed(): pl.pallas_call(feed_kernel, out_shape=(sds((ROW, D), bf16), sds((ROW, D),...  103 us
    pallas_call x1, Pallas kernels, backward(): pl.pallas_call(functools.partial(backward_kernel, groups), out_shape=(sds...  101 us
    pallas_call x1, Pallas kernels, forward(): pl.pallas_call(forward_kernel, out_shape=(sds((ROW, D), f32), sds((ROW, D...  78.2 us
    pallas_call x1, Pallas kernels, hand_over(): pl.pallas_call(functools.partial(hand_over_kernel, n), out_shape=tuple((s...  7.97 us

profile of v3, /device:TPU:0, one launch (start us, length us, event | category | flops | bytes accessed | tf_op | source)
XLA Modules:
  0.0 299.5 jit_solution(14963129153398807186)
XLA Ops:
  0.7 1.4 fusion.1
  4.0 0.7 subtract_convert_fusion
  4.6 1.4 broadcast_select_fusion.gains
  6.0 1.5 multiply_sine_fusion
  7.5 78.2 %attention_forward.1 = (f32[1024,1536]{1,0:T(8,128)}, bf16[1024,1536]{1,0:T(8,128)(2,1)}, bf16[1536,1024]{1,0:T(8,128)(2,1)}, bf16[16,128,1024]{2,1,0:T(8,128)(2...) custom-call(s32[1,4]{1,0:T(1,128)} %lengths.1, ...), custom_call_target="tpu_custom_call" | custom-call | tf_op jit(solution)/shard_map/attention_forward/pallas_call | solution.py:446
  85.8 102.9 %feed_forward.1 = (bf16[1024,1536]{1,0:T(8,128)(2,1)}, f32[1024,1536]{1,0:T(8,128)}, bf16[1024,1536]{1,0:T(8,128)(2,1)}, bf16[1536,1024]{1,0:T(8,128)(2,1)}, f32...) custom-call(bf16[2,1536]{1,0:T(2,128)(2,1)} %broadcast_select_fusion.gains, ...), custom_call_target="tpu_custom_call" | custom-call | tf_op jit(solution)/shard_map/feed_forward/pallas_call | solution.py:842
  188.7 101.5 %attention_backward.1 = (bf16[1024,1536]{1,0:T(8,128)(2,1)}, bf16[1024,1536]{1,0:T(8,128)(2,1)}, f32[192,384]{1,0:T(8,128)}, f32[192,192]{1,0:T(8,128)}, f32[192...) custom-call(bf16[2,1536]{1,0:T(2,128)(2,1)} %broadcast_select_fusion.gains, f32[48,1024]{1,0:T(8,128)} %get-tuple-element.86.cos, ...), custom_call_target="tpu_custom_call" | custom-call | tf_op jit(solution)/shard_map/attention_backward/pallas_call | solution.py:1146
  290.1 8.0 %hand_over.1 = (bf16[1024,1536]{1,0:T(8,128)(2,1)}, bf16[1024,1536]{1,0:T(8,128)(2,1)}, f32[192,384]{1,0:T(8,128)}, f32[192,192]{1,0:T(8,128)}, f32[192,192]{1,0...) custom-call(bf16[1024,1536]{1,0:T(8,128)(2,1)} %get-tuple-element.63, ...), custom_call_target="tpu_custom_call" | custom-call | tf_op jit(solution)/shard_map/hand_over/pallas_call | solution.py:1220
  298.1 1.3 fusion
  (2 shorter events, 0.0 us)

commit v4 on v3

--- a/solution.py
+++ b/solution.py
@@ -2,6 +2,7 @@
 
 import jax
 import jax.numpy as jnp
+import numpy as np
 from jax import lax
 from jax.experimental import pallas as pl
 from jax.experimental.pallas import tpu as pltpu
@@ -14,9 +15,11 @@
 NZ = 4
 CH = 256
 TB = 128
-BL = 64
-LAG = 2
-RING = 10
+BL = 32
+LAG = 4
+RING = 18
+BL3 = 64
+AHEAD = 4
 HQ_OWN = 4
 KV_OWN = 2
 QR = HQ_OWN * HD
@@ -155,6 +158,18 @@
             between(qb // 2)
 
 
+def angle_tables(lengths, freqs, cos, sin):
+    place = lax.broadcasted_iota(jnp.int32, (1, ROW), 1)
+    start = jnp.zeros((1, ROW), jnp.int32)
+    finish = jnp.int32(0)
+    for i in range(SEGS - 1):
+        finish = finish + lengths[0, i]
+        start = jnp.where(place >= finish, finish, start)
+    angles = freqs[...] * (place - start).astype(f32)
+    cos[...] = jnp.cos(angles)
+    sin[...] = jnp.sin(angles)
+
+
 def order(z, j):
     places_of = (0, 1, 2, 3), (1, 0, 2, 3), (2, 3, 1, 0), (3, 2, 1, 0)
     s = jnp.int32(0)
@@ -188,9 +203,9 @@
 OSLICE = QR // 8
 
 
-def forward_kernel(lengths, gains, cos, sin, x_i, qw_i, kw, vw, ow, cot,
+def forward_kernel(lengths, gains, freqs, x_i, qw_i, kw, vw, ow, cot,
                    mid_o, hid2_o, ho_o, qt_o, kt_o, kk_o, vv_o, w_o, hid1t_o, hid2t_o, cott_o,
-                   x, qw, w, hid, ho, qt, kt, kk, vt, vv, qaug, kaug, midb, hidb, hidtb, cb, ctb,
+                   cos, sin, x, qw, w, hid, ho, qt, kt, kk, vt, vv, qaug, kaug, midb, hidb, hidtb, cb, ctb,
                    zsend, zrecv, xsend, xrecv, ysend, yrecv, csend, crecv, osem, wsem, msem, tsem):
     dp, z, low = places()
     pc, px, py = (partner(low, dp, bit) for bit in (1, 2, 4))
@@ -298,6 +313,7 @@
         for e in EVENTS.get(("before", j), ()):
             do(*e)
 
+    angle_tables(lengths, freqs, cos, sin)
     place = lax.broadcasted_iota(jnp.int32, (1, ROW), 1)
     row = lax.broadcasted_iota(jnp.int32, (128 - HD, ROW), 0)
     segment = jnp.zeros((1, ROW), jnp.int32)
@@ -439,7 +455,7 @@
                     c.wait_send()
 
 
-def forward(lengths, x, gains, cos, sin, qw, kw, vw, ow, cot):
+def forward(lengths, x, gains, freqs, qw, kw, vw, ow, cot):
     heads = NZ * HQ_OWN
     kv = NZ * KV_OWN
     vm = pltpu.VMEM
@@ -449,9 +465,10 @@
                    sds((heads, 128, ROW), bf16), sds((kv, 128, ROW), bf16), sds((kv, ROW, 128), bf16),
                    sds((kv, ROW, 128), bf16), sds((NZ, WR, D), bf16), sds((D, ROW), bf16), sds((D, ROW), bf16),
                    sds((D, ROW), bf16)),
-        in_specs=[pl.BlockSpec(memory_space=pltpu.SMEM)] + [VM] * 3 + [ANY] * 6,
+        in_specs=[pl.BlockSpec(memory_space=pltpu.SMEM)] + [VM] * 2 + [ANY] * 6,
         out_specs=(ANY,) * 11,
         scratch_shapes=[
+            vm((HD // 2, ROW), f32), vm((HD // 2, ROW), f32),
             vm((ROW, D), bf16), vm((D, QR), bf16), vm((NZ, WR, D), bf16), vm((ROW, D), bf16), vm((heads * HD, ROW), bf16),
             vm((heads, 128, ROW), bf16), vm((kv, 128, ROW), bf16), vm((kv, ROW, 128), bf16),
             vm((kv, 128, ROW), bf16), vm((kv, ROW, 128), bf16),
@@ -462,30 +479,21 @@
         compiler_params=pltpu.CompilerParams(
             collective_id=1, has_side_effects=True, vmem_limit_bytes=60 * 2**20),
         name="attention_forward",
-    )(lengths, gains, cos, sin, x, qw, kw, vw, ow, cot)
-
-
-def angles_of(lengths):
-    place = jnp.arange(ROW, dtype=jnp.int32)
-    start = jnp.zeros((ROW,), jnp.int32)
-    finish = jnp.int32(0)
-    for i in range(SEGS - 1):
-        finish = finish + lengths[i]
-        start = jnp.where(place >= finish, finish, start)
-    positions = (place - start).astype(f32)
-    freqs = rope_base ** (-(jnp.arange(HD // 2, dtype=f32) * 2.0) / HD)
-    angles = freqs[:, None] * positions[None, :]
-    return jnp.cos(angles), jnp.sin(angles)
+    )(lengths, gains, freqs, x, qw, kw, vw, ow, cot)
+
+
+def frequencies():
+    return jnp.asarray(np.power(np.float32(rope_base), -(np.arange(HD // 2, dtype=np.float32) * 2) / np.float32(HD))[:, None])
 
 
 class RowSum:
-    def __init__(self, z, own, rend, rmid, out, ssem, esem, msem, osem, ring, lag):
-        self.z, self.own, self.ring, self.lag = z, own, ring, lag
+    def __init__(self, z, own, rend, rmid, out, ssem, esem, msem, osem, ring, lag, begun=0, turn=1):
+        self.z, self.own, self.ring, self.lag, self.begun, self.turn = z, own, ring, lag, begun, turn
         self.rend, self.rmid, self.out = rend, rmid, out
         self.ssem, self.esem, self.msem, self.osem = ssem, esem, msem, osem
 
     def who(self, i):
-        odd = lax.rem(i, 2)
+        odd = lax.rem(i // self.turn, 2)
         return 3 * odd, 1 + odd, 2 - odd, 3 - 3 * odd
 
     def copy(self, kind, i, to, sem=0):
@@ -520,8 +528,11 @@
         s = lax.rem(i, self.ring)
 
         def go():
-            self.copy("end", i, e).wait_recv()
-            self.copy("mid", i, e).wait_recv()
+            @pl.when(i >= self.begun)
+            def _():
+                self.copy("end", i, e).wait_recv()
+                self.copy("mid", i, e).wait_recv()
+
             self.out[s] = (self.own(i)[...].astype(f32) + self.rend[s].astype(f32)
                            + self.rmid[s].astype(f32)).astype(bf16)
             self.copy("out", i, m, 1).start()
@@ -545,11 +556,14 @@
 
     def drain(self, i):
         e, o, m, f = self.who(i)
-        self.on(e, lambda: self.copy("end", i, o).wait_send())
-        self.on(f, lambda: self.copy("end", i, m).wait_send())
+
+        @pl.when(i >= self.begun)
+        def _():
+            self.on(e, lambda: self.copy("end", i, o).wait_send())
+            self.on(f, lambda: self.copy("end", i, m).wait_send())
+            self.on(m, lambda: self.copy("mid", i, o).wait_send())
 
         def middle():
-            self.copy("mid", i, o).wait_send()
             self.copy("out", i, f, 1).wait_send()
 
         def owner():
@@ -559,7 +573,19 @@
         self.on(m, middle)
         self.on(o, owner)
 
-    def tick(self, t, count, finish):
+    def half_done(self, i):
+        e, o, m, f = self.who(i)
+        self.on(e, lambda: self.copy("end", i, o).wait_send())
+        self.on(f, lambda: self.copy("end", i, m).wait_send())
+        self.on(m, lambda: self.copy("mid", i, o).wait_send())
+
+        def owner():
+            self.copy("end", i, e).wait_recv()
+            self.copy("mid", i, e).wait_recv()
+
+        self.on(o, owner)
+
+    def tick(self, t, count, finish, begun=0, ahead=0):
         def last(i):
             self.arrive(i)
             finish(i)
@@ -567,7 +593,8 @@
 
         for lag, step in ((4, last), (3, self.step4), (2, self.step3), (1, self.step2), (0, self.step1)):
             i = t - lag * self.lag
-            pl.when((i >= 0) & (i < count))(functools.partial(step, i))
+            lo, hi = (begun, count + ahead) if lag < 2 else (0, count)
+            pl.when((i >= lo) & (i < hi))(functools.partial(step, i))
 
 
 class GradSum:
@@ -666,11 +693,11 @@
 
 
 def feed_kernel(gains, hid2, cot, mid, hid2t_i, cott_i, gw_i, uw_i, dw_i,
-                mlp_o, gm_o, gml_o, gmlt_o, gain2_o, gate_o, up_o, down_o,
+                mlp_o, gm_o, gml_o, gmlt_o, gain2_o, gate_o, up_o, down_o, end_o, mid_o,
                 gw, uw, dw, a3, side, own, hb, cb, tb, mb, cb2, gmb, gmlb, gmltb,
                 rend, rmid, out, zs, ze, zm, zo,
                 g, c1, x1, y1, x2, y2, gs, gr,
-                lsem, bsem, tsem, msem, wsem):
+                lsem, bsem, tsem, msem, wsem, asem):
     dp, z, low = places()
     loads = [pltpu.make_async_copy(a, b, lsem.at[i]) for i, (a, b) in enumerate(
         ((gw_i, gw), (uw_i, uw), (dw_i, dw), (hid2t_i, side), (cott_i, side)))]
@@ -678,6 +705,7 @@
     nb = ROW // BL
     nj = ROW // 128
     pair = 128 // BL
+    per = BL3 // BL
 
     def chunk_loads(c):
         return [pltpu.make_async_copy(src.at[chunk(c)], dst.at[lax.rem(c, 2)], bsem.at[i, lax.rem(c, 2)])
@@ -696,7 +724,7 @@
             def _(ref=ref):
                 ref[:, at] = v
 
-    zsum = RowSum(z, lambda i: own.at[chunk(i, BL)], rend, rmid, out, zs, ze, zm, zo, RING, LAG)
+    zsum = RowSum(z, lambda i: own.at[chunk(lax.rem(i, nb), BL)], rend, rmid, out, zs, ze, zm, zo, RING, LAG, turn=BL3 // BL)
     gsum = GradSum(dp, low, MLP_WIDTH, MLP_WIDTH // 2, g, c1, x1, y1, x2, y2, gs, gr, emit)
     gain2_o[...] = jnp.zeros_like(gain2_o)
 
@@ -749,7 +777,10 @@
         c.start()
 
     def tick(t):
-        zsum.tick(t, nb, finish)
+        for k in range(per):
+            zsum.tick(per * t + k, nb, finish, ahead=AHEAD * per)
+
+    again = pltpu.make_async_copy(mlp_o.at[pl.ds(0, AHEAD * BL3)], own.at[pl.ds(0, AHEAD * BL3)], asem)
 
     def mlp_write(c):
         return pltpu.make_async_copy(tb.at[lax.rem(c, 2)], mlp_o.at[chunk(c)], tsem.at[lax.rem(c, 2)])
@@ -814,26 +845,45 @@
     def beat(t, _):
         first = 2 * nc
         u = t - first
+
+        @pl.when(t == first)
+        def _():
+            for c in range(max(nc - 2, 0), nc):
+                mlp_write(c).wait()
+
+        @pl.when(t == nb // per)
+        def _():
+            again.start()
+            again.wait()
+
         pl.when(u < MLP_UNITS)(lambda: unit(u))
         tick(t)
-        for k, lag in ((3, 9), (2, 5), (1, 1)):
+        for k, lag in ((3, 8), (2, 4), (1, 1)):
             v = u - lag
             pl.when((v >= 0) & (v < MLP_UNITS))(functools.partial(gsum.stage, k, v))
         return 0
 
     lax.fori_loop(0, nc, mlp_chunk, 0)
-    lax.fori_loop(2 * nc, nb + 4 * LAG, beat, 0)
+    lax.fori_loop(2 * nc, (nb + 4 * LAG + per - 1) // per, beat, 0)
 
     def drains(u, _):
         gsum.drain(u)
         return 0
 
     lax.fori_loop(0, MLP_UNITS, drains, 0)
-    for c in range(max(nc - 2, 0), nc):
-        mlp_write(c).wait()
     for j in range(nj - 2, nj):
         for c in gm_writes(j):
             c.wait()
+    keep = []
+    for i in range(AHEAD * per):
+        zsum.half_done(nb + i)
+        s = (nb + i) % RING
+        keep += [pltpu.make_async_copy(rend.at[s], end_o.at[i], zs.at[0, s]),
+                 pltpu.make_async_copy(rmid.at[s], mid_o.at[i], zs.at[1, s])]
+    for c in keep:
+        c.start()
+    for c in keep:
+        c.wait()
 
 
 def feed(gains, hid2, cot, mid, hid2t, cott, gw, uw, dw):
@@ -842,9 +892,10 @@
     return pl.pallas_call(
         feed_kernel,
         out_shape=(sds((ROW, D), bf16), sds((ROW, D), f32), sds((ROW, D), bf16), sds((D, ROW), bf16),
-                   sds((1, D), f32), sds((D // 8, ff), f32), sds((D // 8, ff), f32), sds((D // 8, ff), f32)),
+                   sds((1, D), f32), sds((D // 8, ff), f32), sds((D // 8, ff), f32), sds((D // 8, ff), f32),
+                   sds((AHEAD * BL3 // BL, BL, D), bf16), sds((AHEAD * BL3 // BL, BL, D), bf16)),
         in_specs=[VM] + [ANY] * 8,
-        out_specs=(ANY, ANY, ANY, ANY, VM, VM, VM, VM),
+        out_specs=(ANY, ANY, ANY, ANY, VM, VM, VM, VM, ANY, ANY),
         scratch_shapes=[
             vm((D, ff), bf16), vm((D, ff), bf16), vm((ff, D), bf16), vm((3, ROW, ff), bf16),
             vm((D, ROW), bf16), vm((ROW, D), bf16),
@@ -852,17 +903,17 @@
             vm((128, D), f32), vm((128, D), bf16), vm((2, 128, D), f32), vm((2, 128, D), bf16),
             vm((2, D, 128), bf16)]
         + ring_scratch(RING, BL) + sum_scratch(MLP_UNITS, MLP_WIDTH, MLP_WIDTH // 2)
-        + [DMA((5,)), DMA((2, 2)), DMA((2,)), DMA((2,)), DMA((3, 2))],
+        + [DMA((5,)), DMA((2, 2)), DMA((2,)), DMA((2,)), DMA((3, 2)), DMA],
         compiler_params=pltpu.CompilerParams(
             collective_id=2, has_side_effects=True, vmem_limit_bytes=63 * 2**20),
         name="feed_forward",
     )(gains, hid2, cot, mid, hid2t, cott, gw, uw, dw)
 
 
-BL3 = 64
 RING3 = 10
 LAG3 = 2
 WIDTH = QR
+BEATS = 10
 CUT = 128
 
 
@@ -912,12 +963,12 @@
         gt[at, lo:hi] = unrotate(dq[0:HD, h * CH:(h + 1) * CH] * SCALE, cos[:, lo:hi], sin[:, lo:hi])
 
 
-def backward_kernel(groups, gains, cos, sin, gain2_i, x, mid, mlp, gm, gml_i, gmlt, hid1t, ho_i, qt_i, kt_i, kk_i, vv_i, w_i,
+def backward_kernel(groups, lengths, gains, freqs, gain2_i, x, mid, mlp, gm, gml_i, gmlt, hid1t, ho_i, qt_i, kt_i, kk_i, vv_i, w_i, end_i, mid_i,
                     out_o, xg_o, qg_o, kg_o, vg_o, og_o, gains_o,
-                    w, wo, ho, qk, kk, vv, dk, dv, gt, gml, dot, ga1, own, mb2, ob2, xb, gb, ob,
+                    cos, sin, w, wo, ho, qk, kk, vv, dk, dv, gt, gml, dot, ga1, own, mb2, ob2, xb, gb, ob,
                     rend, rmid, out, zs, ze, zm, zo,
                     c1, x1, y1, x2, y2, gs, gr, og, oc1, ox1, oy1, ox2, oy2, ogs, ogr, tb, gsend, grecv,
-                    lsem, bsem, wsem, psem, osem, isem, tsem, ssem, rsem):
+                    lsem, bsem, wsem, psem, osem, isem, tsem, ssem, rsem, asem):
     dp, z, low = places()
     qrows = NZ * HQ_OWN * 128
     loads = [pltpu.make_async_copy(ho_i, ho, lsem.at[1]),
@@ -948,15 +999,20 @@
     def turned_load(k):
         return pltpu.make_async_copy(gmlt.at[pl.ds(k * 192, 192)], tb.at[k % 2], tsem.at[k % 2])
 
-    own_load(0).start()
-    own_load(1).start()
+    begun = [pltpu.make_async_copy(src, dst.at[pl.ds(0, AHEAD)], asem.at[i])
+             for i, (src, dst) in enumerate(((end_i, rend), (mid_i, rmid)))]
+    for c in begun:
+        c.start()
+    for i in range(2 * LAG3 + 2):
+        own_load(i).start()
     mid_load(0).start()
     turned_load(0).start()
     turned_load(1).start()
     for c in loads:
         c.start()
     greet(dp, z, low, range(1, 8))
-    zsum = RowSum(z, lambda i: own.at[lax.rem(i, RING3)], rend, rmid, out, zs, ze, zm, zo, RING3, LAG3)
+    angle_tables(lengths, freqs, cos, sin)
+    zsum = RowSum(z, lambda i: own.at[lax.rem(i, RING3)], rend, rmid, out, zs, ze, zm, zo, RING3, LAG3, AHEAD)
 
     def emit(u, lo, hi, v):
         if u == 0:
@@ -988,16 +1044,18 @@
         def _():
             mid_load(i + 1).start()
 
-    per = 64 // BL3
-
     def tick(beat):
-        for k in range(per):
-            t = beat * per + k
-            pl.when(t < nb)(functools.partial(lambda t: own_load(t).wait(), t))
-            zsum.tick(t, nb, finish)
-            pl.when(t + 2 < nb)(functools.partial(lambda t: own_load(t + 2).start(), t))
-
+        t = beat + 2 * LAG3
+        pl.when((t >= AHEAD) & (t < nb))(lambda: own_load(t).wait())
+        zsum.tick(t, nb, finish, begun=AHEAD)
+        pl.when(t + 2 < nb)(lambda: own_load(t + 2).start())
+
+    for i in range(AHEAD):
+        own_load(i).wait()
+    for c in begun:
+        c.wait()
     tick(0)
+    tick(1)
     loads[0].wait()
     o_rows = ho[pl.ds(pl.multiple_of(z * QR, 128), QR), :]
     for k in range(8):
@@ -1006,15 +1064,12 @@
         if k + 2 < 8:
             turned_load(k + 2).start()
     osum.start(0)
-    tick(1)
+    tick(2)
     for c in loads[1:]:
         c.wait()
     for c in wloads:
         c.start()
 
-    def extra(g):
-        return (5 * g + 4) // 8
-
     def quarter(s, _):
         for h in range(2):
             t = nt(wo[s // 2, lax.rem(s, 2), h], gml[...])
@@ -1024,10 +1079,9 @@
             g = KV_OWN * s + gg
             for qb in range(ROW // CH):
                 attend_back(qk, kk, vv, dot, ho, dk, dv, gt, cos, sin, g, gg, qb)
-                if qb == 2:
-                    pl.when(extra(g + 1) > extra(g))(lambda: tick(2 + g + extra(g)))
-                if qb == 3:
-                    tick(2 + g + extra(g + 1))
+                done = 10 * g + qb * (qb + 1) // 2
+                was, now = (done * BEATS) // 80, ((done + qb + 1) * BEATS) // 80
+                pl.when(now > was)(functools.partial(tick, 3 + was))
             first = pl.multiple_of(s * QKV + QR + gg * HD, 32)
             gt[pl.ds(first, HD), :] = unrotate(dk[...].T[0:HD] * SCALE, cos[...], sin[...])
             gt[pl.ds(pl.multiple_of(first + KR, 32), HD), :] = dv[...].T[0:HD].astype(bf16)
@@ -1039,7 +1093,7 @@
         return 0
 
     lax.fori_loop(0, NZ, quarter, 0)
-    beats = 2 + 13
+    beats = 3 + BEATS
     for c in late:
         c.start()
     for c in wloads + late:
@@ -1119,7 +1173,7 @@
         tick(t)
         return 0
 
-    ends = (nb + 4 * LAG3 + per - 1) // per
+    ends = nb + 2 * LAG3
     if beats < ends:
         lax.fori_loop(beats, ends, rest, 0)
     gsum.stage(3, 1)
@@ -1139,7 +1193,7 @@
         out_write(i).wait()
 
 
-def backward(groups, gains, cos, sin, gain2_sum, x, mid, mlp, gm, gml, gmlt, hid1t, ho, qt, kt, kk, vv, w):
+def backward(groups, lengths, gains, freqs, gain2_sum, x, mid, mlp, gm, gml, gmlt, hid1t, ho, qt, kt, kk, vv, w, ends, mids):
     vm = pltpu.VMEM
     heads = NZ * HQ_OWN
     kv = NZ * KV_OWN
@@ -1147,10 +1201,10 @@
         functools.partial(backward_kernel, groups),
         out_shape=(sds((ROW, D), bf16), sds((ROW, D), bf16), sds((D // 8, QR), f32), sds((D // 8, KR), f32),
                    sds((D // 8, KR), f32), sds((D // 8, QR), f32), sds((8, 256), f32)),
-        in_specs=[VM] * 4 + [ANY] * 13,
+        in_specs=[pl.BlockSpec(memory_space=pltpu.SMEM)] + [VM] * 3 + [ANY] * 15,
         out_specs=(ANY, ANY) + (VM,) * 5,
         scratch_shapes=[
-            vm((NZ, QKV, D), bf16), vm((2, 2, 2, 192, D), bf16), vm((heads * HD, ROW), bf16),
+            vm((HD // 2, ROW), f32), vm((HD // 2, ROW), f32), vm((NZ, QKV, D), bf16), vm((2, 2, 2, 192, D), bf16), vm((heads * HD, ROW), bf16),
             vm(((heads + kv) * 128, ROW), bf16), vm((kv, ROW, 128), bf16), vm((kv, ROW, 128), bf16),
             vm((ROW, 128), f32), vm((ROW, 128), f32), vm((NZ * QKV, ROW), bf16),
             vm((ROW, D), bf16), vm((QR, ROW), bf16), vm((1, D), f32),
@@ -1158,11 +1212,12 @@
             vm((2, TB, D), bf16), vm((2, TB, D), f32), vm((2, TB, D), bf16)]
         + ring_scratch(RING3, BL3) + sum_scratch(2, WIDTH, CUT)[1:] + sum_scratch(1, WIDTH, CUT)
         + [vm((2, 192, ROW), bf16), vm((8, 8, 256), f32), vm((8, 8, 256), f32),
-           DMA((19,)), DMA((2, 2)), DMA((2,)), DMA((2,)), DMA((2, 2)), DMA((RING3,)), DMA((2,)), DMA((8,)), DMA((8,))],
+           DMA((19,)), DMA((2, 2)), DMA((2,)), DMA((2,)), DMA((2, 2)), DMA((RING3,)), DMA((2,)), DMA((8,)), DMA((8,)), DMA((2,))],
         compiler_params=pltpu.CompilerParams(
             collective_id=3, has_side_effects=True, vmem_limit_bytes=63 * 2**20),
         name="attention_backward",
-    )(gains, cos, sin, gain2_sum, x, mid, mlp, gm, gml, gmlt, hid1t, ho, qt, kt, kk, vv, w)
+    )(lengths, gains, freqs, gain2_sum, x, mid, mlp, gm, gml, gmlt, hid1t, ho, qt, kt, kk, vv, w,
+      ends, mids)
 
 
 def by_block(v, groups):
@@ -1178,14 +1233,14 @@
     cot = cotangent.reshape(ROW, D)
     first = lax.broadcasted_iota(jnp.int32, (2, D), 0) == 0
     gains = jnp.where(first, attn_gain[None, :], mlp_gain[None, :])
-    cos, sin = angles_of(lengths[0])
+    freqs = frequencies()
     mid, hid2, ho, qt, kt, kk, vv, w, hid1t, hid2t, cott = forward(
-        lengths, x, gains, cos, sin, q_weight, k_weight.T, v_weight.T, o_weight, cot)
-    mlp, gm, gml, gmlt, gain2_sum, gate_g, up_g, down_g = feed(
+        lengths, x, gains, freqs, q_weight, k_weight.T, v_weight.T, o_weight, cot)
+    mlp, gm, gml, gmlt, gain2_sum, gate_g, up_g, down_g, ends, mids = feed(
         gains, hid2, cot, mid, by_block(hid2t, groups), by_block(cott, groups), gate_weight, up_weight, down_weight)
     output, input_grad, q_g, k_g, v_g, o_g, gain_sums = backward(
-        groups, gains, cos, sin, gain2_sum, x, mid, mlp, gm, gml, by_block(gmlt, groups), by_block(hid1t, groups),
-        ho, qt.reshape(-1, ROW), kt.reshape(-1, ROW), kk, vv, w)
+        groups, lengths, gains, freqs, gain2_sum, x, mid, mlp, gm, gml, by_block(gmlt, groups), by_block(hid1t, groups),
+        ho, qt.reshape(-1, ROW), kt.reshape(-1, ROW), kk, vv, w, ends.reshape(-1, BL3, D), mids.reshape(-1, BL3, D))
     grads = [q_g, k_g, v_g, o_g, gate_g, up_g, down_g, gain_sums]
     if groups > 1:
         same = [[g * 8 + low for g in range(groups)] for low in range(8)]

time: 300 us -> 285 us (0.950)
  Pallas kernels: 291 us -> 281 us
    pallas_call x1, Pallas kernels: 101 us -> 90.5 us  [backward(): pl.pallas_call(functools.partial(backward_kernel, groups), out_shape=(sds...]
where the time goes in v4:
time: 285 us; the launch traced here: 284 us
  Pallas kernels  281 us (99%)
    pallas_call x1, Pallas kernels, feed(): pl.pallas_call(feed_kernel, out_shape=(sds((ROW, D), bf16), sds((ROW, D),...  104 us
    pallas_call x1, Pallas kernels, backward(): pl.pallas_call(functools.partial(backward_kernel, groups), out_shape=(sds...  90.5 us
    pallas_call x1, Pallas kernels, forward(): pl.pallas_call(forward_kernel, out_shape=(sds((ROW, D), f32), sds((ROW, D...  77.8 us
    pallas_call x1, Pallas kernels, hand_over(): pl.pallas_call(functools.partial(hand_over_kernel, n), out_shape=tuple((s...  7.97 us

profile of v4, /device:TPU:0, one launch (start us, length us, event | category | flops | bytes accessed | tf_op | source)
XLA Modules:
  0.0 284.0 jit_solution(5961426470576271807)
XLA Ops:
  0.7 1.4 broadcast_select_fusion.gains
  2.0 77.8 %attention_forward.1 = (f32[1024,1536]{1,0:T(8,128)}, bf16[1024,1536]{1,0:T(8,128)(2,1)}, bf16[1536,1024]{1,0:T(8,128)(2,1)}, bf16[16,128,1024]{2,1,0:T(8,128)(2...) custom-call(s32[1,4]{1,0:T(1,128)} %lengths.3, ...), custom_call_target="tpu_custom_call" | custom-call | tf_op jit(solution)/shard_map/attention_forward/pallas_call | solution.py:462
  79.8 104.4 %feed_forward.1 = (bf16[1024,1536]{1,0:T(8,128)(2,1)}, f32[1024,1536]{1,0:T(8,128)}, bf16[1024,1536]{1,0:T(8,128)(2,1)}, bf16[1536,1024]{1,0:T(8,128)(2,1)}, f32...) custom-call(bf16[2,1536]{1,0:T(2,128)(2,1)} %broadcast_select_fusion, ...), custom_call_target="tpu_custom_call" | custom-call | tf_op jit(solution)/shard_map/feed_forward/pallas_call | solution.py:892
  184.2 90.5 %attention_backward.1 = (bf16[1024,1536]{1,0:T(8,128)(2,1)}, bf16[1024,1536]{1,0:T(8,128)(2,1)}, f32[192,384]{1,0:T(8,128)}, f32[192,192]{1,0:T(8,128)}, f32[192...) custom-call(s32[1,4]{1,0:T(1,128)} %lengths.3, bf16[2,1536]{1,0:T(2,128)(2,1)} %broadcast_select_fusion.gains, ...), custom_call_target="tpu_custom_call" | custom-call | tf_op jit(solution)/shard_map/attention_backward/pallas_call | solution.py:1200
  274.7 8.0 %hand_over.1 = (bf16[1024,1536]{1,0:T(8,128)(2,1)}, bf16[1024,1536]{1,0:T(8,128)(2,1)}, f32[192,384]{1,0:T(8,128)}, f32[192,192]{1,0:T(8,128)}, f32[192,192]{1,0...) custom-call(bf16[1024,1536]{1,0:T(8,128)(2,1)} %get-tuple-element.67, ...), custom_call_target="tpu_custom_call" | custom-call | tf_op jit(solution)/shard_map/hand_over/pallas_call | solution.py:1275
  282.7 1.3 fusion
  (1 shorter events, 0.0 us)

commit v5 on v4

--- a/solution.py
+++ b/solution.py
@@ -14,10 +14,10 @@
 SEGS = 4
 NZ = 4
 CH = 256
-TB = 128
-BL = 32
-LAG = 4
-RING = 18
+TB = 256
+BL = 64
+LAG = 2
+RING = 10
 BL3 = 64
 AHEAD = 4
 HQ_OWN = 4
@@ -130,22 +130,27 @@
 
 
 def attend(qt, kk, vt, ho, qaug, g, between):
-    for qb in range(ROW // CH):
+    ki = lax.broadcasted_iota(jnp.int32, (CH, CH), 0)
+    qi = lax.broadcasted_iota(jnp.int32, (CH, CH), 1)
+    keep = jnp.concatenate([ki <= qi, ki <= qi], axis=1)
+
+    def scores(qb):
         lo = qb * CH
         nk = lo + CH
         q = jnp.concatenate([qt[2 * g, :, lo:nk], qt[2 * g + 1, :, lo:nk]], axis=1)
-        st = nn(kk[g, 0:nk, :], q)
-        ki = lax.broadcasted_iota(jnp.int32, (CH, CH), 0)
-        qi = lax.broadcasted_iota(jnp.int32, (CH, CH), 1)
-        keep = jnp.concatenate([ki <= qi, ki <= qi], axis=1)
-        dg = jnp.where(keep, st[lo:nk], NEG)
-        m = jnp.max(dg, axis=0, keepdims=True)
-        if qb:
-            m = jnp.maximum(m, jnp.max(st[0:lo], axis=0, keepdims=True))
+        return [nn(kk[g, kb * CH:(kb + 1) * CH, :], q) for kb in range(qb + 1)]
+
+    def rest(qb, st):
+        lo = qb * CH
+        nk = lo + CH
+        st[qb] = jnp.where(keep, st[qb], NEG)
+        m = jnp.max(st[qb], axis=0, keepdims=True)
+        for kb in range(qb):
+            m = jnp.maximum(m, jnp.max(st[kb], axis=0, keepdims=True))
         mc = m * C2
-        o = nn(vt[g, :, lo:nk], jnp.exp2(dg * C2 - mc).astype(bf16))
-        if qb:
-            o = o + nn(vt[g, :, 0:lo], jnp.exp2(st[0:lo] * C2 - mc).astype(bf16))
+        o = jnp.zeros((128, 2 * CH), f32)
+        for kb in range(qb + 1):
+            o = o + nn(vt[g, :, kb * CH:(kb + 1) * CH], jnp.exp2(st[kb] * C2 - mc).astype(bf16))
         total = o[HD:HD + 1]
         r = (o[0:HD] / total).astype(bf16)
         back = (mc + jnp.log2(total)) * (-1.0 / C2)
@@ -154,8 +159,14 @@
             ho[pl.ds(pl.multiple_of(g * 2 * HD + h * HD, 32), HD), lo:nk] = r[:, part]
             base = qaug[:, lo:nk].astype(f32)
             qt[2 * g + h, HD:128, lo:nk] = extra_rows(base, back[:, part], SEGS)
-        if qb % 2:
-            between(qb // 2)
+
+    st = scores(0)
+    for qb in range(ROW // CH):
+        following = scores(qb + 1) if qb + 1 < ROW // CH else None
+        rest(qb, st)
+        st = following
+    between(0)
+    between(1)
 
 
 def angle_tables(lengths, freqs, cos, sin):
@@ -692,15 +703,22 @@
 MLP_WIDTH = 512
 
 
-def feed_kernel(gains, hid2, cot, mid, hid2t_i, cott_i, gw_i, uw_i, dw_i,
-                mlp_o, gm_o, gml_o, gmlt_o, gain2_o, gate_o, up_o, down_o, end_o, mid_o,
-                gw, uw, dw, a3, side, own, hb, cb, tb, mb, cb2, gmb, gmlb, gmltb,
+def feed_kernel(gains, hid2, cot, mid, hid2t_i, cott_i, gw_i, uw_i, dw_i, w_i,
+                mlp_o, gm_o, dot_o, gmlt_o, gain2_o, gate_o, up_o, down_o, end_o, mid_o,
+                gw, uw, dw, a3, side, own, hb, cb, tb, mb, cb2, gmb, dotb, gmltb,
                 rend, rmid, out, zs, ze, zm, zo,
                 g, c1, x1, y1, x2, y2, gs, gr,
-                lsem, bsem, tsem, msem, wsem, asem):
+                lsem, bsem, tsem, msem, wsem, asem, vsem):
     dp, z, low = places()
     loads = [pltpu.make_async_copy(a, b, lsem.at[i]) for i, (a, b) in enumerate(
         ((gw_i, gw), (uw_i, uw), (dw_i, dw), (hid2t_i, side), (cott_i, side)))]
+    oloads = []
+    for s in range(NZ):
+        for ref, lo, hi in ((dw, 0, D - 2 * CH), (hb.at[0], D - 2 * CH, D - CH), (hb.at[1], D - CH, D)):
+            a, b = max(lo, s * QR), min(hi, (s + 1) * QR)
+            if a < b:
+                oloads.append(pltpu.make_async_copy(
+                    w_i.at[s, pl.ds(QKV + a - s * QR, b - a)], ref.at[pl.ds(a - lo, b - a)], vsem.at[len(oloads)]))
     nc = ROW // CH
     nb = ROW // BL
     nj = ROW // 128
@@ -737,7 +755,7 @@
         r = chunk(j, 128)
         s = lax.rem(j, 2)
         return [pltpu.make_async_copy(gmb.at[s], gm_o.at[r], wsem.at[0, s]),
-                pltpu.make_async_copy(gmlb.at[s], gml_o.at[r], wsem.at[1, s]),
+                pltpu.make_async_copy(dotb.at[s], dot_o.at[:, r], wsem.at[1, s]),
                 pltpu.make_async_copy(gmltb.at[s], gmlt_o.at[:, r], wsem.at[2, s])]
 
     def finish_pair(j):
@@ -760,8 +778,17 @@
         gm = cb2[...].astype(f32) + f * (gh * ga - n * jnp.mean(gn * ga, axis=1, keepdims=True))
         gmb[s] = gm
         low_gm = gm.astype(bf16)
-        gmlb[s] = low_gm
         gmltb[s] = low_gm.T
+
+        @pl.when(j == 0)
+        def _():
+            for c in oloads:
+                c.wait()
+
+        dotb[s, 0:D - 2 * CH] = nt(dw[...], low_gm).astype(bf16)
+        for k in range(2):
+            first = D - (2 - k) * CH
+            dotb[s, first:first + CH] = nt(hb[k], low_gm).astype(bf16)
         for c in gm_writes(j):
             c.start()
 
@@ -858,12 +885,14 @@
 
         pl.when(u < MLP_UNITS)(lambda: unit(u))
         tick(t)
-        for k, lag in ((3, 8), (2, 4), (1, 1)):
+        for k, lag in ((3, 10), (2, 6), (1, 2)):
             v = u - lag
             pl.when((v >= 0) & (v < MLP_UNITS))(functools.partial(gsum.stage, k, v))
         return 0
 
     lax.fori_loop(0, nc, mlp_chunk, 0)
+    for c in oloads:
+        c.start()
     lax.fori_loop(2 * nc, (nb + 4 * LAG + per - 1) // per, beat, 0)
 
     def drains(u, _):
@@ -886,34 +915,34 @@
         c.wait()
 
 
-def feed(gains, hid2, cot, mid, hid2t, cott, gw, uw, dw):
+def feed(gains, hid2, cot, mid, hid2t, cott, gw, uw, dw, w):
     vm = pltpu.VMEM
     ff = gw.shape[1]
     return pl.pallas_call(
         feed_kernel,
-        out_shape=(sds((ROW, D), bf16), sds((ROW, D), f32), sds((ROW, D), bf16), sds((D, ROW), bf16),
+        out_shape=(sds((ROW, D), bf16), sds((ROW, D), f32), sds((D, ROW), bf16), sds((D, ROW), bf16),
                    sds((1, D), f32), sds((D // 8, ff), f32), sds((D // 8, ff), f32), sds((D // 8, ff), f32),
                    sds((AHEAD * BL3 // BL, BL, D), bf16), sds((AHEAD * BL3 // BL, BL, D), bf16)),
-        in_specs=[VM] + [ANY] * 8,
+        in_specs=[VM] + [ANY] * 9,
         out_specs=(ANY, ANY, ANY, ANY, VM, VM, VM, VM, ANY, ANY),
         scratch_shapes=[
             vm((D, ff), bf16), vm((D, ff), bf16), vm((ff, D), bf16), vm((3, ROW, ff), bf16),
             vm((D, ROW), bf16), vm((ROW, D), bf16),
             vm((2, CH, D), bf16), vm((2, CH, D), bf16), vm((2, CH, D), bf16),
-            vm((128, D), f32), vm((128, D), bf16), vm((2, 128, D), f32), vm((2, 128, D), bf16),
+            vm((128, D), f32), vm((128, D), bf16), vm((2, 128, D), f32), vm((2, D, 128), bf16),
             vm((2, D, 128), bf16)]
         + ring_scratch(RING, BL) + sum_scratch(MLP_UNITS, MLP_WIDTH, MLP_WIDTH // 2)
-        + [DMA((5,)), DMA((2, 2)), DMA((2,)), DMA((2,)), DMA((3, 2)), DMA],
+        + [DMA((5,)), DMA((2, 2)), DMA((2,)), DMA((2,)), DMA((3, 2)), DMA, DMA((6,))],
         compiler_params=pltpu.CompilerParams(
             collective_id=2, has_side_effects=True, vmem_limit_bytes=63 * 2**20),
         name="feed_forward",
-    )(gains, hid2, cot, mid, hid2t, cott, gw, uw, dw)
+    )(gains, hid2, cot, mid, hid2t, cott, gw, uw, dw, w)
 
 
 RING3 = 10
 LAG3 = 2
 WIDTH = QR
-BEATS = 10
+BEATS = 9
 CUT = 128
 
 
@@ -930,7 +959,7 @@
     q = jnp.concatenate([qk[pl.ds(pl.multiple_of((2 * g + h) * 128, 128), 128), lo:hi] for h in range(2)], axis=1)
     parts = []
     for h in range(2):
-        do = dot[pl.ds(pl.multiple_of((2 * gg + h) * HD, 32), HD), lo:hi]
+        do = dot[pl.ds(pl.multiple_of((2 * g + h) * HD, 32), HD), lo:hi]
         o = ho[pl.ds(pl.multiple_of((2 * g + h) * HD, 32), HD), lo:hi]
         delta = jnp.sum(do.astype(f32) * o.astype(f32), axis=0, keepdims=True)
         extra = extra_rows(jnp.zeros((128 - HD, CH), f32), -delta, 0)
@@ -963,20 +992,18 @@
         gt[at, lo:hi] = unrotate(dq[0:HD, h * CH:(h + 1) * CH] * SCALE, cos[:, lo:hi], sin[:, lo:hi])
 
 
-def backward_kernel(groups, lengths, gains, freqs, gain2_i, x, mid, mlp, gm, gml_i, gmlt, hid1t, ho_i, qt_i, kt_i, kk_i, vv_i, w_i, end_i, mid_i,
+def backward_kernel(groups, lengths, gains, freqs, gain2_i, x, mid, mlp, gm, dot_i, gmlt, hid1t, ho_i, qt_i, kt_i, kk_i, vv_i, w_i, end_i, mid_i,
                     out_o, xg_o, qg_o, kg_o, vg_o, og_o, gains_o,
-                    cos, sin, w, wo, ho, qk, kk, vv, dk, dv, gt, gml, dot, ga1, own, mb2, ob2, xb, gb, ob,
+                    cos, sin, w, gbuf, ho, qk, kk, vv, dk, dv, gt, dot, ga1, own, mb2, ob2, xb, gb, ob,
                     rend, rmid, out, zs, ze, zm, zo,
                     c1, x1, y1, x2, y2, gs, gr, og, oc1, ox1, oy1, ox2, oy2, ogs, ogr, tb, gsend, grecv,
                     lsem, bsem, wsem, psem, osem, isem, tsem, ssem, rsem, asem):
     dp, z, low = places()
     qrows = NZ * HQ_OWN * 128
     loads = [pltpu.make_async_copy(ho_i, ho, lsem.at[1]),
-             pltpu.make_async_copy(gml_i, gml, lsem.at[0]),
+             pltpu.make_async_copy(dot_i, dot, lsem.at[0]),
              pltpu.make_async_copy(kk_i, kk, lsem.at[2]),
              pltpu.make_async_copy(vv_i, vv, lsem.at[3])]
-    loads += [pltpu.make_async_copy(w_i.at[s, pl.ds(QKV + 192 * h, 192)], wo.at[s // 2, s % 2, h], lsem.at[4 + 2 * s + h])
-              for s in range(NZ) for h in range(2)]
     loads += [pltpu.make_async_copy(qt_i, qk.at[pl.ds(0, qrows)], lsem.at[12]),
               pltpu.make_async_copy(kt_i, qk.at[pl.ds(qrows, NZ * KV_OWN * 128)], lsem.at[13])]
     wloads = [pltpu.make_async_copy(w_i.at[s, pl.ds(0, QKV)], w.at[s], lsem.at[14 + s]) for s in range(NZ)]
@@ -1026,7 +1053,7 @@
     def emit_o(u, lo, hi, v):
         og_o[:, lo:hi] = v
 
-    gsum = GradSum(dp, low, WIDTH, CUT, wo, c1, x1, y1, x2, y2, gs, gr, emit, True)
+    gsum = GradSum(dp, low, WIDTH, CUT, gbuf, c1, x1, y1, x2, y2, gs, gr, emit, True)
     osum = GradSum(dp, low, WIDTH, CUT, og, oc1, ox1, oy1, ox2, oy2, ogs, ogr, emit_o)
 
     def finish(i):
@@ -1071,10 +1098,6 @@
         c.start()
 
     def quarter(s, _):
-        for h in range(2):
-            t = nt(wo[s // 2, lax.rem(s, 2), h], gml[...])
-            dot[h * 192:(h + 1) * 192, :] = t.astype(bf16)
-
         def one(gg, _):
             g = KV_OWN * s + gg
             for qb in range(ROW // CH):
@@ -1147,15 +1170,15 @@
         res = gb[slot] + f * (acc * ga - n * jnp.mean(gn * ga, axis=1, keepdims=True))
         ob[slot] = res.astype(bf16)
         out_copy(b, slot).start()
-        pl.when(lax.rem(b, 2) == 1)(lambda: tick(beats + b // 2))
+        tick(beats + b)
         pl.when(b == 0)(lambda: (gsum.stage(1, 0), gsum.stage(1, 1)) and None)
-        pl.when(b == 2)(lambda: gsum.stage(2, 0))
-        pl.when(b == 4)(lambda: gsum.stage(2, 1))
-        pl.when(b == 6)(lambda: gsum.stage(3, 0))
+        pl.when(b == 1)(lambda: gsum.stage(2, 0))
+        pl.when(b == 2)(lambda: gsum.stage(2, 1))
+        pl.when(b == 3)(lambda: gsum.stage(3, 0))
         return 0
 
     lax.fori_loop(0, nt_blocks, tail, 0)
-    beats += nt_blocks // 2
+    beats += nt_blocks
 
     def gains_copy(mask):
         to = flip(low, mask)
@@ -1193,7 +1216,7 @@
         out_write(i).wait()
 
 
-def backward(groups, lengths, gains, freqs, gain2_sum, x, mid, mlp, gm, gml, gmlt, hid1t, ho, qt, kt, kk, vv, w, ends, mids):
+def backward(groups, lengths, gains, freqs, gain2_sum, x, mid, mlp, gm, dot, gmlt, hid1t, ho, qt, kt, kk, vv, w, ends, mids):
     vm = pltpu.VMEM
     heads = NZ * HQ_OWN
     kv = NZ * KV_OWN
@@ -1204,10 +1227,10 @@
         in_specs=[pl.BlockSpec(memory_space=pltpu.SMEM)] + [VM] * 3 + [ANY] * 15,
         out_specs=(ANY, ANY) + (VM,) * 5,
         scratch_shapes=[
-            vm((HD // 2, ROW), f32), vm((HD // 2, ROW), f32), vm((NZ, QKV, D), bf16), vm((2, 2, 2, 192, D), bf16), vm((heads * HD, ROW), bf16),
+            vm((HD // 2, ROW), f32), vm((HD // 2, ROW), f32), vm((NZ, QKV, D), bf16), vm((2, 2, 2, 192, 2 * WIDTH), bf16), vm((heads * HD, ROW), bf16),
             vm(((heads + kv) * 128, ROW), bf16), vm((kv, ROW, 128), bf16), vm((kv, ROW, 128), bf16),
             vm((ROW, 128), f32), vm((ROW, 128), f32), vm((NZ * QKV, ROW), bf16),
-            vm((ROW, D), bf16), vm((QR, ROW), bf16), vm((1, D), f32),
+            vm((heads * HD, ROW), bf16), vm((1, D), f32),
             vm((RING3, BL3, D), bf16), vm((2, BL3, D), f32), vm((2, BL3, D), bf16),
             vm((2, TB, D), bf16), vm((2, TB, D), f32), vm((2, TB, D), bf16)]
         + ring_scratch(RING3, BL3) + sum_scratch(2, WIDTH, CUT)[1:] + sum_scratch(1, WIDTH, CUT)
@@ -1216,7 +1239,7 @@
         compiler_params=pltpu.CompilerParams(
             collective_id=3, has_side_effects=True, vmem_limit_bytes=63 * 2**20),
         name="attention_backward",
-    )(lengths, gains, freqs, gain2_sum, x, mid, mlp, gm, gml, gmlt, hid1t, ho, qt, kt, kk, vv, w,
+    )(lengths, gains, freqs, gain2_sum, x, mid, mlp, gm, dot, gmlt, hid1t, ho, qt, kt, kk, vv, w,
       ends, mids)
 
 
@@ -1236,51 +1259,58 @@
     freqs = frequencies()
     mid, hid2, ho, qt, kt, kk, vv, w, hid1t, hid2t, cott = forward(
         lengths, x, gains, freqs, q_weight, k_weight.T, v_weight.T, o_weight, cot)
-    mlp, gm, gml, gmlt, gain2_sum, gate_g, up_g, down_g, ends, mids = feed(
-        gains, hid2, cot, mid, by_block(hid2t, groups), by_block(cott, groups), gate_weight, up_weight, down_weight)
+    mlp, gm, dot, gmlt, gain2_sum, gate_g, up_g, down_g, ends, mids = feed(
+        gains, hid2, cot, mid, by_block(hid2t, groups), by_block(cott, groups), gate_weight, up_weight, down_weight, w)
     output, input_grad, q_g, k_g, v_g, o_g, gain_sums = backward(
-        groups, lengths, gains, freqs, gain2_sum, x, mid, mlp, gm, gml, by_block(gmlt, groups), by_block(hid1t, groups),
+        groups, lengths, gains, freqs, gain2_sum, x, mid, mlp, gm, dot, by_block(gmlt, groups), by_block(hid1t, groups),
         ho, qt.reshape(-1, ROW), kt.reshape(-1, ROW), kk, vv, w, ends.reshape(-1, BL3, D), mids.reshape(-1, BL3, D))
-    grads = [q_g, k_g, v_g, o_g, gate_g, up_g, down_g, gain_sums]
+    grads = [q_g, k_g, v_g, o_g, gate_g, up_g, down_g]
     if groups > 1:
         same = [[g * 8 + low for g in range(groups)] for low in range(8)]
-        grads = [lax.psum_scatter(v, "dp", scatter_dimension=int(i == 7), axis_index_groups=same, tiled=True)
-                 for i, v in enumerate(grads[:7] + [gain_sums[:, 0:D // 8]])]
-    output, input_grad, *grads = hand_over(output, input_grad, *grads)
+        def over(v, dim=0):
+            return lax.psum_scatter(v, "dp", scatter_dimension=dim, axis_index_groups=same, tiled=True)
+
+        grads = [over(v) for v in grads]
+        gain_sums = over(gain_sums[:, 0:D // 8], 1)
+    output, input_grad, *grads = hand_over(gain_sums, output, input_grad, *grads)
     grads[3], grads[6] = grads[3].T, grads[6].T
-    grads[7:] = grads[7][0, 0:D // 8 // groups], grads[7][1, 0:D // 8 // groups]
     return (output.reshape(1, ROW, D), input_grad.reshape(1, ROW, D), *grads)
 
 
-def hand_over_kernel(n, *refs):
+def hand_over_kernel(n, sums, *refs):
+    first, second = refs[2 * n:2 * n + 2]
+    refs = refs[:2 * n] + refs[2 * n + 2:]
     held, load, store = refs[2 * n:3 * n], refs[3 * n], refs[3 * n + 1]
+    first[...] = sums[0, 0:first.shape[0]]
+    second[...] = sums[1, 0:second.shape[0]]
     pieces = []
     for i in range(n):
         rows = held[i].shape[0]
         parts = 4 if rows % 64 == 0 and rows > 512 else 1
         pieces += [(i, pl.ds(p * (rows // parts), rows // parts)) for p in range(parts)]
-    first = [pltpu.make_async_copy(refs[i].at[r], held[i].at[r], load.at[k]) for k, (i, r) in enumerate(pieces)]
-    then = [pltpu.make_async_copy(held[i].at[r], refs[n + i].at[r], store.at[k]) for k, (i, r) in enumerate(pieces)]
-    for c in first:
+    come = [pltpu.make_async_copy(refs[i].at[r], held[i].at[r], load.at[k]) for k, (i, r) in enumerate(pieces)]
+    go = [pltpu.make_async_copy(held[i].at[r], refs[n + i].at[r], store.at[k]) for k, (i, r) in enumerate(pieces)]
+    for c in come:
         c.start()
-    for a, b in zip(first, then):
+    for a, b in zip(come, go):
         a.wait()
         b.start()
-    for c in then:
+    for c in go:
         c.wait()
 
 
-def hand_over(*arrays):
+def hand_over(sums, *arrays):
     n = len(arrays)
+    keep = arrays[-1].shape[0]
     return pl.pallas_call(
         functools.partial(hand_over_kernel, n),
-        out_shape=tuple(sds(v.shape, v.dtype) for v in arrays),
-        in_specs=[ANY] * n,
-        out_specs=(ANY,) * n,
+        out_shape=tuple(sds(v.shape, v.dtype) for v in arrays) + (sds((keep,), f32),) * 2,
+        in_specs=[VM] + [ANY] * n,
+        out_specs=(ANY,) * n + (VM,) * 2,
         scratch_shapes=[pltpu.VMEM(v.shape, v.dtype) for v in arrays] + [DMA((4 * n,)), DMA((4 * n,))],
         compiler_params=pltpu.CompilerParams(vmem_limit_bytes=63 * 2**20),
         name="hand_over",
-    )(*arrays)
+    )(sums, *arrays)
 
 
 def solution(mesh):

time: 285 us -> 278 us (0.975)
  Pallas kernels: 281 us -> 275 us
    pallas_call x1, Pallas kernels: 90.5 us -> 83.7 us  [backward(): pl.pallas_call(functools.partial(backward_kernel, groups), out_shape=(sds...]
where the time goes in v5:
time: 278 us; the launch traced here: 277 us
  Pallas kernels  275 us (99%)
    pallas_call x1, Pallas kernels, feed(): pl.pallas_call(feed_kernel, out_shape=(sds((ROW, D), bf16), sds((ROW, D),...  106 us
    pallas_call x1, Pallas kernels, backward(): pl.pallas_call(functools.partial(backward_kernel, groups), out_shape=(sds...  83.7 us
    pallas_call x1, Pallas kernels, forward(): pl.pallas_call(forward_kernel, out_shape=(sds((ROW, D), f32), sds((ROW, D...  75.9 us
    pallas_call x1, Pallas kernels, hand_over(): pl.pallas_call(functools.partial(hand_over_kernel, n), out_shape=tuple((s...  9.16 us

profile of v5, /device:TPU:0, one launch (start us, length us, event | category | flops | bytes accessed | tf_op | source)
XLA Modules:
  0.0 277.2 jit_solution(14116857683866959272)
XLA Ops:
  0.7 1.4 broadcast_select_fusion.gains
  2.0 75.9 %attention_forward.1 = (f32[1024,1536]{1,0:T(8,128)}, bf16[1024,1536]{1,0:T(8,128)(2,1)}, bf16[1536,1024]{1,0:T(8,128)(2,1)}, bf16[16,128,1024]{2,1,0:T(8,128)(2...) custom-call(s32[1,4]{1,0:T(1,128)} %lengths.3, ...), custom_call_target="tpu_custom_call" | custom-call | tf_op jit(solution)/shard_map/attention_forward/pallas_call | solution.py:473
  77.9 106.3 %feed_forward.1 = (bf16[1024,1536]{1,0:T(8,128)(2,1)}, f32[1024,1536]{1,0:T(8,128)}, bf16[1536,1024]{1,0:T(8,128)(2,1)}, bf16[1536,1024]{1,0:T(8,128)(2,1)}, f32...) custom-call(bf16[2,1536]{1,0:T(2,128)(2,1)} %broadcast_select_fusion, ...), custom_call_target="tpu_custom_call" | custom-call | tf_op jit(solution)/shard_map/feed_forward/pallas_call | solution.py:921
  184.2 83.7 %attention_backward.1 = (bf16[1024,1536]{1,0:T(8,128)(2,1)}, bf16[1024,1536]{1,0:T(8,128)(2,1)}, f32[192,384]{1,0:T(8,128)}, f32[192,192]{1,0:T(8,128)}, f32[192...) custom-call(s32[1,4]{1,0:T(1,128)} %lengths.3, bf16[2,1536]{1,0:T(2,128)(2,1)} %broadcast_select_fusion.gains, ...), custom_call_target="tpu_custom_call" | custom-call | tf_op jit(solution)/shard_map/attention_backward/pallas_call | solution.py:1223
  267.9 9.2 %hand_over.1 = (bf16[1024,1536]{1,0:T(8,128)(2,1)}, bf16[1024,1536]{1,0:T(8,128)(2,1)}, f32[192,384]{1,0:T(8,128)}, f32[192,192]{1,0:T(8,128)}, f32[192,192]{1,0...) custom-call(f32[8,256]{1,0:T(8,128)} %get-tuple-element.68.sums, ...), custom_call_target="tpu_custom_call" | custom-call | tf_op jit(solution)/shard_map/hand_over/pallas_call | solution.py:1305
  (1 shorter events, 0.0 us)

commit v6 on v5

--- a/solution.py
+++ b/solution.py
@@ -942,7 +942,7 @@
 RING3 = 10
 LAG3 = 2
 WIDTH = QR
-BEATS = 9
+BEATS = 8
 CUT = 128
 
 

time: 278 us -> 277 us (level)
  no operation moved by 1% of the time
where the time goes in v6:
time: 277 us; the launch traced here: 276 us
  Pallas kernels  274 us (99%)
    pallas_call x1, Pallas kernels, feed(): pl.pallas_call(feed_kernel, out_shape=(sds((ROW, D), bf16), sds((ROW, D),...  106 us
    pallas_call x1, Pallas kernels, backward(): pl.pallas_call(functools.partial(backward_kernel, groups), out_shape=(sds...  82.7 us
    pallas_call x1, Pallas kernels, forward(): pl.pallas_call(forward_kernel, out_shape=(sds((ROW, D), f32), sds((ROW, D...  75.9 us
    pallas_call x1, Pallas kernels, hand_over(): pl.pallas_call(functools.partial(hand_over_kernel, n), out_shape=tuple((s...  9.16 us

profile of v6, /device:TPU:0, one launch (start us, length us, event | category | flops | bytes accessed | tf_op | source)
XLA Modules:
  0.0 276.3 jit_solution(2638596573067340560)
XLA Ops:
  0.7 1.4 broadcast_select_fusion.gains
  2.0 75.9 %attention_forward.1 = (f32[1024,1536]{1,0:T(8,128)}, bf16[1024,1536]{1,0:T(8,128)(2,1)}, bf16[1536,1024]{1,0:T(8,128)(2,1)}, bf16[16,128,1024]{2,1,0:T(8,128)(2...) custom-call(s32[1,4]{1,0:T(1,128)} %lengths.3, ...), custom_call_target="tpu_custom_call" | custom-call | tf_op jit(solution)/shard_map/attention_forward/pallas_call | solution.py:473
  77.9 106.3 %feed_forward.1 = (bf16[1024,1536]{1,0:T(8,128)(2,1)}, f32[1024,1536]{1,0:T(8,128)}, bf16[1536,1024]{1,0:T(8,128)(2,1)}, bf16[1536,1024]{1,0:T(8,128)(2,1)}, f32...) custom-call(bf16[2,1536]{1,0:T(2,128)(2,1)} %broadcast_select_fusion, ...), custom_call_target="tpu_custom_call" | custom-call | tf_op jit(solution)/shard_map/feed_forward/pallas_call | solution.py:921
  184.2 82.7 %attention_backward.1 = (bf16[1024,1536]{1,0:T(8,128)(2,1)}, bf16[1024,1536]{1,0:T(8,128)(2,1)}, f32[192,384]{1,0:T(8,128)}, f32[192,192]{1,0:T(8,128)}, f32[192...) custom-call(s32[1,4]{1,0:T(1,128)} %lengths.3, bf16[2,1536]{1,0:T(2,128)(2,1)} %broadcast_select_fusion.gains, ...), custom_call_target="tpu_custom_call" | custom-call | tf_op jit(solution)/shard_map/attention_backward/pallas_call | solution.py:1223
  266.9 9.2 %hand_over.1 = (bf16[1024,1536]{1,0:T(8,128)(2,1)}, bf16[1024,1536]{1,0:T(8,128)(2,1)}, f32[192,384]{1,0:T(8,128)}, f32[192,192]{1,0:T(8,128)}, f32[192,192]{1,0...) custom-call(f32[8,256]{1,0:T(8,128)} %get-tuple-element.68.sums, ...), custom_call_target="tpu_custom_call" | custom-call | tf_op jit(solution)/shard_map/hand_over/pallas_call | solution.py:1305
  (1 shorter events, 0.0 us)
